TPU v7x, 32 devices: a whole 2x2x4 slice. The times are simulated.
32 devices in a mesh: blk: 8 (over y, x, core), dp: 4 (over z).
Axes of the slice: x: 2, y: 2, z: 4, core: 2. Of those that a mesh axis runs over, the one named last changes fastest.
Arguments:
- saved_query: bfloat16 [4, 2048, 640], P('dp', 'blk'), may hold values from -180 to 180
- saved_key: bfloat16 [4, 2048, 640], P('dp', 'blk'), may hold values from -6 to 6
- saved_value: bfloat16 [4, 2048, 640], P('dp', 'blk'), may hold values from -6 to 6
- out_weight: bfloat16 [640, 1280], replicated, may hold values from -0.15625 to 0.15625
- llm_grad: bfloat16 [2048, 5120], P(('blk', 'dp')), may hold values from -8 to 8
- row_source: int32 [4, 512], P('dp', 'blk'), may hold values from 0 to 2047, as said below
- page_start: int32 [4, 8], P('dp', 'blk'), may hold values from 0 to 7, as said below
- page_size: int32 [4, 8], P('dp', 'blk'), may hold values from 1 to 7, as said below
Outputs:
- query_grad: bfloat16 [4, 2048, 640], P('dp', 'blk')
- key_grad: bfloat16 [4, 2048, 640], P('dp', 'blk')
- value_grad: bfloat16 [4, 2048, 640], P('dp', 'blk')
- weight_grad: float32 [1280, 640], P('blk', 'dp')
Inputs may be any that keep to these rules, and one draw needn't show every extreme that they name: `row_source`: A permutation of the rows of llm_grad. For the device at blk index b of lane l, its merged rows j * 256 // (4 * 4) onward, 256 // (4 * 4) of them, come from the rows held by the llm_grad shard of index b * 4 + j, in any order. Pages tile each lane as runs of whole blocks: for every block, page_start and page_size give the run that contains it, and all blocks of a run carry the same two numbers. In every lane the first page spans more than half of the blocks. `page_size`: see page_start.
All inputs are finite; a program needn't handle non-finite values.
Results may differ from a plain program's by a relative error of at most 0.02.
Values may be sent and summed in bfloat16 or wider, within the bound.
No kernel may reach another device: no remote copies, remote signals or barrier semaphores. Data moves between devices by JAX's collectives and lax.ppermute only.
A program may use at most 128 MiB of HBM per device.

v0:
```python
import math

import jax
import jax.numpy as jnp
from jax import lax
from jax.sharding import PartitionSpec as P

HEADS = 8
HD = 80
MERGE = 4


def head_dots(left_rows, right_rows):
    left_heads = left_rows.reshape(left_rows.shape[0], HEADS, HD)
    right_heads = right_rows.reshape(right_rows.shape[0], HEADS, HD)
    return jnp.einsum("thd,shd->hts", left_heads, right_heads, preferred_element_type=jnp.float32)


def head_mix(weights, rows_in):
    heads_in = rows_in.reshape(rows_in.shape[0], HEADS, HD)
    mixed = jnp.einsum("hts,shd->thd", weights, heads_in, preferred_element_type=jnp.float32)
    return mixed.reshape(weights.shape[1], HEADS * HD)


def head_back(weights, rows_in):
    heads_in = rows_in.reshape(rows_in.shape[0], HEADS, HD)
    mixed = jnp.einsum("hts,thd->shd", weights, heads_in, preferred_element_type=jnp.float32)
    return mixed.reshape(weights.shape[2], HEADS * HD)


def head_delta(grad_rows, context):
    product = grad_rows.astype(jnp.float32) * context.astype(jnp.float32)
    return jnp.sum(product.reshape(product.shape[0], HEADS, HD), axis=2).T


def score_grads(
    query_rows, grad_rows, log_rows, delta_rows, key_part, value_part, visible, scaling
):
    scores = head_dots(query_rows, key_part) * scaling
    attn_probs = jnp.where(visible, jnp.exp(scores - log_rows[:, :, None]), 0.0)
    probs_low = attn_probs.astype(jnp.bfloat16)
    d_probs = head_dots(grad_rows, value_part)
    d_scores = (attn_probs * (d_probs - delta_rows[:, :, None])).astype(jnp.bfloat16)
    return (probs_low, d_scores)


def sweep_rows(stepper, initial, first_row, count, block_rows, seen_of):

    def advance(carried, block_index):
        start_row = first_row + block_index * block_rows
        visible = seen_of(start_row, block_rows)
        return (stepper(carried, start_row, visible), None)

    result, unused = lax.scan(advance, initial, jnp.arange(count // block_rows, dtype=jnp.int32))
    return result


def sweep_emit(stepper, initial, count, block_rows, seen_of, columns):

    def advance(carried, block_index):
        start_row = block_index * block_rows
        visible = seen_of(start_row, block_rows)
        return stepper(carried, start_row, visible)

    result, emitted = lax.scan(advance, initial, jnp.arange(count // block_rows, dtype=jnp.int32))
    return (result, emitted.reshape(count, columns))


def body(
    saved_query, saved_key, saved_value, out_weight, llm_grad, row_source, page_start, page_size
):
    rows_dev = saved_query.shape[1]
    feat_width = saved_query.shape[2]
    model_width = out_weight.shape[1]
    lane_devices = lax.axis_size("dp")
    cycle_devices = lax.axis_size("blk")
    merged_rows = rows_dev // MERGE
    portion = merged_rows // lane_devices
    seq_len = rows_dev * cycle_devices
    block_rows = min(512, seq_len)
    scaling = 1.0 / math.sqrt(HD)
    owners = (
        lax.axis_index("blk") * lane_devices + jnp.arange(lane_devices, dtype=jnp.int32)
    ) * merged_rows
    wanted = row_source[0].reshape(lane_devices, portion) - owners[:, None]
    asked_rows = lax.all_to_all(wanted, "dp", split_axis=0, concat_axis=0, tiled=True)
    picked = jnp.take(llm_grad, asked_rows.reshape(-1), axis=0).reshape(
        lane_devices, portion, llm_grad.shape[1]
    )
    answered = lax.all_to_all(picked, "dp", split_axis=0, concat_axis=0, tiled=True)
    grad_out = answered.reshape(rows_dev, model_width)
    d_attn = lax.dot_general(
        grad_out, out_weight, (((1,), (1,)), ((), ())), preferred_element_type=jnp.float32
    ).astype(jnp.bfloat16)
    query_rows = saved_query[0]
    own_keys = saved_key[0]
    own_values = saved_value[0]
    keys_all, values_all = (
        lax.all_gather(own_keys, "blk", axis=0, tiled=True),
        lax.all_gather(own_values, "blk", axis=0, tiled=True),
    )
    page_first = page_start[0, 0]
    page_span = page_size[0, 0]

    def owned_by_page(start_row, count):
        owner_block = (start_row + jnp.arange(count, dtype=jnp.int32)) // rows_dev
        return (owner_block >= page_first) & (owner_block < page_first + page_span)

    def key_seen(start_row, count):
        return owned_by_page(start_row, count)[None, None, :]

    def stat_step(carried, start_row, visible):
        running_max, running_sum = carried
        key_part = lax.dynamic_slice_in_dim(keys_all, start_row, block_rows, 0)
        scores = head_dots(query_rows, key_part) * scaling
        block_max = jnp.max(jnp.where(visible, scores, -1e30), axis=2)
        new_max = jnp.maximum(running_max, block_max)
        factor = jnp.exp(running_max - new_max)
        weights = jnp.where(visible, jnp.exp(scores - new_max[:, :, None]), 0.0)
        return (new_max, running_sum * factor + jnp.sum(weights, axis=2))

    stat_shape = (HEADS, rows_dev)
    empty_rows = jnp.zeros((rows_dev, feat_width), jnp.float32)
    start_stats = (jnp.full(stat_shape, -1e30, jnp.float32), jnp.zeros(stat_shape, jnp.float32))
    running_max, running_sum = sweep_rows(stat_step, start_stats, 0, seq_len, block_rows, key_seen)
    log_total = running_max + jnp.log(running_sum)

    def context_step(carried, start_row, visible):
        key_part = lax.dynamic_slice_in_dim(keys_all, start_row, block_rows, 0)
        value_part = lax.dynamic_slice_in_dim(values_all, start_row, block_rows, 0)
        scores = head_dots(query_rows, key_part) * scaling
        probs_low = jnp.where(visible, jnp.exp(scores - log_total[:, :, None]), 0.0).astype(
            jnp.bfloat16
        )
        return carried + head_mix(probs_low, value_part)

    context = sweep_rows(context_step, empty_rows, 0, seq_len, block_rows, key_seen).astype(
        jnp.bfloat16
    )
    row_delta = head_delta(d_attn, context)

    def joint_step(carried, start_row, visible):
        key_part = lax.dynamic_slice_in_dim(keys_all, start_row, block_rows, 0)
        value_part = lax.dynamic_slice_in_dim(values_all, start_row, block_rows, 0)
        probs_low, d_scores = score_grads(
            query_rows, d_attn, log_total, row_delta, key_part, value_part, visible, scaling
        )
        terms = jnp.concatenate(
            [head_back(d_scores, query_rows) * scaling, head_back(probs_low, d_attn)], axis=1
        )
        return (carried + head_mix(d_scores, key_part), terms)

    query_sum, all_terms = sweep_emit(
        joint_step, empty_rows, seq_len, block_rows, key_seen, 2 * feat_width
    )
    query_grad = (query_sum * scaling).astype(jnp.bfloat16)
    combined = lax.psum_scatter(all_terms, "blk", scatter_dimension=0, tiled=True)
    key_grad = combined[:, :feat_width].astype(jnp.bfloat16)
    value_grad = combined[:, feat_width:].astype(jnp.bfloat16)
    whole_term = lax.dot_general(
        grad_out, context, (((0,), (0,)), ((), ())), preferred_element_type=jnp.float32
    )
    lane_sums = lax.psum_scatter(
        whole_term.astype(jnp.bfloat16), "dp", scatter_dimension=1, tiled=True
    )
    weight_grad = lax.psum_scatter(lane_sums, "blk", scatter_dimension=0, tiled=True).astype(
        jnp.float32
    )
    return (query_grad[None], key_grad[None], value_grad[None], weight_grad)


def solution(mesh):
    in_specs = (
        P("dp", "blk", None),
        P("dp", "blk", None),
        P("dp", "blk", None),
        P(),
        P(("blk", "dp"), None),
        P("dp", "blk"),
        P("dp", "blk"),
        P("dp", "blk"),
    )
    out_specs = (P("dp", "blk", None), P("dp", "blk", None), P("dp", "blk", None), P("blk", "dp"))
    return jax.shard_map(body, mesh=mesh, in_specs=in_specs, out_specs=out_specs, check_vma=False)
```

profile of v0, /device:TPU:0, one launch (start us, length us, event | category | flops | bytes accessed | tf_op | source)
XLA Modules:
  0.0 302.6 jit_solution(5528922926552818602)
XLA Ops:
  7.2 2.0 copy.33
  11.3 11.7 %all_to_all.11 = s32[4,1,16]{2,1,0:T(1,128)S(1)} all-to-all(s32[4,1,16]{2,1,0:T(1,128)S(1)} %bitcast.150), channel_id=1, replica_groups=mesh['blk'=8,'dp'=4] {'dp'}, dimensions={0} | all-to-all | bytes 512 | tf_op jit(solution)/shard_map/all_to_all | solution.py:86
  25.6 3.5 %all-to-all-start.1 = ((bf16[4,16,5120]{2,1,0:T(8,128)(2,1)}), bf16[4,16,5120]{2,1,0:T(8,128)(2,1)S(1)}, u32[]{:S(2)}, u32[]{:S(2)}) async-start(bf16[4,16,5120]{2,1,0:T(8,128)(2,1)} %broadcast_select_fusion), calls=%async_computation.1 | async-start | bytes 1310720 | tf_op jit(solution)/shard_map/all_to_all | solution.py:90
  29.2 1.9 copy.35
  33.6 11.6 %all-to-all-done.1 = bf16[4,16,5120]{2,1,0:T(8,128)(2,1)S(1)} async-done(((bf16[4,16,5120]{2,1,0:T(8,128)(2,1)}), bf16[4,16,5120]{2,1,0:T(8,128)(2,1)S(1)}, u32[]{:S(2)}, u32[]{:S(2)}) %all-to-all-start.1) | async-done | bytes 655392 | tf_op jit(solution)/shard_map/all_to_all | solution.py:90
  46.5 20.4 %while.43 = (s32[]{:T(128)}, f32[8,256]{1,0:T(8,128)S(1)}, f32[8,256]{1,0:T(8,128)S(1)}, s32[4]{0:T(128)S(1)}, s32[]{:T(128)}, /*index=5*/s32[]{:T(128)}, bf16[2...) while((s32[]{:T(128)}, f32[8,256]{1,0:T(8,128)S(1)}, ...), condition=%wide.region_3.4_spmd.clone, body=%wide.region_0.3_spmd.clone.sunk | while | flops 175132160 | bytes 10790610 | solution.py:54
  66.9 9.8 %all-gather.7.cloned.1.call-done = bf16[1,2048,640]{1,2,0:T(8,128)(2,1)} async-done(((bf16[1,256,640]{1,2,0:T(8,128)(2,1)}), bf16[1,2048,640]{1,2,0:T(8,128)(2,1)}) %all-gather.7.cloned.1.call-update) | async-done | bytes 2621456 | tf_op jit(solution)/shard_map/all_gather | solution.py:100
  76.7 28.5 %while.44 = (s32[]{:T(128)}, f32[256,640]{0,1:T(8,128)S(1)}, s32[4]{0:T(128)S(1)}, bf16[2048,640]{0,1:T(8,128)(2,1)}, s32[]{:T(128)}, /*index=5*/s32[]{:T(128)},...) while((s32[]{:T(128)}, f32[256,640]{0,1:T(8,128)S(1)}, ...), condition=%wide.region_5.6_spmd.clone, body=%wide.region_4.5_spmd.clone.sunk | while | flops 340076032 | bytes 6890713 | solution.py:54
  78.6 2.4 constant_dynamic-slice_fusion.9
  81.1 2.6 fusion.71
  85.7 2.4 constant_dynamic-slice_fusion.9
  88.2 2.6 fusion.71
  92.9 2.4 constant_dynamic-slice_fusion.9
  95.3 2.6 fusion.71
  100.0 2.4 constant_dynamic-slice_fusion.9
  102.5 2.6 fusion.71
  106.1 3.0 convolution_convert_fusion
  109.2 2.6 convert_multiply_fusion
  113.2 1.9 copy.41
  115.1 30.5 %reduce-scatter.8.cloned.1.call-done = bf16[1280,160]{0,1:T(8,128)(2,1)} async-done(((bf16[1280,640]{0,1:T(8,128)(2,1)}), bf16[1280,160]{0,1:T(8,128)(2,1)}) %reduce-scatter.8.cloned.1.call-update) | async-done | bytes 409616 | tf_op jit(solution)/shard_map/reduce_scatter | solution.py:163
  145.6 2.1 copy.45
  147.9 65.2 %while.45 = (s32[]{:T(128)}, f32[256,640]{0,1:T(8,128)S(1)}, f32[4,512,1280]{2,1,0:T(8,128)}, s32[4]{0:T(128)S(1)}, bf16[2048,640]{0,1:T(8,128)(2,1)}, /*index=5...) while((s32[]{:T(128)}, f32[256,640]{0,1:T(8,128)S(1)}, ...), condition=%wide.region_8.9_spmd.clone, body=%wide.region_7.8_spmd.clone.sunk | while | flops 850667008 | bytes 47081232 | solution.py:65
  155.9 1.7 maximum_bitcast_fusion.2
  157.6 3.3 %copy.51 = f32[1,512,1280]{2,1,0:T(8,128)} copy(f32[1,512,1280]{1,2,0:T(8,128)} %maximum_bitcast_fusion.2) | data formatting | bytes 5242880 | tf_op jit(solution)/shard_map/while/body/jit(dynamic_update_index_in_dim)/dynamic_update_slice | solution.py:65
  160.8 3.4 %constant_dynamic-update-slice_fusion.2 = f32[4,512,1280]{2,1,0:T(8,128)} fusion(f32[4,512,1280]{2,1,0:T(8,128)} %get-tuple-element.931, f32[1,512,1280]{2,1,0:T(8,128)} %copy.51, s32[]{:T(128)S(6)} %copy.71), kind=kLoop, calls=%fused_computation.55.clone.1 | loop fusion | bytes 5242884 | tf_op jit(solution)/shard_map/while/body/jit(dynamic_update_index_in_dim)/dynamic_update_slice | solution.py:65
  173.9 3.2 %copy.51 = f32[1,512,1280]{2,1,0:T(8,128)} copy(f32[1,512,1280]{1,2,0:T(8,128)} %maximum_bitcast_fusion.2) | data formatting | bytes 5242880 | tf_op jit(solution)/shard_map/while/body/jit(dynamic_update_index_in_dim)/dynamic_update_slice | solution.py:65
  177.1 3.5 %constant_dynamic-update-slice_fusion.2 = f32[4,512,1280]{2,1,0:T(8,128)} fusion(f32[4,512,1280]{2,1,0:T(8,128)} %get-tuple-element.931, f32[1,512,1280]{2,1,0:T(8,128)} %copy.51, s32[]{:T(128)S(6)} %copy.71), kind=kLoop, calls=%fused_computation.55.clone.1 | loop fusion | bytes 5242884 | tf_op jit(solution)/shard_map/while/body/jit(dynamic_update_index_in_dim)/dynamic_update_slice | solution.py:65
  190.2 3.2 %copy.51 = f32[1,512,1280]{2,1,0:T(8,128)} copy(f32[1,512,1280]{1,2,0:T(8,128)} %maximum_bitcast_fusion.2) | data formatting | bytes 5242880 | tf_op jit(solution)/shard_map/while/body/jit(dynamic_update_index_in_dim)/dynamic_update_slice | solution.py:65
  193.4 3.4 %constant_dynamic-update-slice_fusion.2 = f32[4,512,1280]{2,1,0:T(8,128)} fusion(f32[4,512,1280]{2,1,0:T(8,128)} %get-tuple-element.931, f32[1,512,1280]{2,1,0:T(8,128)} %copy.51, s32[]{:T(128)S(6)} %copy.71), kind=kLoop, calls=%fused_computation.55.clone.1 | loop fusion | bytes 5242884 | tf_op jit(solution)/shard_map/while/body/jit(dynamic_update_index_in_dim)/dynamic_update_slice | solution.py:65
  206.4 3.2 %copy.51 = f32[1,512,1280]{2,1,0:T(8,128)} copy(f32[1,512,1280]{1,2,0:T(8,128)} %maximum_bitcast_fusion.2) | data formatting | bytes 5242880 | tf_op jit(solution)/shard_map/while/body/jit(dynamic_update_index_in_dim)/dynamic_update_slice | solution.py:65
  209.6 3.5 %constant_dynamic-update-slice_fusion.2 = f32[4,512,1280]{2,1,0:T(8,128)} fusion(f32[4,512,1280]{2,1,0:T(8,128)} %get-tuple-element.931, f32[1,512,1280]{2,1,0:T(8,128)} %copy.51, s32[]{:T(128)S(6)} %copy.71), kind=kLoop, calls=%fused_computation.55.clone.1 | loop fusion | bytes 5242884 | tf_op jit(solution)/shard_map/while/body/jit(dynamic_update_index_in_dim)/dynamic_update_slice | solution.py:65
  215.9 77.9 %reduce-scatter.6.cloned.1.call-done = f32[256,1280]{1,0:T(8,128)} async-done(((f32[2048,1280]{1,0:T(8,128)}), f32[256,1280]{1,0:T(8,128)}) %reduce-scatter.6.cloned.1.call-update) | async-done | bytes 1310736 | tf_op jit(solution)/shard_map/reduce_scatter | solution.py:157
  (141 shorter events, 71.9 us)
Async XLA Ops:
  7.2 102.0 %copy-start = (bf16[640,1280]{1,0:T(8,128)(2,1)S(1)}, bf16[640,1280]{1,0:T(8,128)(2,1)}, u32[]{:S(2)}) copy-start(bf16[640,1280]{1,0:T(8,128)(2,1)} %param.17) | copy-start | bytes 4915204
  7.2 16.5 %copy-start.1 = (bf16[64,5120]{1,0:T(8,128)(2,1)S(1)}, bf16[64,5120]{1,0:T(8,128)(2,1)}, u32[]{:S(2)}) copy-start(bf16[64,5120]{1,0:T(8,128)(2,1)} %param.18) | copy-start | bytes 1966084
  7.2 39.3 %all-gather.5.cloned.1.call-start = ((), (), s32[]{:S(2)}) async-start(), calls=%async_computation.7 | async-start | bytes 2949120 | tf_op jit(solution)/shard_map/all_gather | solution.py:99
  25.6 19.6 %all-to-all-start.1 = ((bf16[4,16,5120]{2,1,0:T(8,128)(2,1)}), bf16[4,16,5120]{2,1,0:T(8,128)(2,1)S(1)}, u32[]{:S(2)}, u32[]{:S(2)}) async-start(bf16[4,16,5120]{2,1,0:T(8,128)(2,1)} %broadcast_select_fusion), calls=%async_computation.1 | async-start | bytes 1310720 | tf_op jit(solution)/shard_map/all_to_all | solution.py:90
  29.1 47.6 %all-gather.7.cloned.1.call-start = ((), (), s32[]{:S(2)}) async-start(), calls=%async_computation.8 | async-start | bytes 2949120 | tf_op jit(solution)/shard_map/all_gather | solution.py:100
  31.1 114.5 %reduce-scatter.8.cloned.1.call-start = ((), (), s32[]{:S(2)}) async-start(), calls=%async_computation.6 | async-start | bytes 2048000 | tf_op jit(solution)/shard_map/reduce_scatter | solution.py:163
  105.2 4.0 %copy-start.2 = (bf16[256,1280]{1,0:T(8,128)(2,1)S(1)}, bf16[256,1280]{1,0:T(8,128)(2,1)}, u32[]{:S(2)}) copy-start(bf16[256,1280]{1,0:T(8,128)(2,1)} %reshape.240) | copy-start | bytes 1966084
  109.1 105.0 %reduce-scatter.10.cloned.1.call-start = ((), (), s32[]{:S(2)}) async-start(), calls=%async_computation.9 | async-start | bytes 737280
  147.7 146.1 %reduce-scatter.6.cloned.1.call-start = ((), (), s32[]{:S(2)}) async-start(), calls=%async_computation.5 | async-start | bytes 11796480 | tf_op jit(solution)/shard_map/reduce_scatter | solution.py:157
  147.9 4.1 %copy-start.3 = (bf16[256,640]{0,1:T(8,128)(2,1)S(1)}, bf16[256,640]{0,1:T(8,128)(2,1)}, u32[]{:S(2)}) copy-start(bf16[256,640]{0,1:T(8,128)(2,1)} %get-tuple-element.955) | copy-start | bytes 983044 | tf_op jit(solution)/shard_map/while
  164.2 4.1 %copy-start.3 = (bf16[256,640]{0,1:T(8,128)(2,1)S(1)}, bf16[256,640]{0,1:T(8,128)(2,1)}, u32[]{:S(2)}) copy-start(bf16[256,640]{0,1:T(8,128)(2,1)} %get-tuple-element.955) | copy-start | bytes 983044 | tf_op jit(solution)/shard_map/while
  180.5 4.1 %copy-start.3 = (bf16[256,640]{0,1:T(8,128)(2,1)S(1)}, bf16[256,640]{0,1:T(8,128)(2,1)}, u32[]{:S(2)}) copy-start(bf16[256,640]{0,1:T(8,128)(2,1)} %get-tuple-element.955) | copy-start | bytes 983044 | tf_op jit(solution)/shard_map/while
  196.8 4.1 %copy-start.3 = (bf16[256,640]{0,1:T(8,128)(2,1)S(1)}, bf16[256,640]{0,1:T(8,128)(2,1)}, u32[]{:S(2)}) copy-start(bf16[256,640]{0,1:T(8,128)(2,1)} %get-tuple-element.955) | copy-start | bytes 983044 | tf_op jit(solution)/shard_map/while
Sparse Core Ops, SparseCore 0:
  10.5 33.1 all-gather.4
  46.2 30.4 all-gather.6
  109.2 36.2 reduce-scatter.7
  148.8 33.5 reduce-scatter.9
  213.2 80.4 reduce-scatter.5
where the time goes:
time: 304 us; the launch traced here: 303 us
  waiting for transfers between devices  130 us (43%)
  local copies, waits for them, and re-layouts  70.5 us (23%)
  matrix products  38.4 us (13%)
  other arithmetic  24.5 us (8%)
  between operations  15.3 us (5%)
  blocking collectives  11.7 us (4%)
  loops' own time  8.39 us (3%)
  starting transfers between devices  3.87 us (1%)
    reduce_scatter x1, waiting for transfers between devices, body(): lax.psum_scatter(all_terms, 'blk', scatter_dimension=0, tiled=True)  77.9 us
    reduce_scatter x1, waiting for transfers between devices, body(): lax.psum_scatter(whole_term.astype(jnp.bfloat16), 'dp', scatter_dimension...  30.5 us
    dynamic_update_slice x8, local copies, waits for them, and re-layouts, sweep_emit(): lax.scan(advance, initial, jnp.arange(count // block_rows, dtype=jnp.int32))  26.6 us
    dot_general x12, matrix products, head_dots(): jnp.einsum('thd,shd->hts', left_heads, right_heads, preferred_element_typ...  13.6 us
    dot_general x8, matrix products, head_mix(): jnp.einsum('hts,shd->thd', weights, heads_in, preferred_element_type=jnp....  12.4 us
    all_to_all x1, blocking collectives, body(): lax.all_to_all(wanted, 'dp', split_axis=0, concat_axis=0, tiled=True)  11.7 us
    all_to_all x1, waiting for transfers between devices, body(): lax.all_to_all(picked, 'dp', split_axis=0, concat_axis=0, tiled=True)  11.6 us
    unnamed x14, local copies, waits for them, and re-layouts  11.3 us
  transfers between devices with their start and end apart: 6, of which 4 were waited for; matrix products, arithmetic and copies ran while one was open for 32% of the time, Pallas kernels for 0%

commit v1 on v0

v1 whole, which is shorter than its diff:
```python
import functools
import math

import jax
import jax.numpy as jnp
from jax import lax
from jax.experimental import pallas as pl
from jax.experimental.pallas import tpu as pltpu
from jax.sharding import PartitionSpec as P

HEADS = 8
HD = 80
MERGE = 4
INFO = 16
HIDE = -1e30
SCALING = 1.0 / math.sqrt(HD)
EXP2_SCALE = SCALING * math.log2(math.e)
F32 = jnp.float32
BF16 = jnp.bfloat16
VMEM = pl.BlockSpec(memory_space=pltpu.VMEM)
SMEM = pl.BlockSpec(memory_space=pltpu.SMEM)
PARAMS = pltpu.CompilerParams(vmem_limit_bytes=48 * 2**20)


def dot_nn(left, right):
    return lax.dot_general(left, right, (((1,), (0,)), ((), ())), preferred_element_type=F32)


def dot_nt(left, right):
    return lax.dot_general(left, right, (((1,), (1,)), ((), ())), preferred_element_type=F32)


def dot_tn(left, right):
    return lax.dot_general(left, right, (((0,), (0,)), ((), ())), preferred_element_type=F32)


def pack_kernel(start_ref, size_ref, query_ref, key_ref, value_ref, out_ref, *, groups):
    rows, width = query_ref.shape
    feat = width // groups
    for slot, ref in enumerate((query_ref, key_ref, value_ref)):
        turned = ref[...].T
        for g in range(groups):
            out_ref[g, slot * feat : (slot + 1) * feat, :] = turned[g * feat : (g + 1) * feat, :]
    line = lax.broadcasted_iota(jnp.int32, (INFO, rows), 0)
    info = jnp.where(line < INFO // 2, start_ref[0], size_ref[0]).astype(F32).astype(BF16)
    for g in range(groups):
        out_ref[g, 3 * feat :, :] = info


def pack(page_start, page_size, query, key, value, groups):
    rows, width = query.shape
    return pl.pallas_call(
        functools.partial(pack_kernel, groups=groups),
        out_shape=jax.ShapeDtypeStruct((groups, 3 * (width // groups) + INFO, rows), BF16),
        in_specs=[SMEM, SMEM, VMEM, VMEM, VMEM],
        out_specs=VMEM,
        compiler_params=PARAMS,
    )(page_start, page_size, query, key, value)


def project_kernel(grad_ref, weight_ref, out_ref):
    merged = grad_ref.shape[0]
    width = weight_ref.shape[1]
    for c in range(MERGE):
        part = grad_ref[:, c * width : (c + 1) * width]
        out_ref[c * merged : (c + 1) * merged, :] = dot_nt(part, weight_ref[...]).astype(BF16)


def project(llm_grad, weight):
    merged = llm_grad.shape[0]
    return pl.pallas_call(
        project_kernel,
        out_shape=jax.ShapeDtypeStruct((merged * MERGE, weight.shape[0]), BF16),
        in_specs=[VMEM, VMEM],
        out_specs=VMEM,
        compiler_params=PARAMS,
    )(llm_grad, weight)


def select_kernel(asked_ref, source_ref, grad_ref, rows_ref, merged_ref):
    partners, part_rows, width = rows_ref.shape
    total = partners * part_rows
    merged = total // MERGE
    portion = part_rows // MERGE
    asked = asked_ref[...]
    held = lax.broadcasted_iota(jnp.int32, (total, total), 1)
    line = lax.broadcasted_iota(jnp.int32, (total, 1), 0)
    wanted = asked + (line % MERGE) * merged
    chosen = dot_nn((held == wanted).astype(BF16), source_ref[...]).astype(BF16)
    for k in range(partners):
        rows_ref[k] = chosen[k * part_rows : (k + 1) * part_rows, :]
    every = lax.broadcasted_iota(jnp.int32, (total, merged), 1)
    pick_line = lax.broadcasted_iota(jnp.int32, (merged, total), 1)
    pick_row = lax.broadcasted_iota(jnp.int32, (merged, total), 0)
    thin = dot_nn(
        (pick_line == pick_row * MERGE).astype(BF16), (every == asked).astype(BF16)
    ).astype(BF16)
    picked = dot_nn(thin, grad_ref[...]).astype(BF16)
    for k in range(partners):
        merged_ref[k] = picked[k * portion : (k + 1) * portion, :]


def select(asked, source, llm_grad, partners):
    total, width = source.shape
    merged = llm_grad.shape[0]
    return pl.pallas_call(
        select_kernel,
        out_shape=(
            jax.ShapeDtypeStruct((partners, total // partners, width), BF16),
            jax.ShapeDtypeStruct((partners, merged // partners, llm_grad.shape[1]), BF16),
        ),
        in_specs=[VMEM, VMEM, VMEM],
        out_specs=(VMEM, VMEM),
        compiler_params=PARAMS,
    )(asked, source, llm_grad)


def turn_kernel(place_ref, *refs):
    out_ref, held = refs[-2:]
    groups, feat, rows = out_ref.shape
    for k, ref in enumerate(refs[:-2]):
        count = ref.shape[0]
        first = pl.multiple_of(place_ref[k] * count, count)
        held[pl.ds(first, count), :] = ref[...]
    turned = held[...].T
    for g in range(groups):
        out_ref[g] = turned[g * feat : (g + 1) * feat, :]


def turn(place, parts, groups):
    count, width = parts[0].shape
    rows = count * len(parts)
    return pl.pallas_call(
        turn_kernel,
        out_shape=jax.ShapeDtypeStruct((groups, width // groups, rows), BF16),
        in_specs=[SMEM] + [VMEM] * len(parts),
        out_specs=VMEM,
        scratch_shapes=[pltpu.VMEM((rows, width), BF16)],
        compiler_params=PARAMS,
    )(place, *parts)


def hidden_row(ref, block, key_block, feat):
    info = ref[block, 3 * feat : 3 * feat + INFO, :].astype(F32)
    first = info[0:1, :]
    count = info[INFO // 2 : INFO // 2 + 1, :]
    return jnp.where((first <= key_block) & (first + count > key_block), 0.0, HIDE)


def forward_kernel(first_ref, all_ref, context_ref, log_ref, keys, score, *, heads, shares):
    blocks, _, rows = all_ref.shape
    count = blocks // shares
    first = first_ref[0] if shares > 1 else 0
    feat = heads * HD
    if shares > 1:
        context_ref[...] = jnp.zeros(context_ref.shape, BF16)
    for h in range(heads):
        for j in range(blocks):
            keys[j * rows : (j + 1) * rows, :] = all_ref[
                j, feat + h * HD : feat + (h + 1) * HD, :
            ].T

        def step(index, carried):
            b = first + index
            query = all_ref[b, h * HD : (h + 1) * HD, :]
            hidden = [hidden_row(all_ref, b, j, feat) for j in range(blocks)]
            top = None
            for j in range(blocks):
                part = dot_nn(keys[j * rows : (j + 1) * rows, :], query)
                score[j * rows : (j + 1) * rows, :] = part
                part_top = jnp.max(part, axis=0, keepdims=True) + hidden[j]
                top = part_top if top is None else jnp.maximum(top, part_top)
            base = top * EXP2_SCALE
            total, mixed = None, None
            for j in range(blocks):
                weight = jnp.exp2(
                    score[j * rows : (j + 1) * rows, :] * EXP2_SCALE + (hidden[j] - base)
                )
                part_sum = jnp.sum(weight, axis=0, keepdims=True)
                value = all_ref[j, 2 * feat + h * HD : 2 * feat + (h + 1) * HD, :]
                part_mix = dot_nn(value, weight.astype(BF16))
                total = part_sum if total is None else total + part_sum
                mixed = part_mix if mixed is None else mixed + part_mix
            context_ref[b, h * HD : (h + 1) * HD, :] = (mixed / total).astype(BF16)
            log_ref[b, h : h + 1, :] = base + jnp.log2(total)
            return carried

        lax.fori_loop(0, count, step, 0)


def forward(first, gathered, heads, shares):
    blocks, _, rows = gathered.shape
    return pl.pallas_call(
        functools.partial(forward_kernel, heads=heads, shares=shares),
        out_shape=(
            jax.ShapeDtypeStruct((blocks, heads * HD, rows), BF16),
            jax.ShapeDtypeStruct((blocks, heads, rows), F32),
        ),
        in_specs=[SMEM, VMEM],
        out_specs=(VMEM, VMEM),
        scratch_shapes=[pltpu.VMEM((blocks * rows, HD), BF16), pltpu.VMEM((blocks * rows, rows), F32)],
        compiler_params=PARAMS,
    )(first, gathered)


def backward_kernel(
    first_ref, all_ref, grad_ref, context_ref, log_ref, out_ref, query_sum, delta, keys, values,
    *, heads, shares
):
    blocks, _, rows = all_ref.shape
    count = blocks // shares
    first = first_ref[0] if shares > 1 else 0
    feat = heads * HD
    for h in range(heads):
        own = slice(h * HD, (h + 1) * HD)
        key_own = slice(feat + h * HD, feat + (h + 1) * HD)
        value_own = slice(2 * feat + h * HD, 2 * feat + (h + 1) * HD)
        for j in range(blocks):
            keys[j] = all_ref[j, key_own, :].T
            values[j] = all_ref[j, value_own, :].T
        for index in range(count):
            b = first + index
            product = grad_ref[b, own, :].astype(F32) * context_ref[b, own, :].astype(F32)
            delta[index] = jnp.sum(product, axis=0, keepdims=True)
            query_sum[index] = jnp.zeros((HD, rows), F32)

        def step(j, carried):
            key, value, turned_key = keys[j], values[j], all_ref[j, key_own, :]
            key_sum = jnp.zeros((HD, rows), F32)
            value_sum = jnp.zeros((HD, rows), F32)
            for index in range(count):
                b = first + index
                query, grad = all_ref[b, own, :], grad_ref[b, own, :]
                shift = hidden_row(all_ref, b, j.astype(F32), feat) - log_ref[b, h : h + 1, :]
                probs = jnp.exp2(dot_nn(key, query) * EXP2_SCALE + shift)
                d_scores = (probs * (dot_nn(value, grad) - delta[index])).astype(BF16)
                value_sum = value_sum + dot_nt(grad, probs.astype(BF16))
                key_sum = key_sum + dot_nt(query, d_scores)
                query_sum[index] += dot_nn(turned_key, d_scores)
            out_ref[j, key_own, :] = (key_sum * SCALING).astype(BF16)
            out_ref[j, value_own, :] = value_sum.astype(BF16)
            return carried

        lax.fori_loop(0, blocks, step, 0)
        if shares > 1:
            for b in range(blocks):
                out_ref[b, own, :] = jnp.zeros((HD, rows), BF16)
        for index in range(count):
            out_ref[first + index, own, :] = (query_sum[index] * SCALING).astype(BF16)


def backward(first, gathered, grads, context, log_total, heads, shares):
    blocks, _, rows = gathered.shape
    return pl.pallas_call(
        functools.partial(backward_kernel, heads=heads, shares=shares),
        out_shape=jax.ShapeDtypeStruct((blocks, 3 * heads * HD, rows), BF16),
        in_specs=[SMEM] + [VMEM] * 4,
        out_specs=VMEM,
        scratch_shapes=[
            pltpu.VMEM((blocks // shares, HD, rows), F32),
            pltpu.VMEM((blocks // shares, 1, rows), F32),
            pltpu.VMEM((blocks, rows, HD), BF16),
            pltpu.VMEM((blocks, rows, HD), BF16),
        ],
        compiler_params=PARAMS,
    )(first, gathered, grads, context, log_total)


def summed(ref, group, shares, lines):
    if shares == 1:
        return ref[group, lines, :]
    total = ref[group * shares, lines, :].astype(F32)
    for r in range(1, shares):
        total = total + ref[group * shares + r, lines, :].astype(F32)
    return total.astype(BF16)


def unpack_kernel(all_ref, query_ref, key_ref, value_ref, held, *, groups, shares):
    rows, width = query_ref.shape
    feat = width // groups
    for slot, ref in enumerate((query_ref, key_ref, value_ref)):
        for g in range(groups):
            held[g * feat : (g + 1) * feat, :] = summed(
                all_ref, g, shares, slice(slot * feat, (slot + 1) * feat)
            )
        ref[...] = held[...].T


def unpack(returned, width, groups, shares):
    rows = returned.shape[2]
    shape = jax.ShapeDtypeStruct((rows, width), BF16)
    return pl.pallas_call(
        functools.partial(unpack_kernel, groups=groups, shares=shares),
        out_shape=(shape, shape, shape),
        in_specs=[VMEM],
        out_specs=(VMEM, VMEM, VMEM),
        scratch_shapes=[pltpu.VMEM((width, rows), BF16)],
        compiler_params=PARAMS,
    )(returned)


def weight_kernel(place_ref, context_ref, *refs, groups, shares):
    out_ref, held = refs[-2:]
    parts = refs[:-2]
    feat = context_ref.shape[1]
    rows = context_ref.shape[2]
    portion, wide = parts[0].shape
    width = wide // MERGE
    merged = rows // MERGE
    for g in range(groups):
        held[g * feat : (g + 1) * feat, :] = summed(context_ref, g, shares, slice(0, feat))
    line = lax.broadcasted_iota(jnp.int32, (rows, rows), 0)
    column = lax.broadcasted_iota(jnp.int32, (rows, rows), 1)
    within = line % merged
    slot = within // portion
    place = jnp.zeros((rows, rows), jnp.int32)
    for k in range(len(parts)):
        place = jnp.where(slot == k, place_ref[k], place)
    target = (place * portion + within % portion) * MERGE + line // merged
    ordered = dot_nt((column == target).astype(BF16), held[...]).astype(BF16)
    grads = jnp.concatenate([ref[...] for ref in parts], axis=0)
    total = None
    for c in range(MERGE):
        term = dot_tn(
            grads[:, c * width : (c + 1) * width], ordered[c * merged : (c + 1) * merged, :]
        )
        total = term if total is None else total + term
    out_ref[...] = total.astype(BF16)


def weight_terms(place, context, parts, width, groups, shares):
    wide = parts[0].shape[1]
    return pl.pallas_call(
        functools.partial(weight_kernel, groups=groups, shares=shares),
        out_shape=jax.ShapeDtypeStruct((wide // MERGE, width), BF16),
        in_specs=[SMEM, VMEM] + [VMEM] * len(parts),
        out_specs=VMEM,
        scratch_shapes=[pltpu.VMEM((width, context.shape[2]), BF16)],
        compiler_params=PARAMS,
    )(place, context, *parts)


def swap(array, axis, size, mask):
    return lax.ppermute(array, axis, [(i, i ^ mask) for i in range(size)])


def body(
    saved_query, saved_key, saved_value, out_weight, llm_grad, row_source, page_start, page_size
):
    lanes = lax.axis_size("dp")
    cycle = lax.axis_size("blk")
    width = saved_query.shape[2]
    model_width = out_weight.shape[1]
    merged = llm_grad.shape[0]
    portion = merged // lanes
    groups = min(HEADS, cycle)
    heads = HEADS // groups
    shares = cycle // groups
    my_lane = lax.axis_index("dp")
    my_block = lax.axis_index("blk")
    partner = my_lane ^ jnp.arange(lanes, dtype=jnp.int32)
    first = ((my_block % shares) * (cycle // shares)).astype(jnp.int32).reshape(1)

    def spread(array):
        if shares > 1:
            array = jnp.repeat(array, shares, axis=0)
        return lax.all_to_all(array, "blk", split_axis=0, concat_axis=0, tiled=True)

    owners = (my_block * lanes + jnp.arange(lanes, dtype=jnp.int32)) * merged
    wanted = jnp.take(row_source[0].reshape(lanes, portion) - owners[:, None], partner, axis=0)
    asked = [wanted[0]] + [swap(wanted[k], "dp", lanes, k) for k in range(1, lanes)]
    asked_lines = jnp.repeat(jnp.concatenate(asked), MERGE)[:, None]
    source = project(llm_grad, out_weight)
    packed = pack(
        page_start.reshape(1), page_size.reshape(1), saved_query[0], saved_key[0], saved_value[0], groups
    )
    chosen, picked = select(asked_lines, source, llm_grad, lanes)
    grad_parts = [chosen[0]] + [swap(chosen[k], "dp", lanes, k) for k in range(1, lanes)]
    gathered = spread(packed)
    merged_parts = [picked[0]] + [swap(picked[k], "dp", lanes, k) for k in range(1, lanes)]
    context, log_total = forward(first, gathered, heads, shares)
    grads = spread(turn(partner, grad_parts, groups))
    back_context = lax.all_to_all(context, "blk", split_axis=0, concat_axis=0, tiled=True)
    results = backward(first, gathered, grads, context, log_total, heads, shares)
    returned = lax.all_to_all(results, "blk", split_axis=0, concat_axis=0, tiled=True)
    query_grad, key_grad, value_grad = unpack(returned, width, groups, shares)

    terms = weight_terms(partner, back_context, merged_parts, width, groups, shares)
    terms = terms.reshape(cycle, model_width // cycle, width)
    mask = 1
    while mask < cycle:
        terms = terms.reshape(terms.shape[0] // 2, 2, *terms.shape[1:])
        side = (my_block // mask) % 2
        keep = lax.dynamic_index_in_dim(terms, side, 1, keepdims=False)
        send = lax.dynamic_index_in_dim(terms, 1 - side, 1, keepdims=False)
        terms = (keep.astype(F32) + swap(send, "blk", cycle, mask).astype(F32)).astype(BF16)
        mask *= 2
    terms = terms.reshape(model_width // cycle, lanes, width // lanes).transpose(1, 0, 2)
    terms = jnp.take(terms, partner, axis=0)
    weight_grad = terms[0].astype(F32)
    for k in range(1, lanes):
        weight_grad = weight_grad + swap(terms[k], "dp", lanes, k).astype(F32)
    return (query_grad[None], key_grad[None], value_grad[None], weight_grad)


def solution(mesh):
    in_specs = (
        P("dp", "blk", None),
        P("dp", "blk", None),
        P("dp", "blk", None),
        P(),
        P(("blk", "dp"), None),
        P("dp", "blk"),
        P("dp", "blk"),
        P("dp", "blk"),
    )
    out_specs = (P("dp", "blk", None), P("dp", "blk", None), P("dp", "blk", None), P("blk", "dp"))
    return jax.shard_map(body, mesh=mesh, in_specs=in_specs, out_specs=out_specs, check_vma=False)
```

time: 304 us -> 136 us (0.45)
  waiting for transfers between devices: 130 us -> 40.8 us
  local copies, waits for them, and re-layouts: 70.5 us -> 13.3 us
  Pallas kernels: 0 us -> 39.1 us
  matrix products: 38.4 us -> 0 us
  starting transfers between devices: 3.87 us -> 36.1 us
  other arithmetic: 24.5 us -> 3.24 us
  between operations: 15.3 us -> 2.18 us
  blocking collectives: 11.7 us -> 0 us
  loops' own time: 8.39 us -> 0 us
    reduce_scatter x2 -> x0, waiting for transfers between devices: 108 us -> none  [the longest x1 77.9 us: body(): lax.psum_scatter(all_terms, 'blk', scatter_dimension=0, tiled=True)]
    pallas_call x0 -> x8, Pallas kernels: none -> 39.1 us  [the longest x1 19.2 us: backward(): pl.pallas_call(functools.partial(backward_kernel, heads=heads, shares=sha...]
    dot_general x30 -> x0, matrix products: 38.4 us -> none  [the longest x12 13.6 us: head_dots(): jnp.einsum('thd,shd->hts', left_heads, right_heads, preferred_element_typ...]
    dynamic_slice x24 -> x0, local copies, waits for them, and re-layouts: 26.9 us -> none  [the longest x4 9.77 us: context_step(): key_part = lax.dynamic_slice_in_dim(keys_all, start_row, block_rows, 0)]
    dynamic_update_slice x8 -> x0, local copies, waits for them, and re-layouts: 26.6 us -> none  [sweep_emit(): lax.scan(advance, initial, jnp.arange(count // block_rows, dtype=jnp.int32))]
    ppermute x0 -> x15, waiting for transfers between devices: none -> 21.9 us  [swap(): return lax.ppermute(array, axis, [(i, i ^ mask) for i in range(size)])]
    ppermute x0 -> x15, starting transfers between devices: none -> 20.5 us  [swap(): return lax.ppermute(array, axis, [(i, i ^ mask) for i in range(size)])]
    all_to_all x1 -> x4, starting transfers between devices: 3.48 us -> 15.6 us  [the longest x2 8.6 us: spread(): return lax.all_to_all(array, 'blk', split_axis=0, concat_axis=0, tiled=True)]
  transfers between devices with their start and end apart: 6 -> 19, of which waited for: 4 -> 9; matrix products, arithmetic and copies ran while one was open for 32% -> 3% of each run, Pallas kernels for 0% -> 18%
where the time goes in v1:
time: 136 us; the launch traced here: 135 us
  waiting for transfers between devices  40.8 us (30%)
  Pallas kernels  39.1 us (29%)
  starting transfers between devices  36.1 us (27%)
  local copies, waits for them, and re-layouts  13.3 us (10%)
  other arithmetic  3.24 us (2%)
  between operations  2.18 us (2%)
    ppermute x15, waiting for transfers between devices, swap(): return lax.ppermute(array, axis, [(i, i ^ mask) for i in range(size)])  21.9 us
    ppermute x15, starting transfers between devices, swap(): return lax.ppermute(array, axis, [(i, i ^ mask) for i in range(size)])  20.5 us
    pallas_call x1, Pallas kernels, backward(): pl.pallas_call(functools.partial(backward_kernel, heads=heads, shares=sha...  19.2 us
    pallas_call x1, Pallas kernels, forward(): pl.pallas_call(functools.partial(forward_kernel, heads=heads, shares=shar...  10.8 us
    all_to_all x1, waiting for transfers between devices, body(): lax.all_to_all(results, 'blk', split_axis=0, concat_axis=0, tiled=True)  9.98 us
    unnamed x33, local copies, waits for them, and re-layouts  9.88 us
    all_to_all x2, waiting for transfers between devices, spread(): return lax.all_to_all(array, 'blk', split_axis=0, concat_axis=0, tiled=True)  8.91 us
    all_to_all x2, starting transfers between devices, spread(): return lax.all_to_all(array, 'blk', split_axis=0, concat_axis=0, tiled=True)  8.6 us
  transfers between devices with their start and end apart: 19, of which 9 were waited for; matrix products, arithmetic and copies ran while one was open for 3% of the time, Pallas kernels for 18%

profile of v1, /device:TPU:0, one launch (start us, length us, event | category | flops | bytes accessed | tf_op | source)
XLA Modules:
  0.0 134.8 jit_solution(9398153565746982571)
XLA Ops:
  2.9 1.0 copy-done.5
  3.9 1.0 copy-done.6
  4.9 1.3 shard_map.111
  6.1 5.2 %all-to-all-start = ((bf16[8,256,256]{2,1,0:T(8,128)(2,1)}), bf16[8,256,256]{2,1,0:T(8,128)(2,1)S(1)}, u32[]{:S(2)}, u32[]{:S(2)}) async-start(bf16[8,256,256]{2,1,0:T(8,128)(2,1)} %shard_map.111), calls=%async_computation | async-start | bytes 2097152 | tf_op jit(solution)/shard_map/all_to_all | solution.py:367
  13.3 3.6 %collective-permute-start.2 = (s32[16]{0:T(128)S(1)}, s32[16]{0:T(128)S(1)}, u32[]{:S(2)}, u32[]{:S(2)}) collective-permute-start(s32[16]{0:T(128)S(1)} %get-tuple-element.30), channel_id=1, source_target_pairs={{0,3},{1,2},{2,1},{3,0},{4,7},{5,6},{6,5},{7,4},{8,11},{9,10},{10,... | collective-permute-start | bytes 200 | tf_op jit(solution)/shard_map/ppermute | solution.py:344
  17.8 2.1 %shard_map.112.source_ref = bf16[256,640]{1,0:T(8,128)(2,1)S(1)} custom-call(bf16[64,5120]{1,0:T(8,128)(2,1)S(1)} %copy-done, bf16[640,1280]{1,0:T(8,128)(2,1)S(1)} %copy-done.1), custom_call_target="tpu_custom_call" | custom-call | tf_op jit(solution)/shard_map/pallas_call | solution.py:71
  21.7 1.0 copy-done.3
  23.3 3.5 %all-to-all-done.all_ref = bf16[8,256,256]{2,1,0:T(8,128)(2,1)S(1)} async-done(((bf16[8,256,256]{2,1,0:T(8,128)(2,1)}), bf16[8,256,256]{2,1,0:T(8,128)(2,1)S(1)}, u32[]{:S(2)}, u32[]{:S(2)}) %all-to-all-start) | async-done | bytes 1048608 | tf_op jit(solution)/shard_map/all_to_all | solution.py:367
  26.7 10.8 %shard_map.115 = (bf16[8,80,256]{2,1,0:T(8,128)(2,1)}, f32[8,1,256]{2,1,0:T(1,128)S(1)}) custom-call(s32[1]{0:T(128)} %constant.107.clone.1.first_ref, bf16[8,256,256]{2,1,0:T(8,128)(2,1)S(1)} %all-to-all-done.all_ref), custom_call_target="tpu_custom_call" | custom-call | tf_op jit(solution)/shard_map/pallas_call | solution.py:193
  37.5 3.4 %all-to-all-start.3 = ((bf16[8,80,256]{2,1,0:T(8,128)(2,1)}), bf16[8,80,256]{2,1,0:T(8,128)(2,1)S(1)}, u32[]{:S(2)}, u32[]{:S(2)}) async-start(bf16[8,80,256]{2,1,0:T(8,128)(2,1)} %get-tuple-element.12.context_ref), calls=%async_computation.3 | async-start | bytes 655360 | tf_op jit(solution)/shard_map/all_to_all | solution.py:383
  41.0 3.7 %collective-permute-start.8 = (bf16[16,5120]{1,0:T(8,128)(2,1)S(1)}, bf16[16,5120]{1,0:T(8,128)(2,1)S(1)}, u32[]{:S(2)}, u32[]{:S(2)}) collective-permute-start(bf16[16,5120]{1,0:T(8,128)(2,1)S(1)} %get-tuple-element.18), channel_id=1, source_target_pairs={{0,3},{1,2},{2,1},{3,0},{4,7},{5,6},{6,5},{7,4},{8,11},{9,10},{10,... | collective-permute-start | bytes 491528 | tf_op jit(solution)/shard_map/ppermute | solution.py:344
  45.4 4.5 %collective-permute-done.8.refs_3_ = bf16[16,5120]{1,0:T(8,128)(2,1)S(1)} collective-permute-done((bf16[16,5120]{1,0:T(8,128)(2,1)S(1)}, bf16[16,5120]{1,0:T(8,128)(2,1)S(1)}, u32[]{:S(2)}, u32[]{:S(2)}) %collective-permute-start.8) | collective-permute-done | bytes 163872 | tf_op jit(solution)/shard_map/ppermute | solution.py:344
  50.6 8.5 %collective-permute-done.7.refs_2_ = bf16[16,5120]{1,0:T(8,128)(2,1)S(1)} collective-permute-done((bf16[16,5120]{1,0:T(8,128)(2,1)S(1)}, bf16[16,5120]{1,0:T(8,128)(2,1)S(1)}, u32[]{:S(2)}, u32[]{:S(2)}) %collective-permute-start.7) | collective-permute-done | bytes 163872 | tf_op jit(solution)/shard_map/ppermute | solution.py:344
  63.2 2.7 %shard_map.118 = bf16[1280,640]{1,0:T(8,128)(2,1)S(1)} custom-call(s32[4]{0:T(128)S(1)} %iota_xor_fusion.place_ref, bf16[8,80,256]{2,1,0:T(8,128)(2,1)S(1)} %all-to-all-done.3.context_ref, bf16[16,5120]{1,0:T(8,128)(2,1)S(1)} %get-tuple-element.21.refs_0_, bf16[16,5120]{1,0:T(8,128)(2,1)S(1)} %copy-done.12, bf16[16,5120]{1,0:T(8,128)(2,1)S(1)} %copy-done.10, ...), custom_call_target="tpu_custom_call" | custom-call | tf_op jit(solution)/shard_map/pallas_call | solution.py:333
  65.9 1.0 dynamic-slice_bitcast_fusion
  66.9 2.7 %collective-permute-done.9 = bf16[4,160,640]{2,1,0:T(8,128)(2,1)} collective-permute-done((bf16[4,160,640]{2,1,0:T(8,128)(2,1)}, bf16[4,160,640]{2,1,0:T(8,128)(2,1)}, u32[]{:S(2)}, u32[]{:S(2)}) %collective-permute-start.9) | collective-permute-done | bytes 819232 | tf_op jit(solution)/shard_map/ppermute | solution.py:344
  69.6 1.3 fusion
  71.0 1.7 %collective-permute-start.10 = (bf16[2,160,640]{2,1,0:T(8,128)(2,1)S(1)}, bf16[2,160,640]{2,1,0:T(8,128)(2,1)S(1)}, u32[]{:S(2)}, u32[]{:S(2)}) collective-permute-start(bf16[2,160,640]{2,1,0:T(8,128)(2,1)S(1)} %dynamic-slice_bitcast_fusion.1), channel_id=1, source_target_pairs={{0,8},{4,12},{8,0},{12,4},{16,24},{20,28},{24,16},{28,20},{1,9},{5... | collective-permute-start | bytes 1228808 | tf_op jit(solution)/shard_map/ppermute | solution.py:344
  73.3 2.5 %collective-permute-start.5 = (bf16[64,640]{1,0:T(8,128)(2,1)}, bf16[64,640]{1,0:T(8,128)(2,1)S(1)}, u32[]{:S(2)}, u32[]{:S(2)}) collective-permute-start(bf16[64,640]{1,0:T(8,128)(2,1)} %get-tuple-element.25), channel_id=1, source_target_pairs={{0,3},{1,2},{2,1},{3,0},{4,7},{5,6},{6,5},{7,4},{8,11},{9,10},{10,... | collective-permute-start | bytes 245768 | tf_op jit(solution)/shard_map/ppermute | solution.py:344
  75.8 1.9 %collective-permute-start.3 = (bf16[64,640]{1,0:T(8,128)(2,1)S(1)}, bf16[64,640]{1,0:T(8,128)(2,1)S(1)}, u32[]{:S(2)}, u32[]{:S(2)}) collective-permute-start(bf16[64,640]{1,0:T(8,128)(2,1)S(1)} %get-tuple-element.27), channel_id=1, source_target_pairs={{0,1},{1,0},{2,3},{3,2},{4,5},{5,4},{6,7},{7,6},{8,9},{9,8},{10,11... | collective-permute-start | bytes 245768 | tf_op jit(solution)/shard_map/ppermute | solution.py:344
  77.7 3.0 %collective-permute-done.5.refs_3_ = bf16[64,640]{1,0:T(8,128)(2,1)S(1)} collective-permute-done((bf16[64,640]{1,0:T(8,128)(2,1)}, bf16[64,640]{1,0:T(8,128)(2,1)S(1)}, u32[]{:S(2)}, u32[]{:S(2)}) %collective-permute-start.5) | collective-permute-done | bytes 81952 | tf_op jit(solution)/shard_map/ppermute | solution.py:344
  80.7 2.4 %collective-permute-done.4.refs_2_ = bf16[64,640]{1,0:T(8,128)(2,1)S(1)} collective-permute-done((bf16[64,640]{1,0:T(8,128)(2,1)S(1)}, bf16[64,640]{1,0:T(8,128)(2,1)S(1)}, u32[]{:S(2)}, u32[]{:S(2)}) %collective-permute-start.4) | collective-permute-done | bytes 81952 | tf_op jit(solution)/shard_map/ppermute | solution.py:344
  83.1 1.4 %shard_map.114 = bf16[8,80,256]{2,1,0:T(8,128)(2,1)} custom-call(s32[4]{0:T(128)S(1)} %iota_xor_fusion.place_ref, bf16[64,640]{1,0:T(8,128)(2,1)S(1)} %get-tuple-element.28.refs_0_, bf16[64,640]{1,0:T(8,128)(2,1)S(1)} %collective-permute-done.3.refs_1_, bf16[64,640]{1,0:T(8,128)(2,1)S(1)} %collective-permute-done.4.refs_2_, ...), custom_call_target="tpu_custom_call" | custom-call | tf_op jit(solution)/shard_map/pallas_call | solution.py:133
  84.5 3.4 %all-to-all-start.1 = ((bf16[8,80,256]{2,1,0:T(8,128)(2,1)}), bf16[8,80,256]{2,1,0:T(8,128)(2,1)S(1)}, u32[]{:S(2)}, u32[]{:S(2)}) async-start(bf16[8,80,256]{2,1,0:T(8,128)(2,1)} %shard_map.114), calls=%async_computation.1 | async-start | bytes 655360 | tf_op jit(solution)/shard_map/all_to_all | solution.py:367
  88.1 2.0 %collective-permute-start.11 = (bf16[1,160,640]{2,1,0:T(8,128)(2,1)S(1)}, bf16[1,160,640]{2,1,0:T(8,128)(2,1)S(1)}, u32[]{:S(2)}, u32[]{:S(2)}) collective-permute-start(bf16[1,160,640]{2,1,0:T(8,128)(2,1)S(1)} %constant_dynamic-slice_fusion), channel_id=1, source_target_pairs={{0,16},{4,20},{8,24},{12,28},{16,0},{20,4},{24,8},{28,12},{1,17},{... | collective-permute-start | bytes 614408 | tf_op jit(solution)/shard_map/ppermute | solution.py:344
  90.1 5.4 %all-to-all-done.1.grad_ref = bf16[8,80,256]{2,1,0:T(8,128)(2,1)S(1)} async-done(((bf16[8,80,256]{2,1,0:T(8,128)(2,1)}), bf16[8,80,256]{2,1,0:T(8,128)(2,1)S(1)}, u32[]{:S(2)}, u32[]{:S(2)}) %all-to-all-start.1) | async-done | bytes 327712 | tf_op jit(solution)/shard_map/all_to_all | solution.py:367
  95.6 19.2 %shard_map.116 = bf16[8,240,256]{2,1,0:T(8,128)(2,1)} custom-call(s32[1]{0:T(128)} %constant.107.clone.1.first_ref, bf16[8,256,256]{2,1,0:T(8,128)(2,1)S(1)} %all-to-all-done.all_ref, bf16[8,80,256]{2,1,0:T(8,128)(2,1)S(1)} %all-to-all-done.1.grad_ref, bf16[8,80,256]{2,1,0:T(8,128)(2,1)} %get-tuple-element.12.context_ref, ...), custom_call_target="tpu_custom_call" | custom-call | tf_op jit(solution)/shard_map/pallas_call | solution.py:254
  114.8 3.6 %all-to-all-start.2 = ((bf16[8,240,256]{2,1,0:T(8,128)(2,1)}), bf16[8,240,256]{2,1,0:T(8,128)(2,1)S(1)}, u32[]{:S(2)}, u32[]{:S(2)}) async-start(bf16[8,240,256]{2,1,0:T(8,128)(2,1)} %shard_map.116), calls=%async_computation.2 | async-start | bytes 1966080 | tf_op jit(solution)/shard_map/all_to_all | solution.py:385
  120.2 1.8 %collective-permute-start.14 = (bf16[160,160]{1,0:T(8,128)(2,1)S(1)}, bf16[160,160]{1,0:T(8,128)(2,1)S(1)}, u32[]{:S(2)}, u32[]{:S(2)}) collective-permute-start(bf16[160,160]{1,0:T(8,128)(2,1)S(1)} %get-tuple-element.23), channel_id=1, source_target_pairs={{0,3},{1,2},{2,1},{3,0},{4,7},{5,6},{6,5},{7,4},{8,11},{9,10},{10,... | collective-permute-start | bytes 153608 | tf_op jit(solution)/shard_map/ppermute | solution.py:344
  122.0 1.0 collective-permute-start.13
  123.0 10.0 %all-to-all-done.2.all_ref = bf16[8,240,256]{2,1,0:T(8,128)(2,1)S(1)} async-done(((bf16[8,240,256]{2,1,0:T(8,128)(2,1)}), bf16[8,240,256]{2,1,0:T(8,128)(2,1)S(1)}, u32[]{:S(2)}, u32[]{:S(2)}) %all-to-all-start.2) | async-done | bytes 983072 | tf_op jit(solution)/shard_map/all_to_all | solution.py:385
  133.0 1.1 shard_map.117
  (75 shorter events, 15.2 us)
Async XLA Ops:
  1.9 1.0 copy-start.4
  2.9 1.0 copy-start.5
  3.9 1.0 copy-start.6
  4.8 7.0 %copy-start.15 = (s32[1,64]{1,0:T(1,128)S(1)}, s32[1,64]{1,0:T(1,128)}, u32[]{:S(2)}) copy-start(s32[1,64]{1,0:T(1,128)} %param.13) | copy-start | bytes 772
  4.8 12.9 %copy-start = (bf16[64,5120]{1,0:T(8,128)(2,1)S(1)}, bf16[64,5120]{1,0:T(8,128)(2,1)}, u32[]{:S(2)}) copy-start(bf16[64,5120]{1,0:T(8,128)(2,1)} %grad_ref.3) | copy-start | bytes 1966084
  4.8 12.9 %copy-start.1 = (bf16[640,1280]{1,0:T(8,128)(2,1)S(1)}, bf16[640,1280]{1,0:T(8,128)(2,1)}, u32[]{:S(2)}) copy-start(bf16[640,1280]{1,0:T(8,128)(2,1)} %weight_ref.1) | copy-start | bytes 4915204
  6.1 20.6 %all-to-all-start = ((bf16[8,256,256]{2,1,0:T(8,128)(2,1)}), bf16[8,256,256]{2,1,0:T(8,128)(2,1)S(1)}, u32[]{:S(2)}, u32[]{:S(2)}) async-start(bf16[8,256,256]{2,1,0:T(8,128)(2,1)} %shard_map.111), calls=%async_computation | async-start | bytes 2097152 | tf_op jit(solution)/shard_map/all_to_all | solution.py:367
  13.3 7.2 %collective-permute-start.2 = (s32[16]{0:T(128)S(1)}, s32[16]{0:T(128)S(1)}, u32[]{:S(2)}, u32[]{:S(2)}) collective-permute-start(s32[16]{0:T(128)S(1)} %get-tuple-element.30), channel_id=1, source_target_pairs={{0,3},{1,2},{2,1},{3,0},{4,7},{5,6},{6,5},{7,4},{8,11},{9,10},{10,... | collective-permute-start | bytes 200 | tf_op jit(solution)/shard_map/ppermute | solution.py:344
  17.0 4.4 %collective-permute-start.1 = (s32[16]{0:T(128)S(1)}, s32[16]{0:T(128)S(1)}, u32[]{:S(2)}, u32[]{:S(2)}) collective-permute-start(s32[16]{0:T(128)S(1)} %get-tuple-element.31), channel_id=1, source_target_pairs={{0,2},{1,3},{2,0},{3,1},{4,6},{5,7},{6,4},{7,5},{8,10},{9,11},{10,... | collective-permute-start | bytes 200 | tf_op jit(solution)/shard_map/ppermute | solution.py:344
  17.0 4.4 %collective-permute-start = (s32[16]{0:T(128)S(1)}, s32[16]{0:T(128)S(1)}, u32[]{:S(2)}, u32[]{:S(2)}) collective-permute-start(s32[16]{0:T(128)S(1)} %get-tuple-element.32), channel_id=1, source_target_pairs={{0,1},{1,0},{2,3},{3,2},{4,5},{5,4},{6,7},{7,6},{8,9},{9,8},{10,11... | collective-permute-start | bytes 200 | tf_op jit(solution)/shard_map/ppermute | solution.py:344
  19.8 0.7 copy-start.2
  21.7 1.0 copy-start.3
  37.5 23.0 %all-to-all-start.3 = ((bf16[8,80,256]{2,1,0:T(8,128)(2,1)}), bf16[8,80,256]{2,1,0:T(8,128)(2,1)S(1)}, u32[]{:S(2)}, u32[]{:S(2)}) async-start(bf16[8,80,256]{2,1,0:T(8,128)(2,1)} %get-tuple-element.12.context_ref), calls=%async_computation.3 | async-start | bytes 655360 | tf_op jit(solution)/shard_map/all_to_all | solution.py:383
  41.0 9.0 %collective-permute-start.8 = (bf16[16,5120]{1,0:T(8,128)(2,1)S(1)}, bf16[16,5120]{1,0:T(8,128)(2,1)S(1)}, u32[]{:S(2)}, u32[]{:S(2)}) collective-permute-start(bf16[16,5120]{1,0:T(8,128)(2,1)S(1)} %get-tuple-element.18), channel_id=1, source_target_pairs={{0,3},{1,2},{2,1},{3,0},{4,7},{5,6},{6,5},{7,4},{8,11},{9,10},{10,... | collective-permute-start | bytes 491528 | tf_op jit(solution)/shard_map/ppermute | solution.py:344
  44.7 14.5 %collective-permute-start.7 = (bf16[16,5120]{1,0:T(8,128)(2,1)S(1)}, bf16[16,5120]{1,0:T(8,128)(2,1)S(1)}, u32[]{:S(2)}, u32[]{:S(2)}) collective-permute-start(bf16[16,5120]{1,0:T(8,128)(2,1)S(1)} %get-tuple-element.19), channel_id=1, source_target_pairs={{0,2},{1,3},{2,0},{3,1},{4,6},{5,7},{6,4},{7,5},{8,10},{9,11},{10,... | collective-permute-start | bytes 491528 | tf_op jit(solution)/shard_map/ppermute | solution.py:344
  44.7 15.1 %collective-permute-start.6 = (bf16[16,5120]{1,0:T(8,128)(2,1)S(1)}, bf16[16,5120]{1,0:T(8,128)(2,1)S(1)}, u32[]{:S(2)}, u32[]{:S(2)}) collective-permute-start(bf16[16,5120]{1,0:T(8,128)(2,1)S(1)} %get-tuple-element.20), channel_id=1, source_target_pairs={{0,1},{1,0},{2,3},{3,2},{4,5},{5,4},{6,7},{7,6},{8,9},{9,8},{10,11... | collective-permute-start | bytes 491528 | tf_op jit(solution)/shard_map/ppermute | solution.py:344
  60.5 0.9 copy-start.8
  61.4 0.9 copy-start.10
  62.3 0.9 copy-start.12
  66.9 2.7 %collective-permute-start.9 = (bf16[4,160,640]{2,1,0:T(8,128)(2,1)}, bf16[4,160,640]{2,1,0:T(8,128)(2,1)}, u32[]{:S(2)}, u32[]{:S(2)}) collective-permute-start(bf16[4,160,640]{2,1,0:T(8,128)(2,1)} %dynamic-slice_bitcast_fusion), channel_id=1, source_target_pairs={{0,4},{4,0},{8,12},{12,8},{16,20},{20,16},{24,28},{28,24},{1,5},{5... | collective-permute-start | bytes 2457608 | tf_op jit(solution)/shard_map/ppermute | solution.py:344
  70.9 4.9 %copy-start.13 = (bf16[4,160,640]{2,1,0:T(8,128)(2,1)}, bf16[4,160,640]{2,1,0:T(8,128)(2,1)S(1)}, u32[]{:S(2)}) copy-start(bf16[4,160,640]{2,1,0:T(8,128)(2,1)S(1)} %fusion) | copy-start | bytes 2457604
  71.0 17.0 %collective-permute-start.10 = (bf16[2,160,640]{2,1,0:T(8,128)(2,1)S(1)}, bf16[2,160,640]{2,1,0:T(8,128)(2,1)S(1)}, u32[]{:S(2)}, u32[]{:S(2)}) collective-permute-start(bf16[2,160,640]{2,1,0:T(8,128)(2,1)S(1)} %dynamic-slice_bitcast_fusion.1), channel_id=1, source_target_pairs={{0,8},{4,12},{8,0},{12,4},{16,24},{20,28},{24,16},{28,20},{1,9},{5... | collective-permute-start | bytes 1228808 | tf_op jit(solution)/shard_map/ppermute | solution.py:344
  73.3 7.4 %collective-permute-start.5 = (bf16[64,640]{1,0:T(8,128)(2,1)}, bf16[64,640]{1,0:T(8,128)(2,1)S(1)}, u32[]{:S(2)}, u32[]{:S(2)}) collective-permute-start(bf16[64,640]{1,0:T(8,128)(2,1)} %get-tuple-element.25), channel_id=1, source_target_pairs={{0,3},{1,2},{2,1},{3,0},{4,7},{5,6},{6,5},{7,4},{8,11},{9,10},{10,... | collective-permute-start | bytes 245768 | tf_op jit(solution)/shard_map/ppermute | solution.py:344
  75.8 7.3 %collective-permute-start.4 = (bf16[64,640]{1,0:T(8,128)(2,1)S(1)}, bf16[64,640]{1,0:T(8,128)(2,1)S(1)}, u32[]{:S(2)}, u32[]{:S(2)}) collective-permute-start(bf16[64,640]{1,0:T(8,128)(2,1)S(1)} %get-tuple-element.26), channel_id=1, source_target_pairs={{0,2},{1,3},{2,0},{3,1},{4,6},{5,7},{6,4},{7,5},{8,10},{9,11},{10,... | collective-permute-start | bytes 245768 | tf_op jit(solution)/shard_map/ppermute | solution.py:344
  75.8 12.1 %copy-start.14 = (bf16[4,160,640]{2,1,0:T(8,128)(2,1)S(1)}, bf16[4,160,640]{2,1,0:T(8,128)(2,1)}, u32[]{:S(2)}) copy-start(bf16[4,160,640]{2,1,0:T(8,128)(2,1)} %copy-done.13) | copy-start | bytes 2457604
  75.8 7.3 %collective-permute-start.3 = (bf16[64,640]{1,0:T(8,128)(2,1)S(1)}, bf16[64,640]{1,0:T(8,128)(2,1)S(1)}, u32[]{:S(2)}, u32[]{:S(2)}) collective-permute-start(bf16[64,640]{1,0:T(8,128)(2,1)S(1)} %get-tuple-element.27), channel_id=1, source_target_pairs={{0,1},{1,0},{2,3},{3,2},{4,5},{5,4},{6,7},{7,6},{8,9},{9,8},{10,11... | collective-permute-start | bytes 245768 | tf_op jit(solution)/shard_map/ppermute | solution.py:344
  84.5 11.1 %all-to-all-start.1 = ((bf16[8,80,256]{2,1,0:T(8,128)(2,1)}), bf16[8,80,256]{2,1,0:T(8,128)(2,1)S(1)}, u32[]{:S(2)}, u32[]{:S(2)}) async-start(bf16[8,80,256]{2,1,0:T(8,128)(2,1)} %shard_map.114), calls=%async_computation.1 | async-start | bytes 655360 | tf_op jit(solution)/shard_map/all_to_all | solution.py:367
  88.1 30.2 %collective-permute-start.11 = (bf16[1,160,640]{2,1,0:T(8,128)(2,1)S(1)}, bf16[1,160,640]{2,1,0:T(8,128)(2,1)S(1)}, u32[]{:S(2)}, u32[]{:S(2)}) collective-permute-start(bf16[1,160,640]{2,1,0:T(8,128)(2,1)S(1)} %constant_dynamic-slice_fusion), channel_id=1, source_target_pairs={{0,16},{4,20},{8,24},{12,28},{16,0},{20,4},{24,8},{28,12},{1,17},{... | collective-permute-start | bytes 614408 | tf_op jit(solution)/shard_map/ppermute | solution.py:344
  114.8 18.2 %all-to-all-start.2 = ((bf16[8,240,256]{2,1,0:T(8,128)(2,1)}), bf16[8,240,256]{2,1,0:T(8,128)(2,1)S(1)}, u32[]{:S(2)}, u32[]{:S(2)}) async-start(bf16[8,240,256]{2,1,0:T(8,128)(2,1)} %shard_map.116), calls=%async_computation.2 | async-start | bytes 1966080 | tf_op jit(solution)/shard_map/all_to_all | solution.py:385
  119.4 14.6 %collective-permute-start.12 = (bf16[160,160]{1,0:T(8,128)(2,1)S(1)}, bf16[160,160]{1,0:T(8,128)(2,1)S(1)}, u32[]{:S(2)}, u32[]{:S(2)}) collective-permute-start(bf16[160,160]{1,0:T(8,128)(2,1)S(1)} %get-tuple-element.22), channel_id=1, source_target_pairs={{0,1},{1,0},{2,3},{3,2},{4,5},{5,4},{6,7},{7,6},{8,9},{9,8},{10,11... | collective-permute-start | bytes 153608 | tf_op jit(solution)/shard_map/ppermute | solution.py:344
  120.2 13.8 %collective-permute-start.14 = (bf16[160,160]{1,0:T(8,128)(2,1)S(1)}, bf16[160,160]{1,0:T(8,128)(2,1)S(1)}, u32[]{:S(2)}, u32[]{:S(2)}) collective-permute-start(bf16[160,160]{1,0:T(8,128)(2,1)S(1)} %get-tuple-element.23), channel_id=1, source_target_pairs={{0,3},{1,2},{2,1},{3,0},{4,7},{5,6},{6,5},{7,4},{8,11},{9,10},{10,... | collective-permute-start | bytes 153608 | tf_op jit(solution)/shard_map/ppermute | solution.py:344
  122.0 12.1 %collective-permute-start.13 = (bf16[160,160]{1,0:T(8,128)(2,1)S(1)}, bf16[160,160]{1,0:T(8,128)(2,1)S(1)}, u32[]{:S(2)}, u32[]{:S(2)}) collective-permute-start(bf16[160,160]{1,0:T(8,128)(2,1)S(1)} %get-tuple-element.24), channel_id=1, source_target_pairs={{0,2},{1,3},{2,0},{3,1},{4,6},{5,7},{6,4},{7,5},{8,10},{9,11},{10,... | collective-permute-start | bytes 153608 | tf_op jit(solution)/shard_map/ppermute | solution.py:344
  (3 other events, 2.0 us)

commit v2 on v1

v2 whole, which is shorter than its diff:
```python
import functools
import math

import jax
import jax.numpy as jnp
from jax import lax
from jax.experimental import pallas as pl
from jax.experimental.pallas import tpu as pltpu
from jax.sharding import PartitionSpec as P

HEADS = 8
HD = 80
MERGE = 4
INFO = 16
CORES = 2
HIDE = -1e30
SCALING = 1.0 / math.sqrt(HD)
F32 = jnp.float32
BF16 = jnp.bfloat16
VMEM = pl.BlockSpec(memory_space=pltpu.VMEM)
SMEM = pl.BlockSpec(memory_space=pltpu.SMEM)
PARAMS = pltpu.CompilerParams(vmem_limit_bytes=24 * 2**20)
WHOLE = pltpu.CompilerParams(vmem_limit_bytes=60 * 2**20)


def cost(micros):
    return pl.CostEstimate(flops=int(micros * 1.15e9), bytes_accessed=0, transcendentals=0)


def dot_nn(left, right):
    return lax.dot_general(left, right, (((1,), (0,)), ((), ())), preferred_element_type=F32)


def dot_nt(left, right):
    return lax.dot_general(left, right, (((1,), (1,)), ((), ())), preferred_element_type=F32)


def dot_tn(left, right):
    return lax.dot_general(left, right, (((0,), (0,)), ((), ())), preferred_element_type=F32)


def pack_kernel(start_ref, size_ref, query_ref, key_ref, value_ref, out_ref, *, groups):
    rows, width = query_ref.shape
    feat = width // groups
    for slot, ref in enumerate((query_ref, key_ref, value_ref)):
        turned = ref[...].T
        for g in range(groups):
            out_ref[g, slot * feat : (slot + 1) * feat, :] = turned[g * feat : (g + 1) * feat, :]
    line = lax.broadcasted_iota(jnp.int32, (INFO, rows), 0)
    page = jnp.where(line < INFO // 2, start_ref[...], size_ref[...])
    info = page.astype(F32).astype(BF16)
    for g in range(groups):
        out_ref[g, 3 * feat :, :] = info


def pack(page_start, page_size, query, key, value, groups):
    rows, width = query.shape
    return pl.pallas_call(
        functools.partial(pack_kernel, groups=groups),
        out_shape=jax.ShapeDtypeStruct((groups, 3 * (width // groups) + INFO, rows), BF16),
        in_specs=[VMEM] * 5,
        out_specs=VMEM,
        cost_estimate=cost(2.6),
        compiler_params=WHOLE,
    )(page_start, page_size, query, key, value)


def project_kernel(weight_ref, *refs, groups):
    parts, out_ref = refs[:-1], refs[-1]
    width = weight_ref.shape[1]
    grads = jnp.concatenate([ref[...] for ref in parts], axis=0)
    merged = grads.shape[0]
    total = merged * MERGE
    parted = jnp.concatenate([grads[:, c * width : (c + 1) * width] for c in range(MERGE)], axis=0)
    source = dot_nt(weight_ref[...], parted).astype(BF16)
    target = row_order(total, len(parts))
    column = lax.broadcasted_iota(jnp.int32, (total, total), 1)
    turned = dot_nn(source, (column == target).astype(BF16)).astype(BF16)
    feat = turned.shape[0] // groups
    for g in range(groups):
        out_ref[g] = turned[g * feat : (g + 1) * feat, :]


def row_order(total, lanes):
    merged = total // MERGE
    portion = merged // lanes
    line = lax.broadcasted_iota(jnp.int32, (total, 1), 0)
    within = line % merged
    source = lax.axis_index("dp") ^ (within // portion)
    return (source * portion + within % portion) * MERGE + line // merged


def project(weight, parts, groups):
    rows = sum(part.shape[0] for part in parts) * MERGE
    return pl.pallas_call(
        functools.partial(project_kernel, groups=groups),
        out_shape=jax.ShapeDtypeStruct((groups, weight.shape[0] // groups, rows), BF16),
        in_specs=[VMEM] * (1 + len(parts)),
        out_specs=VMEM,
        cost_estimate=cost(1.0),
        compiler_params=PARAMS,
    )(weight, *parts)


def wanted_rows(asked_refs, lane, base, merged, each):
    lanes = len(asked_refs)
    portion = merged // lanes
    asked = jnp.concatenate([ref[...] for ref in asked_refs], axis=0) - base
    asked = jnp.concatenate([asked.astype(F32), jnp.zeros((8, merged), F32)], axis=0).astype(BF16)
    line = lax.broadcasted_iota(jnp.int32, (merged * each, merged), 0)
    place = lax.broadcasted_iota(jnp.int32, (merged * each, merged), 1)
    hit = (place == lane * portion + (line // each) % portion).astype(BF16)
    every = dot_nt(hit, asked)
    partner = lax.broadcasted_iota(jnp.int32, every.shape, 1)
    slot = lax.broadcasted_iota(jnp.int32, every.shape, 0) // (each * portion)
    return jnp.sum(jnp.where(partner == slot, every, 0.0), axis=1, keepdims=True).astype(jnp.int32)


def first_held(merged, lanes):
    return (lax.axis_index("blk") * lanes + lax.axis_index("dp")) * merged


def pick_kernel(grad_ref, *refs):
    lanes = len(refs) // 2
    merged = grad_ref.shape[0]
    portion = merged // lanes
    every = lax.broadcasted_iota(jnp.int32, (merged, merged), 1)
    target = wanted_rows(refs[:lanes], lax.axis_index("dp"), first_held(merged, lanes), merged, 1)
    picked = dot_nn((every == target).astype(BF16), grad_ref[...])
    for k, ref in enumerate(refs[lanes:]):
        ref[...] = picked[k * portion : (k + 1) * portion, :].astype(BF16)


def pick(llm_grad, asked):
    lanes = len(asked)
    part = jax.ShapeDtypeStruct((llm_grad.shape[0] // lanes, llm_grad.shape[1]), BF16)
    return pl.pallas_call(
        pick_kernel,
        out_shape=(part,) * lanes,
        in_specs=[VMEM] * (1 + lanes),
        out_specs=(VMEM,) * lanes,
        cost_estimate=cost(0.5),
        compiler_params=PARAMS,
    )(llm_grad, *asked)


def hidden_row(ref, block, key_block, feat):
    info = ref[block, 3 * feat : 3 * feat + INFO, :].astype(F32)
    first = info[0:1, :]
    count = info[INFO // 2 : INFO // 2 + 1, :]
    return jnp.where((first <= key_block) & (first + count > key_block), 0.0, HIDE)


def shared_block(index, shares):
    return index * shares + lax.axis_index("blk") % shares if shares > 1 else index


def forward_kernel(all_ref, *refs, heads, shares):
    blocks, _, rows = all_ref.shape
    chips = blocks // CORES
    context_refs = refs[:chips]
    mixes, log_ref, keys, even, odd = refs[chips:]
    count = blocks // shares
    feat = heads * HD
    for h in range(heads):
        own = slice(h * HD, (h + 1) * HD)
        value_own = slice(2 * feat + h * HD, 2 * feat + (h + 1) * HD)
        for j in range(blocks):
            keys[j * rows : (j + 1) * rows, :] = all_ref[
                j, feat + h * HD : feat + (h + 1) * HD, :
            ].T

        def score(index, j, into):
            b = shared_block(index, shares)
            part = dot_nn(keys[j * rows : (j + 1) * rows, :], all_ref[b, own, :])
            into[j * rows : (j + 1) * rows, :] = part
            return jnp.max(part, axis=0, keepdims=True) + hidden_row(all_ref, b, j, feat)

        def one_block(index, following, held, into, top):
            b = shared_block(index, shares)
            base = top * SCALING
            total, mixed, waiting, next_top = None, None, None, None
            for j in range(blocks + 1):
                weight = None
                if j < blocks:
                    part_top = score(following, j, into)
                    next_top = part_top if next_top is None else jnp.maximum(next_top, part_top)
                    weight = jnp.exp(
                        held[j * rows : (j + 1) * rows, :] * SCALING
                        + (hidden_row(all_ref, b, j, feat) - base)
                    )
                    part_sum = jnp.sum(weight, axis=0, keepdims=True)
                    total = part_sum if total is None else total + part_sum
                    weight = weight.astype(BF16)
                if waiting is not None:
                    part_mix = dot_nn(all_ref[j - 1, value_own, :], waiting)
                    mixed = part_mix if mixed is None else mixed + part_mix
                waiting = weight
            mixes[index, own, :] = (mixed / total).astype(BF16)
            log_ref[index, h : h + 1, :] = base + jnp.log(total)
            return next_top

        def step(pair, top):
            top = one_block(2 * pair, 2 * pair + 1, even, odd, top)
            return one_block(2 * pair + 1, jnp.minimum(2 * pair + 2, count - 1), odd, even, top)

        top = score(0, 0, even)
        for j in range(1, blocks):
            top = jnp.maximum(top, score(0, j, even))
        if count % 2:
            raise ValueError("odd count")
        lax.fori_loop(0, count // 2, step, top)
    me = lax.axis_index("blk")
    for k, ref in enumerate(context_refs):
        for c in range(CORES):
            b = ((me // CORES) ^ k) * CORES + c
            mix = mixes[b // shares]
            if shares > 1:
                mix = jnp.where(b % shares == me % shares, mix.astype(F32), 0.0).astype(BF16)
            ref[c] = mix


def forward(gathered, heads, shares):
    blocks, _, rows = gathered.shape
    chips = blocks // CORES
    count = blocks // shares
    return pl.pallas_call(
        functools.partial(forward_kernel, heads=heads, shares=shares),
        out_shape=(
            *([jax.ShapeDtypeStruct((CORES, heads * HD, rows), BF16)] * chips),
            jax.ShapeDtypeStruct((count, heads * HD, rows), BF16),
            jax.ShapeDtypeStruct((count, heads, rows), F32),
        ),
        in_specs=[VMEM],
        out_specs=(VMEM,) * (chips + 2),
        scratch_shapes=[
            pltpu.VMEM((blocks * rows, HD), BF16),
            pltpu.VMEM((blocks * rows, rows), F32),
            pltpu.VMEM((blocks * rows, rows), F32),
        ],
        cost_estimate=cost(7.0),
        compiler_params=PARAMS,
    )(gathered)


def backward_kernel(
    all_ref, grads_ref, context_ref, log_ref, out_ref, query_sum, delta, shift, keys, values,
    *, heads, shares
):
    blocks, _, rows = all_ref.shape
    count = blocks // shares
    feat = heads * HD
    for h in range(heads):
        own = slice(h * HD, (h + 1) * HD)
        key_own = slice(feat + h * HD, feat + (h + 1) * HD)
        value_own = slice(2 * feat + h * HD, 2 * feat + (h + 1) * HD)
        for j in range(blocks):
            keys[j] = all_ref[j, key_own, :].T
            values[j] = all_ref[j, value_own, :].T
        for index in range(count):
            b = shared_block(index, shares)
            product = grads_ref[b, own, :].astype(F32) * context_ref[index, own, :].astype(F32)
            delta[index] = jnp.sum(product, axis=0, keepdims=True)
            query_sum[index] = jnp.zeros((HD, rows), F32)
            for j in range(blocks):
                shift[index, j : j + 1, :] = (
                    hidden_row(all_ref, b, j, feat) - log_ref[index, h : h + 1, :]
                )

        def step(j, carried):
            key, value, turned_key = keys[j], values[j], all_ref[j, key_own, :]
            key_sum = jnp.zeros((HD, rows), F32)
            value_sum = jnp.zeros((HD, rows), F32)

            def products(index):
                b = shared_block(index, shares)
                return dot_nn(key, all_ref[b, own, :]), dot_nn(value, grads_ref[b, own, :])

            def weights(index, score, d_probs):
                probs = jnp.exp(score * SCALING + shift[index, pl.ds(j, 1), :])
                d_scores = probs * (d_probs - delta[index])
                return probs.astype(BF16), d_scores.astype(BF16)

            ready = weights(0, *products(0))
            formed = products(1) if count > 1 else None
            for index in range(count):
                b = shared_block(index, shares)
                probs, d_scores = ready
                following = products(index + 2) if index + 2 < count else None
                if formed is not None:
                    ready = weights(index + 1, *formed)
                formed = following
                value_sum = value_sum + dot_nt(grads_ref[b, own, :], probs)
                key_sum = key_sum + dot_nt(all_ref[b, own, :], d_scores)
                query_sum[index] += dot_nn(turned_key, d_scores)
            out_ref[j, key_own, :] = (key_sum * SCALING).astype(BF16)
            out_ref[j, value_own, :] = value_sum.astype(BF16)
            return carried

        lax.fori_loop(0, blocks, step, 0)
        if shares > 1:
            for b in range(blocks):
                out_ref[b, own, :] = jnp.zeros((HD, rows), BF16)
        for index in range(count):
            out_ref[shared_block(index, shares), own, :] = (query_sum[index] * SCALING).astype(BF16)


def backward(gathered, grads, context, log_total, heads, shares):
    blocks, _, rows = gathered.shape
    count = blocks // shares
    return pl.pallas_call(
        functools.partial(backward_kernel, heads=heads, shares=shares),
        out_shape=jax.ShapeDtypeStruct((blocks, 3 * heads * HD, rows), BF16),
        in_specs=[VMEM] * 4,
        out_specs=VMEM,
        scratch_shapes=[
            pltpu.VMEM((count, HD, rows), F32),
            pltpu.VMEM((count, 1, rows), F32),
            pltpu.VMEM((count, blocks, rows), F32),
            pltpu.VMEM((blocks, rows, HD), BF16),
            pltpu.VMEM((blocks, rows, HD), BF16),
        ],
        cost_estimate=cost(11.0),
        compiler_params=PARAMS,
    )(gathered, grads, context, log_total)


def summed(ref, group, shares, lines):
    if shares == 1:
        return ref[group, lines, :]
    total = ref[group * shares, lines, :].astype(F32)
    for r in range(1, shares):
        total = total + ref[group * shares + r, lines, :].astype(F32)
    return total.astype(BF16)


def unpack_kernel(all_ref, query_ref, key_ref, value_ref, held, *, groups, shares):
    rows, width = query_ref.shape
    feat = width // groups
    for slot, ref in enumerate((query_ref, key_ref, value_ref)):
        for g in range(groups):
            held[g * feat : (g + 1) * feat, :] = summed(
                all_ref, g, shares, slice(slot * feat, (slot + 1) * feat)
            )
        ref[...] = held[...].T


def unpack(returned, width, groups, shares):
    rows = returned.shape[2]
    shape = jax.ShapeDtypeStruct((rows, width), BF16)
    return pl.pallas_call(
        functools.partial(unpack_kernel, groups=groups, shares=shares),
        out_shape=(shape, shape, shape),
        in_specs=[VMEM],
        out_specs=(VMEM, VMEM, VMEM),
        scratch_shapes=[pltpu.VMEM((width, rows), BF16)],
        cost_estimate=cost(1.1),
        compiler_params=PARAMS,
    )(returned)


def deal_kernel(*refs, cores, blocks):
    parts, keep_ref, send_ref = refs[:-2], refs[-2], refs[-1]
    core = lax.axis_index("blk") % cores
    rows = jnp.concatenate([ref[...] for ref in parts], axis=0)
    chunk = rows.shape[1] // MERGE // blocks
    cuts = [
        jnp.concatenate(
            [
                rows[:, (c * blocks + b) * chunk : (c * blocks + b + 1) * chunk]
                for c in range(MERGE)
                for b in range(own, blocks, cores)
            ],
            axis=1,
        )
        for own in range(cores)
    ]
    keep_ref[...] = jnp.where(core == 0, cuts[0], cuts[1])
    send_ref[...] = jnp.where(core == 0, cuts[1], cuts[0])


def deal(parts, blocks, cores):
    rows = sum(part.shape[0] for part in parts)
    half = jax.ShapeDtypeStruct((rows, parts[0].shape[1] // cores), BF16)
    return pl.pallas_call(
        functools.partial(deal_kernel, cores=cores, blocks=blocks),
        out_shape=(half, half),
        in_specs=[VMEM] * len(parts),
        out_specs=(VMEM, VMEM),
        cost_estimate=cost(0.5),
        compiler_params=PARAMS,
    )(*parts)


def weight_kernel(keep_ref, other_ref, *refs, lanes, cores, shares):
    chips = (len(refs) - 2) // (cores + 1)
    context_refs, out_refs, (held, terms) = refs[:-2][: cores * chips], refs[cores * chips : -2], refs[-2:]
    block = lax.axis_index("blk")
    core, chip = block % cores, block // cores
    feat, rows = context_refs[0].shape[1:]
    merged, wide = keep_ref.shape
    width = wide // MERGE
    if shares > 1:
        held[...] = jnp.zeros(held.shape, held.dtype)
    for place, ref in enumerate(context_refs):
        far, k = place // chips, place % chips
        device = (chip ^ k) * cores + (core ^ far)
        lines = pl.ds(pl.multiple_of((device // shares) * feat, feat), feat)
        for i in range(cores):
            if shares > 1:
                held[i, lines, :] += ref[i].astype(F32)
            else:
                held[i, lines, :] = ref[i]
    target = row_order(rows, lanes)
    column = lax.broadcasted_iota(jnp.int32, (rows, rows), 1)
    order = (column == target).astype(BF16)
    ordered, gathered = [], []
    for i in range(cores):
        ordered.append(dot_nt(order, held[i].astype(BF16)).astype(BF16))
        grads = jnp.where(core == i, keep_ref[...], other_ref[...])
        gathered += [grads[:, c * width : (c + 1) * width] for c in range(MERGE)]
    total = dot_tn(jnp.concatenate(gathered, axis=0), jnp.concatenate(ordered, axis=0)).astype(BF16)
    chunk = width // chips
    for i in range(chips):
        terms[i] = total[i * chunk : (i + 1) * chunk, :]
    for k, ref in enumerate(out_refs):
        ref[...] = terms[chip ^ k]


def weight_terms(keep, other, contexts, width, lanes, cores, shares):
    chips = len(contexts) // cores
    rows = contexts[0].shape[2]
    chunk = keep.shape[1] // MERGE // chips
    part = jax.ShapeDtypeStruct((chunk, width), BF16)
    return pl.pallas_call(
        functools.partial(weight_kernel, lanes=lanes, cores=cores, shares=shares),
        out_shape=(part,) * chips,
        in_specs=[VMEM] * (2 + len(contexts)),
        out_specs=(VMEM,) * chips,
        scratch_shapes=[
            pltpu.VMEM((cores, width, rows), BF16 if shares == 1 else F32),
            pltpu.VMEM((chips, chunk, width), BF16),
        ],
        cost_estimate=cost(1.2),
        compiler_params=PARAMS,
    )(keep, other, *contexts)


def total_of(refs):
    total = None
    for ref in refs:
        part = ref[...].astype(F32)
        total = part if total is None else total + part
    return total


def chip_sum_kernel(*refs, lanes):
    count = len(refs) - lanes - 1
    held = refs[-1]
    total = total_of(refs[:count])
    share = total.shape[1] // lanes
    for i in range(lanes):
        held[i] = total[:, i * share : (i + 1) * share]
    for k, ref in enumerate(refs[count:-1]):
        ref[...] = held[lax.axis_index("dp") ^ k].astype(BF16)


def chip_sum(parts, lanes):
    chunk, width = parts[0].shape
    part = jax.ShapeDtypeStruct((chunk, width // lanes), BF16)
    return pl.pallas_call(
        functools.partial(chip_sum_kernel, lanes=lanes),
        out_shape=(part,) * lanes,
        in_specs=[VMEM] * len(parts),
        out_specs=(VMEM,) * lanes,
        scratch_shapes=[pltpu.VMEM((lanes, chunk, width // lanes), F32)],
        cost_estimate=cost(5.0),
        compiler_params=PARAMS,
    )(*parts)


def lane_sum_kernel(*refs):
    refs[-1][...] = total_of(refs[:-1])


def lane_sum(parts):
    return pl.pallas_call(
        lane_sum_kernel,
        out_shape=jax.ShapeDtypeStruct(parts[0].shape, F32),
        in_specs=[VMEM] * len(parts),
        out_specs=VMEM,
        cost_estimate=cost(5.0),
        compiler_params=PARAMS,
    )(*parts)


def swap(array, axis, size, mask):
    return lax.ppermute(array, axis, [(i, i ^ mask) for i in range(size)])


def swap_all(arrays, axis, size, step=1):
    return [arrays[0]] + [swap(arrays[k], axis, size, k * step) for k in range(1, len(arrays))]


def body(
    saved_query, saved_key, saved_value, out_weight, llm_grad, row_source, page_start, page_size
):
    lanes = lax.axis_size("dp")
    cycle = lax.axis_size("blk")
    width = saved_query.shape[2]
    groups = min(HEADS, cycle)
    heads = HEADS // groups
    shares = cycle // groups
    after = lax.optimization_barrier

    asked = swap_all([row_source] * lanes, "dp", lanes)
    packed = pack(page_start, page_size, saved_query[0], saved_key[0], saved_value[0], groups)
    if shares > 1:
        packed = jnp.repeat(packed, shares, axis=0)
    gathered = lax.all_to_all(packed, "blk", split_axis=0, concat_axis=0, tiled=True)
    picked = pick(llm_grad, asked)
    merged_parts = swap_all(picked, "dp", lanes)
    *near, context, log_total = forward(gathered, heads, shares)
    near = swap_all(near, "blk", cycle, CORES)
    merged_parts, log_total = after((merged_parts, log_total))
    grads = project(out_weight, merged_parts, groups)
    merged_parts, grads = after((merged_parts, grads))
    keep, send = deal(merged_parts, cycle, CORES)
    if shares > 1:
        grads = jnp.repeat(grads, shares, axis=0)
    grads = lax.all_to_all(grads, "blk", split_axis=0, concat_axis=0, tiled=True)
    far = [swap(array, "blk", cycle, 1) for array in near]
    other = swap(send, "blk", cycle, 1)
    terms = weight_terms(keep, other, [*near, *far], width, lanes, CORES, shares)
    grads, terms = after((grads, terms))
    results = backward(gathered, grads, context, log_total, heads, shares)
    returned = lax.all_to_all(results, "blk", split_axis=0, concat_axis=0, tiled=True)
    sums, results = after((swap_all(terms, "blk", cycle, CORES), results))
    sums = chip_sum(sums, lanes)
    weight_grad = lane_sum(swap_all(sums, "dp", lanes))
    query_grad, key_grad, value_grad = unpack(returned, width, groups, shares)
    return (query_grad[None], key_grad[None], value_grad[None], weight_grad)


def solution(mesh):
    in_specs = (
        P("dp", "blk", None),
        P("dp", "blk", None),
        P("dp", "blk", None),
        P(),
        P(("blk", "dp"), None),
        P("dp", "blk"),
        P("dp", "blk"),
        P("dp", "blk"),
    )
    out_specs = (P("dp", "blk", None), P("dp", "blk", None), P("dp", "blk", None), P("blk", "dp"))
    return jax.shard_map(body, mesh=mesh, in_specs=in_specs, out_specs=out_specs, check_vma=False)
```

time: 136 us -> 87.3 us (0.64)
  waiting for transfers between devices: 40.8 us -> 20.2 us
  Pallas kernels: 39.1 us -> 27.1 us
  local copies, waits for them, and re-layouts: 13.3 us -> 3.02 us
  other arithmetic: 3.24 us -> 0 us
  starting transfers between devices: 36.1 us -> 34.5 us
    pallas_call x1, Pallas kernels: 19.2 us -> 10.9 us  [backward(): pl.pallas_call(functools.partial(backward_kernel, heads=heads, shares=sha...]
    all_to_all x1, waiting for transfers between devices: 9.98 us -> 1.94 us  [body(): lax.all_to_all(results, 'blk', split_axis=0, concat_axis=0, tiled=True)]
    unnamed x33 -> x22, local copies, waits for them, and re-layouts: 9.88 us -> 3.02 us
    ppermute x15 -> x20, waiting for transfers between devices: 21.9 us -> 15.3 us  [swap(): return lax.ppermute(array, axis, [(i, i ^ mask) for i in range(size)])]
    all_to_all x3 -> x2, waiting for transfers between devices: 8.92 us -> 2.94 us  [the longest x1 2.94 us: body(): lax.all_to_all(grads, 'blk', split_axis=0, concat_axis=0, tiled=True)]
    pallas_call x1, Pallas kernels: 10.8 us -> 7.62 us  [forward(): pl.pallas_call(functools.partial(forward_kernel, heads=heads, shares=shar...]
    all_to_all x3 -> x2, starting transfers between devices: 12 us -> 9.28 us  [the longest x1 5.3 us: body(): lax.all_to_all(packed, 'blk', split_axis=0, concat_axis=0, tiled=True)]
    squeeze x7 -> x0, local copies, waits for them, and re-layouts: 1.79 us -> none  [the longest x3 1.06 us: body(): send = lax.dynamic_index_in_dim(terms, 1 - side, 1, keepdims=False)]
  transfers between devices with their start and end apart: 19 -> 23, of which waited for: 9 -> 13; matrix products, arithmetic and copies ran while one was open for 3% -> 0% of each run, Pallas kernels for 18% -> 25%
where the time goes in v2:
time: 87.3 us; the launch traced here: 86.9 us
  starting transfers between devices  34.5 us (40%)
  Pallas kernels  27.1 us (31%)
  waiting for transfers between devices  20.2 us (23%)
  local copies, waits for them, and re-layouts  3.02 us (3%)
  between operations  2.03 us (2%)
    ppermute x20, starting transfers between devices, swap(): return lax.ppermute(array, axis, [(i, i ^ mask) for i in range(size)])  21.7 us
    ppermute x20, waiting for transfers between devices, swap(): return lax.ppermute(array, axis, [(i, i ^ mask) for i in range(size)])  15.3 us
    pallas_call x1, Pallas kernels, backward(): pl.pallas_call(functools.partial(backward_kernel, heads=heads, shares=sha...  10.9 us
    pallas_call x1, Pallas kernels, forward(): pl.pallas_call(functools.partial(forward_kernel, heads=heads, shares=shar...  7.62 us
    all_to_all x1, starting transfers between devices, body(): lax.all_to_all(packed, 'blk', split_axis=0, concat_axis=0, tiled=True)  5.3 us
    all_to_all x1, starting transfers between devices, body(): lax.all_to_all(grads, 'blk', split_axis=0, concat_axis=0, tiled=True)  3.98 us
    all_to_all x1, starting transfers between devices, body(): lax.all_to_all(results, 'blk', split_axis=0, concat_axis=0, tiled=True)  3.55 us
    unnamed x22, local copies, waits for them, and re-layouts  3.02 us
  transfers between devices with their start and end apart: 23, of which 13 were waited for; matrix products, arithmetic and copies ran while one was open for 0% of the time, Pallas kernels for 25%

profile of v2, /device:TPU:0, one launch (start us, length us, event | category | flops | bytes accessed | tf_op | source)
XLA Modules:
  0.0 86.9 jit_solution(6762541034045709655)
XLA Ops:
  1.9 2.5 %shard_map.111 = bf16[8,256,256]{2,1,0:T(8,128)(2,1)} custom-call(s32[1,1]{1,0:T(1,128)S(6)} %copy.12.start_ref, s32[1,1]{1,0:T(1,128)S(6)} %copy.13.size_ref, bf16[256,640]{1,0:T(8,128)(2,1)} %bitcast.6, bf16[256,640]{1,0:T(8,128)(2,1)} %bitcast.7, bf16[256,640]{1,0:T(8,128)(2,1)} %bitcast.8), custom_call_target="tpu_custom_call" | custom-call | flops 2990000128 | tf_op jit(solution)/shard_map/pallas_call | solution.py:58
  4.4 5.3 %all-to-all-start = ((bf16[8,256,256]{2,1,0:T(8,128)(2,1)}), bf16[8,256,256]{2,1,0:T(8,128)(2,1)S(1)}, u32[]{:S(2)}, u32[]{:S(2)}) async-start(bf16[8,256,256]{2,1,0:T(8,128)(2,1)} %shard_map.111), calls=%async_computation | async-start | bytes 2097152 | tf_op jit(solution)/shard_map/all_to_all | solution.py:520
  9.7 2.7 %collective-permute-start.1 = (s32[1,64]{1,0:T(1,128)S(1)}, s32[1,64]{1,0:T(1,128)S(1)}, u32[]{:S(2)}, u32[]{:S(2)}) collective-permute-start(s32[1,64]{1,0:T(1,128)S(1)} %copy-done.4), channel_id=1, source_target_pairs={{0,2},{1,3},{2,0},{3,1},{4,6},{5,7},{6,4},{7,5},{8,10},{9,11},{10,... | collective-permute-start | bytes 776 | tf_op jit(solution)/shard_map/ppermute | solution.py:498
  12.4 1.6 %collective-permute-start = (s32[1,64]{1,0:T(1,128)S(1)}, s32[1,64]{1,0:T(1,128)S(1)}, u32[]{:S(2)}, u32[]{:S(2)}) collective-permute-start(s32[1,64]{1,0:T(1,128)S(1)} %copy-done.4), channel_id=1, source_target_pairs={{0,1},{1,0},{2,3},{3,2},{4,5},{5,4},{6,7},{7,6},{8,9},{9,8},{10,11... | collective-permute-start | bytes 776 | tf_op jit(solution)/shard_map/ppermute | solution.py:498
  14.2 1.7 %collective-permute-done.refs_1_ = s32[1,64]{1,0:T(1,128)S(1)} collective-permute-done((s32[1,64]{1,0:T(1,128)S(1)}, s32[1,64]{1,0:T(1,128)S(1)}, u32[]{:S(2)}, u32[]{:S(2)}) %collective-permute-start) | collective-permute-done | bytes 288 | tf_op jit(solution)/shard_map/ppermute | solution.py:498
  15.9 3.4 %collective-permute-done.2.refs_3_ = s32[1,64]{1,0:T(1,128)S(1)} collective-permute-done((s32[1,64]{1,0:T(1,128)S(1)}, s32[1,64]{1,0:T(1,128)S(1)}, u32[]{:S(2)}, u32[]{:S(2)}) %collective-permute-start.2) | collective-permute-done | bytes 288 | tf_op jit(solution)/shard_map/ppermute | solution.py:498
  19.3 1.2 %shard_map.112 = (bf16[16,5120]{1,0:T(8,128)(2,1)S(1)}, bf16[16,5120]{1,0:T(8,128)(2,1)}, bf16[16,5120]{1,0:T(8,128)(2,1)S(1)}, bf16[16,5120]{1,0:T(8,128)(2,1)S(1)}) custom-call(bf16[64,5120]{1,0:T(8,128)(2,1)S(1)} %copy-done.1, s32[1,64]{1,0:T(1,128)S(1)} %copy-done.4, s32[1,64]{1,0:T(1,128)S(1)} %collective-permute-done.refs_1_, ...), custom_call_target="tpu_custom_call" | custom-call | flops 575000000 | tf_op jit(solution)/shard_map/pallas_call | solution.py:137
  20.5 0.7 copy-done.7
  21.1 0.8 collective-permute-start.4
  21.9 3.6 %collective-permute-start.5 = (bf16[16,5120]{1,0:T(8,128)(2,1)S(1)}, bf16[16,5120]{1,0:T(8,128)(2,1)S(1)}, u32[]{:S(2)}, u32[]{:S(2)}) collective-permute-start(bf16[16,5120]{1,0:T(8,128)(2,1)S(1)} %get-tuple-element.49), channel_id=1, source_target_pairs={{0,3},{1,2},{2,1},{3,0},{4,7},{5,6},{6,5},{7,4},{8,11},{9,10},{10,... | collective-permute-start | bytes 491528 | tf_op jit(solution)/shard_map/ppermute | solution.py:498
  25.5 7.6 %shard_map.113 = (bf16[2,80,256]{2,1,0:T(8,128)(2,1)S(1)}, bf16[2,80,256]{2,1,0:T(8,128)(2,1)}, bf16[2,80,256]{2,1,0:T(8,128)(2,1)}, bf16[2,80,256]{2,1,0:T(8,12...) custom-call(bf16[8,256,256]{2,1,0:T(8,128)(2,1)S(1)} %all-to-all-done.all_ref), custom_call_target="tpu_custom_call" | custom-call | flops 8049999872 | tf_op jit(solution)/shard_map/pallas_call | solution.py:227
  33.2 0.6 copy-done.2
  33.8 1.8 %collective-permute-done.4.refs_2_ = bf16[16,5120]{1,0:T(8,128)(2,1)S(1)} collective-permute-done((bf16[16,5120]{1,0:T(8,128)(2,1)S(1)}, bf16[16,5120]{1,0:T(8,128)(2,1)S(1)}, u32[]{:S(2)}, u32[]{:S(2)}) %collective-permute-start.4) | collective-permute-done | bytes 163872 | tf_op jit(solution)/shard_map/ppermute | solution.py:498
  35.6 1.6 %shard_map.114 = bf16[8,80,256]{2,1,0:T(8,128)(2,1)} custom-call(bf16[640,1280]{1,0:T(8,128)(2,1)S(1)} %copy-done, bf16[16,5120]{1,0:T(8,128)(2,1)S(1)} %copy-done.8, bf16[16,5120]{1,0:T(8,128)(2,1)S(1)} %collective-permute-done.3.refs_1_, bf16[16,5120]{1,0:T(8,128)(2,1)S(1)} %collective-permute-done.4.refs_2_, ...), custom_call_target="tpu_custom_call" | custom-call | flops 1150000000 | tf_op jit(solution)/shard_map/pallas_call | solution.py:95
  37.4 0.7 copy-done.5
  38.1 1.8 %collective-permute-start.7 = (bf16[2,80,256]{2,1,0:T(8,128)(2,1)}, bf16[2,80,256]{2,1,0:T(8,128)(2,1)S(1)}, u32[]{:S(2)}, u32[]{:S(2)}) collective-permute-start(bf16[2,80,256]{2,1,0:T(8,128)(2,1)} %get-tuple-element.63), channel_id=1, source_target_pairs={{0,8},{4,12},{8,0},{12,4},{16,24},{20,28},{24,16},{28,20},{1,9},{5... | collective-permute-start | bytes 245768 | tf_op jit(solution)/shard_map/ppermute | solution.py:498
  39.9 1.5 %collective-permute-start.8 = (bf16[2,80,256]{2,1,0:T(8,128)(2,1)}, bf16[2,80,256]{2,1,0:T(8,128)(2,1)S(1)}, u32[]{:S(2)}, u32[]{:S(2)}) collective-permute-start(bf16[2,80,256]{2,1,0:T(8,128)(2,1)} %get-tuple-element.64), channel_id=1, source_target_pairs={{0,16},{4,20},{8,24},{12,28},{16,0},{20,4},{24,8},{28,12},{1,17},{... | collective-permute-start | bytes 245768 | tf_op jit(solution)/shard_map/ppermute | solution.py:498
  41.6 4.0 %all-to-all-start.1 = ((bf16[8,80,256]{2,1,0:T(8,128)(2,1)}), bf16[8,80,256]{2,1,0:T(8,128)(2,1)S(1)}, u32[]{:S(2)}, u32[]{:S(2)}) async-start(bf16[8,80,256]{2,1,0:T(8,128)(2,1)} %shard_map.114), calls=%async_computation.1 | async-start | bytes 655360 | tf_op jit(solution)/shard_map/all_to_all | solution.py:531
  47.6 0.7 collective-permute-done.13.refs_7_
  48.2 1.0 %copy-done.6 = bf16[64,2560]{1,0:T(8,128)(2,1)S(1)} copy-done((bf16[64,2560]{1,0:T(8,128)(2,1)S(1)}, bf16[64,2560]{1,0:T(8,128)(2,1)}, u32[]{:S(2)}) %copy-start.6) | copy-done | bytes 327704
  49.2 1.1 %shard_map.116 = (bf16[160,640]{1,0:T(8,128)(2,1)S(1)}, bf16[160,640]{1,0:T(8,128)(2,1)S(1)}, bf16[160,640]{1,0:T(8,128)(2,1)S(1)}, bf16[160,640]{1,0:T(8,128)(2,1)S(1)}) custom-call(bf16[64,2560]{1,0:T(8,128)(2,1)S(1)} %copy-done.6, bf16[64,2560]{1,0:T(8,128)(2,1)S(1)} %collective-permute-done.6.other_ref, bf16[2,80,256]{2,1,0:T(8,128)(2,1)S(1)} %copy-done.3, ...), custom_call_target="tpu_custom_call" | custom-call | flops 1380000000 | tf_op jit(solution)/shard_map/pallas_call | solution.py:435
  50.3 2.9 %all-to-all-done.1.grads_ref = bf16[8,80,256]{2,1,0:T(8,128)(2,1)S(1)} async-done(((bf16[8,80,256]{2,1,0:T(8,128)(2,1)}), bf16[8,80,256]{2,1,0:T(8,128)(2,1)S(1)}, u32[]{:S(2)}, u32[]{:S(2)}) %all-to-all-start.1) | async-done | bytes 327712 | tf_op jit(solution)/shard_map/all_to_all | solution.py:531
  53.8 0.6 collective-permute-start.15
  54.4 2.4 %collective-permute-start.16 = (bf16[160,640]{1,0:T(8,128)(2,1)S(1)}, bf16[160,640]{1,0:T(8,128)(2,1)S(1)}, u32[]{:S(2)}, u32[]{:S(2)}) collective-permute-start(bf16[160,640]{1,0:T(8,128)(2,1)S(1)} %get-tuple-element.79), channel_id=1, source_target_pairs={{0,24},{4,28},{8,16},{12,20},{16,8},{20,12},{24,0},{28,4},{1,25},{... | collective-permute-start | bytes 614408 | tf_op jit(solution)/shard_map/ppermute | solution.py:498
  56.7 10.9 %shard_map.117 = bf16[8,240,256]{2,1,0:T(8,128)(2,1)} custom-call(bf16[8,256,256]{2,1,0:T(8,128)(2,1)S(1)} %all-to-all-done.all_ref, bf16[8,80,256]{2,1,0:T(8,128)(2,1)S(1)} %all-to-all-done.1.grads_ref, bf16[8,80,256]{2,1,0:T(8,128)(2,1)S(1)} %copy-done.10, f32[8,1,256]{2,1,0:T(1,128)S(1)} %get-tuple-element.72.log_ref), custom_call_target="tpu_custom_call" | custom-call | flops 12650000384 | tf_op jit(solution)/shard_map/pallas_call | solution.py:311
  67.6 3.6 %all-to-all-start.2 = ((bf16[8,240,256]{2,1,0:T(8,128)(2,1)}), bf16[8,240,256]{2,1,0:T(8,128)(2,1)S(1)}, u32[]{:S(2)}, u32[]{:S(2)}) async-start(bf16[8,240,256]{2,1,0:T(8,128)(2,1)} %shard_map.117), calls=%async_computation.2 | async-start | bytes 1966080 | tf_op jit(solution)/shard_map/all_to_all | solution.py:537
  71.5 2.4 %collective-permute-start.17 = (bf16[160,160]{1,0:T(8,128)(2,1)S(1)}, bf16[160,160]{1,0:T(8,128)(2,1)S(1)}, u32[]{:S(2)}, u32[]{:S(2)}) collective-permute-start(bf16[160,160]{1,0:T(8,128)(2,1)S(1)} %get-tuple-element.85), channel_id=1, source_target_pairs={{0,1},{1,0},{2,3},{3,2},{4,5},{5,4},{6,7},{7,6},{8,9},{9,8},{10,11... | collective-permute-start | bytes 153608 | tf_op jit(solution)/shard_map/ppermute | solution.py:498
  74.0 2.4 %collective-permute-start.19 = (bf16[160,160]{1,0:T(8,128)(2,1)S(1)}, bf16[160,160]{1,0:T(8,128)(2,1)S(1)}, u32[]{:S(2)}, u32[]{:S(2)}) collective-permute-start(bf16[160,160]{1,0:T(8,128)(2,1)S(1)} %get-tuple-element.87), channel_id=1, source_target_pairs={{0,3},{1,2},{2,1},{3,0},{4,7},{5,6},{6,5},{7,4},{8,11},{9,10},{10,... | collective-permute-start | bytes 153608 | tf_op jit(solution)/shard_map/ppermute | solution.py:498
  76.9 6.3 %collective-permute-done.18.refs_2_ = bf16[160,160]{1,0:T(8,128)(2,1)S(1)} collective-permute-done((bf16[160,160]{1,0:T(8,128)(2,1)S(1)}, bf16[160,160]{1,0:T(8,128)(2,1)S(1)}, u32[]{:S(2)}, u32[]{:S(2)}) %collective-permute-start.18) | collective-permute-done | bytes 51232 | tf_op jit(solution)/shard_map/ppermute | solution.py:498
  83.2 0.7 shard_map.120
  83.9 1.9 %all-to-all-done.2.all_ref = bf16[8,240,256]{2,1,0:T(8,128)(2,1)S(1)} async-done(((bf16[8,240,256]{2,1,0:T(8,128)(2,1)}), bf16[8,240,256]{2,1,0:T(8,128)(2,1)S(1)}, u32[]{:S(2)}, u32[]{:S(2)}) %all-to-all-start.2) | async-done | bytes 983072 | tf_op jit(solution)/shard_map/all_to_all | solution.py:537
  85.8 1.1 %shard_map.118 = (bf16[256,640]{1,0:T(8,128)(2,1)}, bf16[256,640]{1,0:T(8,128)(2,1)}, bf16[256,640]{1,0:T(8,128)(2,1)}) custom-call(bf16[8,240,256]{2,1,0:T(8,128)(2,1)S(1)} %all-to-all-done.2.all_ref), custom_call_target="tpu_custom_call" | custom-call | flops 1264999936 | tf_op jit(solution)/shard_map/pallas_call | solution.py:351
  (46 shorter events, 4.1 us)
Async XLA Ops:
  4.4 5.3 %copy-start.4 = (s32[1,64]{1,0:T(1,128)S(1)}, s32[1,64]{1,0:T(1,128)}, u32[]{:S(2)}) copy-start(s32[1,64]{1,0:T(1,128)} %refs_0_.1) | copy-start | bytes 772
  4.4 14.9 %copy-start.1 = (bf16[64,5120]{1,0:T(8,128)(2,1)S(1)}, bf16[64,5120]{1,0:T(8,128)(2,1)}, u32[]{:S(2)}) copy-start(bf16[64,5120]{1,0:T(8,128)(2,1)} %grad_ref.1) | copy-start | bytes 1966084
  4.4 21.1 %all-to-all-start = ((bf16[8,256,256]{2,1,0:T(8,128)(2,1)}), bf16[8,256,256]{2,1,0:T(8,128)(2,1)S(1)}, u32[]{:S(2)}, u32[]{:S(2)}) async-start(bf16[8,256,256]{2,1,0:T(8,128)(2,1)} %shard_map.111), calls=%async_computation | async-start | bytes 2097152 | tf_op jit(solution)/shard_map/all_to_all | solution.py:520
  9.7 4.5 %collective-permute-start.1 = (s32[1,64]{1,0:T(1,128)S(1)}, s32[1,64]{1,0:T(1,128)S(1)}, u32[]{:S(2)}, u32[]{:S(2)}) collective-permute-start(s32[1,64]{1,0:T(1,128)S(1)} %copy-done.4), channel_id=1, source_target_pairs={{0,2},{1,3},{2,0},{3,1},{4,6},{5,7},{6,4},{7,5},{8,10},{9,11},{10,... | collective-permute-start | bytes 776 | tf_op jit(solution)/shard_map/ppermute | solution.py:498
  12.4 3.5 %collective-permute-start = (s32[1,64]{1,0:T(1,128)S(1)}, s32[1,64]{1,0:T(1,128)S(1)}, u32[]{:S(2)}, u32[]{:S(2)}) collective-permute-start(s32[1,64]{1,0:T(1,128)S(1)} %copy-done.4), channel_id=1, source_target_pairs={{0,1},{1,0},{2,3},{3,2},{4,5},{5,4},{6,7},{7,6},{8,9},{9,8},{10,11... | collective-permute-start | bytes 776 | tf_op jit(solution)/shard_map/ppermute | solution.py:498
  14.0 5.3 %collective-permute-start.2 = (s32[1,64]{1,0:T(1,128)S(1)}, s32[1,64]{1,0:T(1,128)S(1)}, u32[]{:S(2)}, u32[]{:S(2)}) collective-permute-start(s32[1,64]{1,0:T(1,128)S(1)} %copy-done.4), channel_id=1, source_target_pairs={{0,3},{1,2},{2,1},{3,0},{4,7},{5,6},{6,5},{7,4},{8,11},{9,10},{10,... | collective-permute-start | bytes 776 | tf_op jit(solution)/shard_map/ppermute | solution.py:498
  21.1 12.7 %collective-permute-start.3 = (bf16[16,5120]{1,0:T(8,128)(2,1)}, bf16[16,5120]{1,0:T(8,128)(2,1)S(1)}, u32[]{:S(2)}, u32[]{:S(2)}) collective-permute-start(bf16[16,5120]{1,0:T(8,128)(2,1)} %get-tuple-element.47), channel_id=1, source_target_pairs={{0,1},{1,0},{2,3},{3,2},{4,5},{5,4},{6,7},{7,6},{8,9},{9,8},{10,11... | collective-permute-start | bytes 491528 | tf_op jit(solution)/shard_map/ppermute | solution.py:498
  21.1 14.4 %collective-permute-start.4 = (bf16[16,5120]{1,0:T(8,128)(2,1)S(1)}, bf16[16,5120]{1,0:T(8,128)(2,1)S(1)}, u32[]{:S(2)}, u32[]{:S(2)}) collective-permute-start(bf16[16,5120]{1,0:T(8,128)(2,1)S(1)} %get-tuple-element.48), channel_id=1, source_target_pairs={{0,2},{1,3},{2,0},{3,1},{4,6},{5,7},{6,4},{7,5},{8,10},{9,11},{10,... | collective-permute-start | bytes 491528 | tf_op jit(solution)/shard_map/ppermute | solution.py:498
  21.9 13.6 %copy-start = (bf16[640,1280]{1,0:T(8,128)(2,1)S(1)}, bf16[640,1280]{1,0:T(8,128)(2,1)}, u32[]{:S(2)}) copy-start(bf16[640,1280]{1,0:T(8,128)(2,1)} %weight_ref.1) | copy-start | bytes 4915204
  21.9 13.6 %collective-permute-start.5 = (bf16[16,5120]{1,0:T(8,128)(2,1)S(1)}, bf16[16,5120]{1,0:T(8,128)(2,1)S(1)}, u32[]{:S(2)}, u32[]{:S(2)}) collective-permute-start(bf16[16,5120]{1,0:T(8,128)(2,1)S(1)} %get-tuple-element.49), channel_id=1, source_target_pairs={{0,3},{1,2},{2,1},{3,0},{4,7},{5,6},{6,5},{7,4},{8,11},{9,10},{10,... | collective-permute-start | bytes 491528 | tf_op jit(solution)/shard_map/ppermute | solution.py:498
  25.5 10.0 %copy-start.8 = (bf16[16,5120]{1,0:T(8,128)(2,1)S(1)}, bf16[16,5120]{1,0:T(8,128)(2,1)}, u32[]{:S(2)}) copy-start(bf16[16,5120]{1,0:T(8,128)(2,1)} %copy-done.7) | copy-start | bytes 491524
  33.8 3.4 %copy-start.9 = (bf16[8,80,256]{2,1,0:T(8,128)(2,1)}, bf16[8,80,256]{2,1,0:T(8,128)(2,1)S(1)}, u32[]{:S(2)}) copy-start(bf16[8,80,256]{2,1,0:T(8,128)(2,1)S(1)} %get-tuple-element.71.context_ref) | copy-start | bytes 983044
  37.1 8.5 %copy-start.3 = (bf16[2,80,256]{2,1,0:T(8,128)(2,1)S(1)}, bf16[2,80,256]{2,1,0:T(8,128)(2,1)}, u32[]{:S(2)}) copy-start(bf16[2,80,256]{2,1,0:T(8,128)(2,1)} %copy-done.2) | copy-start | bytes 245764
  37.4 0.7 copy-start.5
  38.1 10.1 %collective-permute-start.6 = (bf16[64,2560]{1,0:T(8,128)(2,1)S(1)}, bf16[64,2560]{1,0:T(8,128)(2,1)S(1)}, u32[]{:S(2)}, u32[]{:S(2)}) collective-permute-start(bf16[64,2560]{1,0:T(8,128)(2,1)S(1)} %get-tuple-element.61), channel_id=1, source_target_pairs={{0,4},{4,0},{8,12},{12,8},{16,20},{20,16},{24,28},{28,24},{1,5},{5... | collective-permute-start | bytes 983048 | tf_op jit(solution)/shard_map/ppermute | solution.py:498
  38.1 8.0 %collective-permute-start.7 = (bf16[2,80,256]{2,1,0:T(8,128)(2,1)}, bf16[2,80,256]{2,1,0:T(8,128)(2,1)S(1)}, u32[]{:S(2)}, u32[]{:S(2)}) collective-permute-start(bf16[2,80,256]{2,1,0:T(8,128)(2,1)} %get-tuple-element.63), channel_id=1, source_target_pairs={{0,8},{4,12},{8,0},{12,4},{16,24},{20,28},{24,16},{28,20},{1,9},{5... | collective-permute-start | bytes 245768 | tf_op jit(solution)/shard_map/ppermute | solution.py:498
  39.9 6.3 %collective-permute-start.8 = (bf16[2,80,256]{2,1,0:T(8,128)(2,1)}, bf16[2,80,256]{2,1,0:T(8,128)(2,1)S(1)}, u32[]{:S(2)}, u32[]{:S(2)}) collective-permute-start(bf16[2,80,256]{2,1,0:T(8,128)(2,1)} %get-tuple-element.64), channel_id=1, source_target_pairs={{0,16},{4,20},{8,24},{12,28},{16,0},{20,4},{24,8},{28,12},{1,17},{... | collective-permute-start | bytes 245768 | tf_op jit(solution)/shard_map/ppermute | solution.py:498
  41.4 5.6 %collective-permute-start.9 = (bf16[2,80,256]{2,1,0:T(8,128)(2,1)}, bf16[2,80,256]{2,1,0:T(8,128)(2,1)S(1)}, u32[]{:S(2)}, u32[]{:S(2)}) collective-permute-start(bf16[2,80,256]{2,1,0:T(8,128)(2,1)} %get-tuple-element.65), channel_id=1, source_target_pairs={{0,24},{4,28},{8,16},{12,20},{16,8},{20,12},{24,0},{28,4},{1,25},{... | collective-permute-start | bytes 245768 | tf_op jit(solution)/shard_map/ppermute | solution.py:498
  41.6 11.6 %all-to-all-start.1 = ((bf16[8,80,256]{2,1,0:T(8,128)(2,1)}), bf16[8,80,256]{2,1,0:T(8,128)(2,1)S(1)}, u32[]{:S(2)}, u32[]{:S(2)}) async-start(bf16[8,80,256]{2,1,0:T(8,128)(2,1)} %shard_map.114), calls=%async_computation.1 | async-start | bytes 655360 | tf_op jit(solution)/shard_map/all_to_all | solution.py:531
  45.6 1.4 %collective-permute-start.10 = (bf16[2,80,256]{2,1,0:T(8,128)(2,1)S(1)}, bf16[2,80,256]{2,1,0:T(8,128)(2,1)S(1)}, u32[]{:S(2)}, u32[]{:S(2)}) collective-permute-start(bf16[2,80,256]{2,1,0:T(8,128)(2,1)S(1)} %copy-done.3), channel_id=1, source_target_pairs={{0,4},{4,0},{8,12},{12,8},{16,20},{20,16},{24,28},{28,24},{1,5},{5... | collective-permute-start | bytes 245768 | tf_op jit(solution)/shard_map/ppermute | solution.py:498
  46.1 1.3 %collective-permute-start.11 = (bf16[2,80,256]{2,1,0:T(8,128)(2,1)S(1)}, bf16[2,80,256]{2,1,0:T(8,128)(2,1)S(1)}, u32[]{:S(2)}, u32[]{:S(2)}) collective-permute-start(bf16[2,80,256]{2,1,0:T(8,128)(2,1)S(1)} %collective-permute-done.7.refs_1_), channel_id=1, source_target_pairs={{0,4},{4,0},{8,12},{12,8},{16,20},{20,16},{24,28},{28,24},{1,5},{5... | collective-permute-start | bytes 245768 | tf_op jit(solution)/shard_map/ppermute | solution.py:498
  46.2 1.4 %collective-permute-start.12 = (bf16[2,80,256]{2,1,0:T(8,128)(2,1)S(1)}, bf16[2,80,256]{2,1,0:T(8,128)(2,1)S(1)}, u32[]{:S(2)}, u32[]{:S(2)}) collective-permute-start(bf16[2,80,256]{2,1,0:T(8,128)(2,1)S(1)} %collective-permute-done.8.refs_2_), channel_id=1, source_target_pairs={{0,4},{4,0},{8,12},{12,8},{16,20},{20,16},{24,28},{28,24},{1,5},{5... | collective-permute-start | bytes 245768 | tf_op jit(solution)/shard_map/ppermute | solution.py:498
  47.0 1.3 %collective-permute-start.13 = (bf16[2,80,256]{2,1,0:T(8,128)(2,1)S(1)}, bf16[2,80,256]{2,1,0:T(8,128)(2,1)S(1)}, u32[]{:S(2)}, u32[]{:S(2)}) collective-permute-start(bf16[2,80,256]{2,1,0:T(8,128)(2,1)S(1)} %collective-permute-done.9.refs_3_), channel_id=1, source_target_pairs={{0,4},{4,0},{8,12},{12,8},{16,20},{20,16},{24,28},{28,24},{1,5},{5... | collective-permute-start | bytes 245768 | tf_op jit(solution)/shard_map/ppermute | solution.py:498
  48.2 1.0 %copy-start.6 = (bf16[64,2560]{1,0:T(8,128)(2,1)S(1)}, bf16[64,2560]{1,0:T(8,128)(2,1)}, u32[]{:S(2)}) copy-start(bf16[64,2560]{1,0:T(8,128)(2,1)} %copy-done.5) | copy-start | bytes 983044
  49.2 7.5 %copy-start.10 = (bf16[8,80,256]{2,1,0:T(8,128)(2,1)S(1)}, bf16[8,80,256]{2,1,0:T(8,128)(2,1)}, u32[]{:S(2)}) copy-start(bf16[8,80,256]{2,1,0:T(8,128)(2,1)} %copy-done.9) | copy-start | bytes 983044
  53.2 17.9 %collective-permute-start.14 = (bf16[160,640]{1,0:T(8,128)(2,1)S(1)}, bf16[160,640]{1,0:T(8,128)(2,1)S(1)}, u32[]{:S(2)}, u32[]{:S(2)}) collective-permute-start(bf16[160,640]{1,0:T(8,128)(2,1)S(1)} %get-tuple-element.77), channel_id=1, source_target_pairs={{0,8},{4,12},{8,0},{12,4},{16,24},{20,28},{24,16},{28,20},{1,9},{5... | collective-permute-start | bytes 614408 | tf_op jit(solution)/shard_map/ppermute | solution.py:498
  53.8 17.4 %collective-permute-start.15 = (bf16[160,640]{1,0:T(8,128)(2,1)S(1)}, bf16[160,640]{1,0:T(8,128)(2,1)S(1)}, u32[]{:S(2)}, u32[]{:S(2)}) collective-permute-start(bf16[160,640]{1,0:T(8,128)(2,1)S(1)} %get-tuple-element.78), channel_id=1, source_target_pairs={{0,16},{4,20},{8,24},{12,28},{16,0},{20,4},{24,8},{28,12},{1,17},{... | collective-permute-start | bytes 614408 | tf_op jit(solution)/shard_map/ppermute | solution.py:498
  54.4 16.8 %collective-permute-start.16 = (bf16[160,640]{1,0:T(8,128)(2,1)S(1)}, bf16[160,640]{1,0:T(8,128)(2,1)S(1)}, u32[]{:S(2)}, u32[]{:S(2)}) collective-permute-start(bf16[160,640]{1,0:T(8,128)(2,1)S(1)} %get-tuple-element.79), channel_id=1, source_target_pairs={{0,24},{4,28},{8,16},{12,20},{16,8},{20,12},{24,0},{28,4},{1,25},{... | collective-permute-start | bytes 614408 | tf_op jit(solution)/shard_map/ppermute | solution.py:498
  67.6 18.2 %all-to-all-start.2 = ((bf16[8,240,256]{2,1,0:T(8,128)(2,1)}), bf16[8,240,256]{2,1,0:T(8,128)(2,1)S(1)}, u32[]{:S(2)}, u32[]{:S(2)}) async-start(bf16[8,240,256]{2,1,0:T(8,128)(2,1)} %shard_map.117), calls=%async_computation.2 | async-start | bytes 1966080 | tf_op jit(solution)/shard_map/all_to_all | solution.py:537
  71.5 5.4 %collective-permute-start.17 = (bf16[160,160]{1,0:T(8,128)(2,1)S(1)}, bf16[160,160]{1,0:T(8,128)(2,1)S(1)}, u32[]{:S(2)}, u32[]{:S(2)}) collective-permute-start(bf16[160,160]{1,0:T(8,128)(2,1)S(1)} %get-tuple-element.85), channel_id=1, source_target_pairs={{0,1},{1,0},{2,3},{3,2},{4,5},{5,4},{6,7},{7,6},{8,9},{9,8},{10,11... | collective-permute-start | bytes 153608 | tf_op jit(solution)/shard_map/ppermute | solution.py:498
  73.9 9.3 %collective-permute-start.18 = (bf16[160,160]{1,0:T(8,128)(2,1)S(1)}, bf16[160,160]{1,0:T(8,128)(2,1)S(1)}, u32[]{:S(2)}, u32[]{:S(2)}) collective-permute-start(bf16[160,160]{1,0:T(8,128)(2,1)S(1)} %get-tuple-element.86), channel_id=1, source_target_pairs={{0,2},{1,3},{2,0},{3,1},{4,6},{5,7},{6,4},{7,5},{8,10},{9,11},{10,... | collective-permute-start | bytes 153608 | tf_op jit(solution)/shard_map/ppermute | solution.py:498
  74.0 9.2 %collective-permute-start.19 = (bf16[160,160]{1,0:T(8,128)(2,1)S(1)}, bf16[160,160]{1,0:T(8,128)(2,1)S(1)}, u32[]{:S(2)}, u32[]{:S(2)}) collective-permute-start(bf16[160,160]{1,0:T(8,128)(2,1)S(1)} %get-tuple-element.87), channel_id=1, source_target_pairs={{0,3},{1,2},{2,1},{3,0},{4,7},{5,6},{6,5},{7,4},{8,11},{9,10},{10,... | collective-permute-start | bytes 153608 | tf_op jit(solution)/shard_map/ppermute | solution.py:498
  (2 other events, 1.3 us)

commit v3 on v2

--- a/solution.py
+++ b/solution.py
@@ -39,34 +39,33 @@
     return lax.dot_general(left, right, (((0,), (0,)), ((), ())), preferred_element_type=F32)
 
 
-def pack_kernel(start_ref, size_ref, query_ref, key_ref, value_ref, out_ref, *, groups):
+def pack_kernel(page_ref, query_ref, key_ref, value_ref, out_ref, *, groups):
     rows, width = query_ref.shape
     feat = width // groups
     for slot, ref in enumerate((query_ref, key_ref, value_ref)):
         turned = ref[...].T
         for g in range(groups):
             out_ref[g, slot * feat : (slot + 1) * feat, :] = turned[g * feat : (g + 1) * feat, :]
-    line = lax.broadcasted_iota(jnp.int32, (INFO, rows), 0)
-    page = jnp.where(line < INFO // 2, start_ref[...], size_ref[...])
-    info = page.astype(F32).astype(BF16)
     for g in range(groups):
-        out_ref[g, 3 * feat :, :] = info
+        out_ref[g, 3 * feat :, :] = page_ref[...]
 
 
 def pack(page_start, page_size, query, key, value, groups):
     rows, width = query.shape
+    line = lax.broadcasted_iota(jnp.int32, (INFO, rows), 0)
+    page = jnp.where(line < INFO // 2, page_start, page_size).astype(BF16)
     return pl.pallas_call(
         functools.partial(pack_kernel, groups=groups),
         out_shape=jax.ShapeDtypeStruct((groups, 3 * (width // groups) + INFO, rows), BF16),
-        in_specs=[VMEM] * 5,
+        in_specs=[VMEM] * 4,
         out_specs=VMEM,
         cost_estimate=cost(2.6),
         compiler_params=WHOLE,
-    )(page_start, page_size, query, key, value)
-
-
-def project_kernel(weight_ref, *refs, groups):
-    parts, out_ref = refs[:-1], refs[-1]
+    )(page, query, key, value)
+
+
+def project_kernel(weight_ref, *refs, groups, lanes, chips, cores):
+    parts, out_ref, keep_ref, send_refs = refs[:lanes], refs[lanes], refs[lanes + 1], refs[lanes + 2 :]
     width = weight_ref.shape[1]
     grads = jnp.concatenate([ref[...] for ref in parts], axis=0)
     merged = grads.shape[0]
@@ -79,6 +78,28 @@
     feat = turned.shape[0] // groups
     for g in range(groups):
         out_ref[g] = turned[g * feat : (g + 1) * feat, :]
+    core = lax.axis_index("blk") % cores
+    blocks = chips * cores
+    chunk = width // blocks
+    cuts = [
+        jnp.concatenate(
+            [
+                grads[:, (c * blocks + b) * chunk : (c * blocks + b + 1) * chunk]
+                for c in range(MERGE)
+                for b in range(own, blocks, cores)
+            ],
+            axis=1,
+        )
+        for own in range(cores)
+    ]
+    keep_ref[...] = jnp.where(core == 0, cuts[0], cuts[1])
+    send = jnp.where(core == 0, cuts[1], cuts[0])
+    share = merged // chips
+    for k, ref in enumerate(send_refs):
+        for i in range(send.shape[1] // total):
+            ref[i * share : (i + 1) * share, :] = send[
+                k * share : (k + 1) * share, i * total : (i + 1) * total
+            ]
 
 
 def row_order(total, lanes):
@@ -90,14 +111,23 @@
     return (source * portion + within % portion) * MERGE + line // merged
 
 
-def project(weight, parts, groups):
-    rows = sum(part.shape[0] for part in parts) * MERGE
-    return pl.pallas_call(
-        functools.partial(project_kernel, groups=groups),
-        out_shape=jax.ShapeDtypeStruct((groups, weight.shape[0] // groups, rows), BF16),
+def project(weight, parts, groups, chips, cores):
+    merged = sum(part.shape[0] for part in parts)
+    rows = merged * MERGE
+    wide = parts[0].shape[1] // cores
+    piece = jax.ShapeDtypeStruct(((merged // chips) * (wide // rows), rows), BF16)
+    return pl.pallas_call(
+        functools.partial(
+            project_kernel, groups=groups, lanes=len(parts), chips=chips, cores=cores
+        ),
+        out_shape=(
+            jax.ShapeDtypeStruct((groups, weight.shape[0] // groups, rows), BF16),
+            jax.ShapeDtypeStruct((merged, wide), BF16),
+            *([piece] * chips),
+        ),
         in_specs=[VMEM] * (1 + len(parts)),
-        out_specs=VMEM,
-        cost_estimate=cost(1.0),
+        out_specs=(VMEM,) * (2 + chips),
+        cost_estimate=cost(0.7),
         compiler_params=PARAMS,
     )(weight, *parts)
 
@@ -153,6 +183,15 @@
 
 def shared_block(index, shares):
     return index * shares + lax.axis_index("blk") % shares if shares > 1 else index
+
+
+def seen_blocks(block, blocks):
+    middle = blocks // 2
+    if block <= middle:
+        return list(range(blocks - 1))
+    if block == blocks - 1:
+        return list(range(middle + 1, blocks))
+    return list(range(blocks))
 
 
 def forward_kernel(all_ref, *refs, heads, shares):
@@ -267,7 +306,7 @@
                     hidden_row(all_ref, b, j, feat) - log_ref[index, h : h + 1, :]
                 )
 
-        def step(j, carried):
+        def step(j, carried, seen):
             key, value, turned_key = keys[j], values[j], all_ref[j, key_own, :]
             key_sum = jnp.zeros((HD, rows), F32)
             value_sum = jnp.zeros((HD, rows), F32)
@@ -281,14 +320,14 @@
                 d_scores = probs * (d_probs - delta[index])
                 return probs.astype(BF16), d_scores.astype(BF16)
 
-            ready = weights(0, *products(0))
-            formed = products(1) if count > 1 else None
-            for index in range(count):
+            ready = weights(seen[0], *products(seen[0]))
+            formed = products(seen[1]) if len(seen) > 1 else None
+            for place, index in enumerate(seen):
                 b = shared_block(index, shares)
                 probs, d_scores = ready
-                following = products(index + 2) if index + 2 < count else None
+                following = products(seen[place + 2]) if place + 2 < len(seen) else None
                 if formed is not None:
-                    ready = weights(index + 1, *formed)
+                    ready = weights(seen[place + 1], *formed)
                 formed = following
                 value_sum = value_sum + dot_nt(grads_ref[b, own, :], probs)
                 key_sum = key_sum + dot_nt(all_ref[b, own, :], d_scores)
@@ -297,7 +336,13 @@
             out_ref[j, value_own, :] = value_sum.astype(BF16)
             return carried
 
-        lax.fori_loop(0, blocks, step, 0)
+        if shares > 1:
+            lax.fori_loop(0, blocks, functools.partial(step, seen=list(range(count))), 0)
+        else:
+            for begin, end in ((0, blocks // 2 + 1), (blocks // 2 + 1, blocks - 1), (blocks - 1, blocks)):
+                if begin < end:
+                    seen = seen_blocks(begin, blocks)
+                    lax.fori_loop(begin, end, functools.partial(step, seen=seen), 0)
         if shares > 1:
             for b in range(blocks):
                 out_ref[b, own, :] = jnp.zeros((HD, rows), BF16)
@@ -359,65 +404,65 @@
     )(returned)
 
 
-def deal_kernel(*refs, cores, blocks):
-    parts, keep_ref, send_ref = refs[:-2], refs[-2], refs[-1]
-    core = lax.axis_index("blk") % cores
-    rows = jnp.concatenate([ref[...] for ref in parts], axis=0)
-    chunk = rows.shape[1] // MERGE // blocks
-    cuts = [
-        jnp.concatenate(
-            [
-                rows[:, (c * blocks + b) * chunk : (c * blocks + b + 1) * chunk]
-                for c in range(MERGE)
-                for b in range(own, blocks, cores)
-            ],
-            axis=1,
-        )
-        for own in range(cores)
-    ]
-    keep_ref[...] = jnp.where(core == 0, cuts[0], cuts[1])
-    send_ref[...] = jnp.where(core == 0, cuts[1], cuts[0])
-
-
-def deal(parts, blocks, cores):
-    rows = sum(part.shape[0] for part in parts)
-    half = jax.ShapeDtypeStruct((rows, parts[0].shape[1] // cores), BF16)
-    return pl.pallas_call(
-        functools.partial(deal_kernel, cores=cores, blocks=blocks),
-        out_shape=(half, half),
-        in_specs=[VMEM] * len(parts),
-        out_specs=(VMEM, VMEM),
-        cost_estimate=cost(0.5),
-        compiler_params=PARAMS,
-    )(*parts)
-
-
-def weight_kernel(keep_ref, other_ref, *refs, lanes, cores, shares):
-    chips = (len(refs) - 2) // (cores + 1)
-    context_refs, out_refs, (held, terms) = refs[:-2][: cores * chips], refs[cores * chips : -2], refs[-2:]
+def join_kernel(*refs):
+    count = len(refs) // 3
+    for near_ref, piece_ref, out_ref in zip(refs[:count], refs[count : 2 * count], refs[2 * count :]):
+        cores, feat, _ = near_ref.shape
+        for i in range(cores):
+            out_ref[i * feat : (i + 1) * feat, :] = near_ref[i]
+        out_ref[cores * feat :, :] = piece_ref[...]
+
+
+def join(near, pieces):
+    cores, feat, rows = near[0].shape
+    out = jax.ShapeDtypeStruct((cores * feat + pieces[0].shape[0], rows), BF16)
+    return pl.pallas_call(
+        join_kernel,
+        out_shape=(out,) * len(near),
+        in_specs=[VMEM] * (2 * len(near)),
+        out_specs=(VMEM,) * len(near),
+        cost_estimate=cost(3.0),
+        compiler_params=PARAMS,
+    )(*near, *pieces)
+
+
+def weight_kernel(keep_ref, *refs, lanes, cores, shares):
+    chips = (len(refs) - 2) // 3
+    near_refs, far_refs, out_refs = refs[:chips], refs[chips : 2 * chips], refs[2 * chips : -2]
+    held, terms = refs[-2:]
     block = lax.axis_index("blk")
     core, chip = block % cores, block // cores
-    feat, rows = context_refs[0].shape[1:]
+    feat, rows = near_refs[0].shape[1:]
     merged, wide = keep_ref.shape
     width = wide // MERGE
     if shares > 1:
         held[...] = jnp.zeros(held.shape, held.dtype)
-    for place, ref in enumerate(context_refs):
-        far, k = place // chips, place % chips
-        device = (chip ^ k) * cores + (core ^ far)
-        lines = pl.ds(pl.multiple_of((device // shares) * feat, feat), feat)
-        for i in range(cores):
-            if shares > 1:
-                held[i, lines, :] += ref[i].astype(F32)
-            else:
-                held[i, lines, :] = ref[i]
-    target = row_order(rows, lanes)
+    for k in range(chips):
+        for far in range(cores):
+            device = (chip ^ k) * cores + (core ^ far)
+            lines = pl.ds(pl.multiple_of((device // shares) * feat, feat), feat)
+            for i in range(cores):
+                part = far_refs[k][i * feat : (i + 1) * feat, :] if far else near_refs[k][i]
+                if shares > 1:
+                    held[i, lines, :] += part.astype(F32)
+                else:
+                    held[i, lines, :] = part
+    share, base = merged // chips, cores * feat
+    other = jnp.concatenate(
+        [
+            jnp.concatenate(
+                [ref[base + i * share : base + (i + 1) * share, :] for i in range(wide // rows)], axis=1
+            )
+            for ref in far_refs
+        ],
+        axis=0,
+    )
     column = lax.broadcasted_iota(jnp.int32, (rows, rows), 1)
-    order = (column == target).astype(BF16)
+    order = (column == row_order(rows, lanes)).astype(BF16)
     ordered, gathered = [], []
     for i in range(cores):
         ordered.append(dot_nt(order, held[i].astype(BF16)).astype(BF16))
-        grads = jnp.where(core == i, keep_ref[...], other_ref[...])
+        grads = jnp.where(core == i, keep_ref[...], other)
         gathered += [grads[:, c * width : (c + 1) * width] for c in range(MERGE)]
     total = dot_tn(jnp.concatenate(gathered, axis=0), jnp.concatenate(ordered, axis=0)).astype(BF16)
     chunk = width // chips
@@ -427,23 +472,23 @@
         ref[...] = terms[chip ^ k]
 
 
-def weight_terms(keep, other, contexts, width, lanes, cores, shares):
-    chips = len(contexts) // cores
-    rows = contexts[0].shape[2]
+def weight_terms(keep, near, far, width, lanes, cores, shares):
+    chips = len(near)
+    rows = near[0].shape[2]
     chunk = keep.shape[1] // MERGE // chips
     part = jax.ShapeDtypeStruct((chunk, width), BF16)
     return pl.pallas_call(
         functools.partial(weight_kernel, lanes=lanes, cores=cores, shares=shares),
         out_shape=(part,) * chips,
-        in_specs=[VMEM] * (2 + len(contexts)),
+        in_specs=[VMEM] * (1 + 2 * len(near)),
         out_specs=(VMEM,) * chips,
         scratch_shapes=[
             pltpu.VMEM((cores, width, rows), BF16 if shares == 1 else F32),
             pltpu.VMEM((chips, chunk, width), BF16),
         ],
-        cost_estimate=cost(1.2),
-        compiler_params=PARAMS,
-    )(keep, other, *contexts)
+        cost_estimate=cost(0.2),
+        compiler_params=PARAMS,
+    )(keep, *near, *far)
 
 
 def total_of(refs):
@@ -521,17 +566,15 @@
     picked = pick(llm_grad, asked)
     merged_parts = swap_all(picked, "dp", lanes)
     *near, context, log_total = forward(gathered, heads, shares)
+    merged_parts[1], near = after((merged_parts[1], near))
     near = swap_all(near, "blk", cycle, CORES)
     merged_parts, log_total = after((merged_parts, log_total))
-    grads = project(out_weight, merged_parts, groups)
-    merged_parts, grads = after((merged_parts, grads))
-    keep, send = deal(merged_parts, cycle, CORES)
+    grads, keep, *pieces = project(out_weight, merged_parts, groups, cycle // CORES, CORES)
     if shares > 1:
         grads = jnp.repeat(grads, shares, axis=0)
     grads = lax.all_to_all(grads, "blk", split_axis=0, concat_axis=0, tiled=True)
-    far = [swap(array, "blk", cycle, 1) for array in near]
-    other = swap(send, "blk", cycle, 1)
-    terms = weight_terms(keep, other, [*near, *far], width, lanes, CORES, shares)
+    far = [swap(array, "blk", cycle, 1) for array in join(near, pieces)]
+    terms = weight_terms(keep, near, far, width, lanes, CORES, shares)
     grads, terms = after((grads, terms))
     results = backward(gathered, grads, context, log_total, heads, shares)
     returned = lax.all_to_all(results, "blk", split_axis=0, concat_axis=0, tiled=True)

time: 87.3 us -> 83.4 us (0.955)
  Pallas kernels: 27.1 us -> 24.6 us
  local copies, waits for them, and re-layouts: 3.02 us -> 2.11 us
    ppermute x20 -> x19, waiting for transfers between devices: 15.3 us -> 13.2 us  [swap(): return lax.ppermute(array, axis, [(i, i ^ mask) for i in range(size)])]
    unnamed x22 -> x6, local copies, waits for them, and re-layouts: 3.02 us -> 1.44 us
    all_to_all x1, waiting for transfers between devices: 2.94 us -> 4.02 us  [body(): lax.all_to_all(grads, 'blk', split_axis=0, concat_axis=0, tiled=True)]
    pallas_call x1, Pallas kernels: 10.9 us -> 9.84 us  [backward(): pl.pallas_call(functools.partial(backward_kernel, heads=heads, shares=sha...]
    ppermute x20 -> x19, starting transfers between devices: 21.7 us -> 21.5 us  [swap(): return lax.ppermute(array, axis, [(i, i ^ mask) for i in range(size)])]
  transfers between devices with their start and end apart: 23 -> 22, of which waited for: 13 -> 12; matrix products, arithmetic and copies ran while one was open for 0% -> 0% of each run, Pallas kernels for 25% -> 25%
where the time goes in v3:
time: 83.4 us; the launch traced here: 83 us
  starting transfers between devices  33.8 us (41%)
  Pallas kernels  24.6 us (29%)
  waiting for transfers between devices  20.4 us (24%)
  local copies, waits for them, and re-layouts  2.11 us (3%)
  between operations  2.08 us (2%)
    ppermute x19, starting transfers between devices, swap(): return lax.ppermute(array, axis, [(i, i ^ mask) for i in range(size)])  21.5 us
    ppermute x19, waiting for transfers between devices, swap(): return lax.ppermute(array, axis, [(i, i ^ mask) for i in range(size)])  13.2 us
    pallas_call x1, Pallas kernels, backward(): pl.pallas_call(functools.partial(backward_kernel, heads=heads, shares=sha...  9.84 us
    pallas_call x1, Pallas kernels, forward(): pl.pallas_call(functools.partial(forward_kernel, heads=heads, shares=shar...  6.94 us
    all_to_all x1, starting transfers between devices, body(): lax.all_to_all(packed, 'blk', split_axis=0, concat_axis=0, tiled=True)  5.3 us
    all_to_all x1, waiting for transfers between devices, body(): lax.all_to_all(grads, 'blk', split_axis=0, concat_axis=0, tiled=True)  4.02 us
    all_to_all x1, starting transfers between devices, body(): lax.all_to_all(results, 'blk', split_axis=0, concat_axis=0, tiled=True)  3.55 us
    all_to_all x1, starting transfers between devices, body(): lax.all_to_all(grads, 'blk', split_axis=0, concat_axis=0, tiled=True)  3.43 us
  transfers between devices with their start and end apart: 22, of which 12 were waited for; matrix products, arithmetic and copies ran while one was open for 0% of the time, Pallas kernels for 25%

profile of v3, /device:TPU:0, one launch (start us, length us, event | category | flops | bytes accessed | tf_op | source)
XLA Modules:
  0.0 83.0 jit_solution(18075087698674367013)
XLA Ops:
  1.9 0.7 iota.7.page_ref
  2.6 2.5 %shard_map.111 = bf16[8,256,256]{2,1,0:T(8,128)(2,1)} custom-call(bf16[16,256]{1,0:T(8,128)(2,1)} %iota.7.page_ref, bf16[256,640]{1,0:T(8,128)(2,1)} %bitcast.10, bf16[256,640]{1,0:T(8,128)(2,1)} %bitcast.11, bf16[256,640]{1,0:T(8,128)(2,1)} %bitcast.12), custom_call_target="tpu_custom_call" | custom-call | flops 2990000128 | tf_op jit(solution)/shard_map/pallas_call | solution.py:57
  5.1 5.3 %all-to-all-start = ((bf16[8,256,256]{2,1,0:T(8,128)(2,1)}), bf16[8,256,256]{2,1,0:T(8,128)(2,1)S(1)}, u32[]{:S(2)}, u32[]{:S(2)}) async-start(bf16[8,256,256]{2,1,0:T(8,128)(2,1)} %shard_map.111), calls=%async_computation | async-start | bytes 2097152 | tf_op jit(solution)/shard_map/all_to_all | solution.py:565
  10.4 2.7 %collective-permute-start.1 = (s32[1,64]{1,0:T(1,128)S(1)}, s32[1,64]{1,0:T(1,128)S(1)}, u32[]{:S(2)}, u32[]{:S(2)}) collective-permute-start(s32[1,64]{1,0:T(1,128)S(1)} %copy-done.2), channel_id=1, source_target_pairs={{0,2},{1,3},{2,0},{3,1},{4,6},{5,7},{6,4},{7,5},{8,10},{9,11},{10,... | collective-permute-start | bytes 776 | tf_op jit(solution)/shard_map/ppermute | solution.py:543
  13.1 1.6 %collective-permute-start = (s32[1,64]{1,0:T(1,128)S(1)}, s32[1,64]{1,0:T(1,128)S(1)}, u32[]{:S(2)}, u32[]{:S(2)}) collective-permute-start(s32[1,64]{1,0:T(1,128)S(1)} %copy-done.2), channel_id=1, source_target_pairs={{0,1},{1,0},{2,3},{3,2},{4,5},{5,4},{6,7},{7,6},{8,9},{9,8},{10,11... | collective-permute-start | bytes 776 | tf_op jit(solution)/shard_map/ppermute | solution.py:543
  14.9 1.7 %collective-permute-done.refs_1_ = s32[1,64]{1,0:T(1,128)S(1)} collective-permute-done((s32[1,64]{1,0:T(1,128)S(1)}, s32[1,64]{1,0:T(1,128)S(1)}, u32[]{:S(2)}, u32[]{:S(2)}) %collective-permute-start) | collective-permute-done | bytes 288 | tf_op jit(solution)/shard_map/ppermute | solution.py:543
  16.6 3.4 %collective-permute-done.2.refs_3_ = s32[1,64]{1,0:T(1,128)S(1)} collective-permute-done((s32[1,64]{1,0:T(1,128)S(1)}, s32[1,64]{1,0:T(1,128)S(1)}, u32[]{:S(2)}, u32[]{:S(2)}) %collective-permute-start.2) | collective-permute-done | bytes 288 | tf_op jit(solution)/shard_map/ppermute | solution.py:543
  20.0 0.5 shard_map.112
  20.6 0.8 collective-permute-start.4
  21.4 3.6 %collective-permute-start.5 = (bf16[16,5120]{1,0:T(8,128)(2,1)S(1)}, bf16[16,5120]{1,0:T(8,128)(2,1)S(1)}, u32[]{:S(2)}, u32[]{:S(2)}) collective-permute-start(bf16[16,5120]{1,0:T(8,128)(2,1)S(1)} %get-tuple-element.62), channel_id=1, source_target_pairs={{0,3},{1,2},{2,1},{3,0},{4,7},{5,6},{6,5},{7,4},{8,11},{9,10},{10,... | collective-permute-start | bytes 491528 | tf_op jit(solution)/shard_map/ppermute | solution.py:543
  25.0 0.9 %all-to-all-done.all_ref = bf16[8,256,256]{2,1,0:T(8,128)(2,1)S(1)} async-done(((bf16[8,256,256]{2,1,0:T(8,128)(2,1)}), bf16[8,256,256]{2,1,0:T(8,128)(2,1)S(1)}, u32[]{:S(2)}, u32[]{:S(2)}) %all-to-all-start) | async-done | bytes 1048608 | tf_op jit(solution)/shard_map/all_to_all | solution.py:565
  25.8 6.9 %shard_map.113 = (bf16[2,80,256]{2,1,0:T(8,128)(2,1)S(1)}, bf16[2,80,256]{2,1,0:T(8,128)(2,1)S(1)}, bf16[2,80,256]{2,1,0:T(8,128)(2,1)S(1)}, bf16[2,80,256]{2,1,...) custom-call(bf16[8,256,256]{2,1,0:T(8,128)(2,1)S(1)} %all-to-all-done.all_ref), custom_call_target="tpu_custom_call" | custom-call | flops 8049999872 | tf_op jit(solution)/shard_map/pallas_call | solution.py:266
  32.8 1.2 %collective-permute-start.6 = (bf16[2,80,256]{2,1,0:T(8,128)(2,1)S(1)}, bf16[2,80,256]{2,1,0:T(8,128)(2,1)S(1)}, u32[]{:S(2)}, u32[]{:S(2)}) collective-permute-start(bf16[2,80,256]{2,1,0:T(8,128)(2,1)S(1)} %get-tuple-element.71), channel_id=1, source_target_pairs={{0,8},{4,12},{8,0},{12,4},{16,24},{20,28},{24,16},{28,20},{1,9},{5... | collective-permute-start | bytes 245768 | tf_op jit(solution)/shard_map/ppermute | solution.py:543
  33.9 1.5 %collective-permute-start.7 = (bf16[2,80,256]{2,1,0:T(8,128)(2,1)S(1)}, bf16[2,80,256]{2,1,0:T(8,128)(2,1)S(1)}, u32[]{:S(2)}, u32[]{:S(2)}) collective-permute-start(bf16[2,80,256]{2,1,0:T(8,128)(2,1)S(1)} %get-tuple-element.72), channel_id=1, source_target_pairs={{0,16},{4,20},{8,24},{12,28},{16,0},{20,4},{24,8},{28,12},{1,17},{... | collective-permute-start | bytes 245768 | tf_op jit(solution)/shard_map/ppermute | solution.py:543
  35.4 0.9 %collective-permute-start.8 = (bf16[2,80,256]{2,1,0:T(8,128)(2,1)S(1)}, bf16[2,80,256]{2,1,0:T(8,128)(2,1)S(1)}, u32[]{:S(2)}, u32[]{:S(2)}) collective-permute-start(bf16[2,80,256]{2,1,0:T(8,128)(2,1)S(1)} %get-tuple-element.73), channel_id=1, source_target_pairs={{0,24},{4,28},{8,16},{12,20},{16,8},{20,12},{24,0},{28,4},{1,25},{... | collective-permute-start | bytes 245768 | tf_op jit(solution)/shard_map/ppermute | solution.py:543
  36.3 1.4 %copy-done = bf16[640,1280]{1,0:T(8,128)(2,1)S(1)} copy-done((bf16[640,1280]{1,0:T(8,128)(2,1)S(1)}, bf16[640,1280]{1,0:T(8,128)(2,1)}, u32[]{:S(2)}) %copy-start) | copy-done | bytes 1638424
  37.8 1.6 %shard_map.114 = (bf16[8,80,256]{2,1,0:T(8,128)(2,1)}, bf16[64,2560]{1,0:T(8,128)(2,1)S(1)}, bf16[160,256]{1,0:T(8,128)(2,1)S(1)}, bf16[160,256]{1,0:T(8,128)(2,...) custom-call(bf16[640,1280]{1,0:T(8,128)(2,1)S(1)} %copy-done, ...), custom_call_target="tpu_custom_call" | custom-call | flops 805000000 | tf_op jit(solution)/shard_map/pallas_call | solution.py:119
  39.3 3.4 %all-to-all-start.1 = ((bf16[8,80,256]{2,1,0:T(8,128)(2,1)}), bf16[8,80,256]{2,1,0:T(8,128)(2,1)S(1)}, u32[]{:S(2)}, u32[]{:S(2)}) async-start(bf16[8,80,256]{2,1,0:T(8,128)(2,1)} %get-tuple-element.68), calls=%async_computation.1 | async-start | bytes 655360 | tf_op jit(solution)/shard_map/all_to_all | solution.py:575
  42.9 0.5 collective-permute-start.9
  45.2 1.1 %shard_map.116 = (bf16[160,640]{1,0:T(8,128)(2,1)S(1)}, bf16[160,640]{1,0:T(8,128)(2,1)S(1)}, bf16[160,640]{1,0:T(8,128)(2,1)S(1)}, bf16[160,640]{1,0:T(8,128)(2,1)S(1)}) custom-call(bf16[64,2560]{1,0:T(8,128)(2,1)S(1)} %get-tuple-element.69.keep_ref, bf16[2,80,256]{2,1,0:T(8,128)(2,1)S(1)} %get-tuple-element.70.refs_0_, ...), custom_call_target="tpu_custom_call" | custom-call | flops 230000000 | tf_op jit(solution)/shard_map/pallas_call | solution.py:480
  46.3 4.0 %all-to-all-done.1.grads_ref = bf16[8,80,256]{2,1,0:T(8,128)(2,1)S(1)} async-done(((bf16[8,80,256]{2,1,0:T(8,128)(2,1)}), bf16[8,80,256]{2,1,0:T(8,128)(2,1)S(1)}, u32[]{:S(2)}, u32[]{:S(2)}) %all-to-all-start.1) | async-done | bytes 327712 | tf_op jit(solution)/shard_map/all_to_all | solution.py:575
  50.3 0.6 collective-permute-start.13
  50.9 0.6 collective-permute-start.14
  51.5 2.4 %collective-permute-start.15 = (bf16[160,640]{1,0:T(8,128)(2,1)S(1)}, bf16[160,640]{1,0:T(8,128)(2,1)S(1)}, u32[]{:S(2)}, u32[]{:S(2)}) collective-permute-start(bf16[160,640]{1,0:T(8,128)(2,1)S(1)} %get-tuple-element.95), channel_id=1, source_target_pairs={{0,24},{4,28},{8,16},{12,20},{16,8},{20,12},{24,0},{28,4},{1,25},{... | collective-permute-start | bytes 614408 | tf_op jit(solution)/shard_map/ppermute | solution.py:543
  53.8 9.8 %shard_map.117 = bf16[8,240,256]{2,1,0:T(8,128)(2,1)} custom-call(bf16[8,256,256]{2,1,0:T(8,128)(2,1)S(1)} %all-to-all-done.all_ref, bf16[8,80,256]{2,1,0:T(8,128)(2,1)S(1)} %all-to-all-done.1.grads_ref, bf16[8,80,256]{2,1,0:T(8,128)(2,1)S(1)} %get-tuple-element.87.context_ref, f32[8,1,256]{2,1,0:T(1,128)S(1)} %get-tuple-element.88.log_ref), custom_call_target="tpu_custom_call" | custom-call | flops 12650000384 | tf_op jit(solution)/shard_map/pallas_call | solution.py:356
  63.7 3.6 %all-to-all-start.2 = ((bf16[8,240,256]{2,1,0:T(8,128)(2,1)}), bf16[8,240,256]{2,1,0:T(8,128)(2,1)S(1)}, u32[]{:S(2)}, u32[]{:S(2)}) async-start(bf16[8,240,256]{2,1,0:T(8,128)(2,1)} %shard_map.117), calls=%async_computation.2 | async-start | bytes 1966080 | tf_op jit(solution)/shard_map/all_to_all | solution.py:580
  67.6 1.8 %collective-permute-start.16 = (bf16[160,160]{1,0:T(8,128)(2,1)S(1)}, bf16[160,160]{1,0:T(8,128)(2,1)S(1)}, u32[]{:S(2)}, u32[]{:S(2)}) collective-permute-start(bf16[160,160]{1,0:T(8,128)(2,1)S(1)} %get-tuple-element.101), channel_id=1, source_target_pairs={{0,1},{1,0},{2,3},{3,2},{4,5},{5,4},{6,7},{7,6},{8,9},{9,8},{10,11... | collective-permute-start | bytes 153608 | tf_op jit(solution)/shard_map/ppermute | solution.py:543
  69.3 2.5 %collective-permute-start.17 = (bf16[160,160]{1,0:T(8,128)(2,1)S(1)}, bf16[160,160]{1,0:T(8,128)(2,1)S(1)}, u32[]{:S(2)}, u32[]{:S(2)}) collective-permute-start(bf16[160,160]{1,0:T(8,128)(2,1)S(1)} %get-tuple-element.102), channel_id=1, source_target_pairs={{0,2},{1,3},{2,0},{3,1},{4,6},{5,7},{6,4},{7,5},{8,10},{9,11},{10,... | collective-permute-start | bytes 153608 | tf_op jit(solution)/shard_map/ppermute | solution.py:543
  72.4 6.5 %collective-permute-done.17.refs_2_ = bf16[160,160]{1,0:T(8,128)(2,1)S(1)} collective-permute-done((bf16[160,160]{1,0:T(8,128)(2,1)S(1)}, bf16[160,160]{1,0:T(8,128)(2,1)S(1)}, u32[]{:S(2)}, u32[]{:S(2)}) %collective-permute-start.17) | collective-permute-done | bytes 51232 | tf_op jit(solution)/shard_map/ppermute | solution.py:543
  78.8 0.7 shard_map.120
  79.6 2.3 %all-to-all-done.2.all_ref = bf16[8,240,256]{2,1,0:T(8,128)(2,1)S(1)} async-done(((bf16[8,240,256]{2,1,0:T(8,128)(2,1)}), bf16[8,240,256]{2,1,0:T(8,128)(2,1)S(1)}, u32[]{:S(2)}, u32[]{:S(2)}) %all-to-all-start.2) | async-done | bytes 983072 | tf_op jit(solution)/shard_map/all_to_all | solution.py:580
  81.9 1.1 %shard_map.118 = (bf16[256,640]{1,0:T(8,128)(2,1)}, bf16[256,640]{1,0:T(8,128)(2,1)}, bf16[256,640]{1,0:T(8,128)(2,1)}) custom-call(bf16[8,240,256]{2,1,0:T(8,128)(2,1)S(1)} %all-to-all-done.2.all_ref), custom_call_target="tpu_custom_call" | custom-call | flops 1264999936 | tf_op jit(solution)/shard_map/pallas_call | solution.py:396
  (30 shorter events, 3.1 us)
Async XLA Ops:
  5.1 5.3 %copy-start.2 = (s32[1,64]{1,0:T(1,128)S(1)}, s32[1,64]{1,0:T(1,128)}, u32[]{:S(2)}) copy-start(s32[1,64]{1,0:T(1,128)} %refs_0_.1) | copy-start | bytes 772
  5.1 14.9 %copy-start.1 = (bf16[64,5120]{1,0:T(8,128)(2,1)S(1)}, bf16[64,5120]{1,0:T(8,128)(2,1)}, u32[]{:S(2)}) copy-start(bf16[64,5120]{1,0:T(8,128)(2,1)} %grad_ref.1) | copy-start | bytes 1966084
  5.1 20.7 %all-to-all-start = ((bf16[8,256,256]{2,1,0:T(8,128)(2,1)}), bf16[8,256,256]{2,1,0:T(8,128)(2,1)S(1)}, u32[]{:S(2)}, u32[]{:S(2)}) async-start(bf16[8,256,256]{2,1,0:T(8,128)(2,1)} %shard_map.111), calls=%async_computation | async-start | bytes 2097152 | tf_op jit(solution)/shard_map/all_to_all | solution.py:565
  10.4 4.5 %collective-permute-start.1 = (s32[1,64]{1,0:T(1,128)S(1)}, s32[1,64]{1,0:T(1,128)S(1)}, u32[]{:S(2)}, u32[]{:S(2)}) collective-permute-start(s32[1,64]{1,0:T(1,128)S(1)} %copy-done.2), channel_id=1, source_target_pairs={{0,2},{1,3},{2,0},{3,1},{4,6},{5,7},{6,4},{7,5},{8,10},{9,11},{10,... | collective-permute-start | bytes 776 | tf_op jit(solution)/shard_map/ppermute | solution.py:543
  13.1 3.5 %collective-permute-start = (s32[1,64]{1,0:T(1,128)S(1)}, s32[1,64]{1,0:T(1,128)S(1)}, u32[]{:S(2)}, u32[]{:S(2)}) collective-permute-start(s32[1,64]{1,0:T(1,128)S(1)} %copy-done.2), channel_id=1, source_target_pairs={{0,1},{1,0},{2,3},{3,2},{4,5},{5,4},{6,7},{7,6},{8,9},{9,8},{10,11... | collective-permute-start | bytes 776 | tf_op jit(solution)/shard_map/ppermute | solution.py:543
  14.6 5.3 %collective-permute-start.2 = (s32[1,64]{1,0:T(1,128)S(1)}, s32[1,64]{1,0:T(1,128)S(1)}, u32[]{:S(2)}, u32[]{:S(2)}) collective-permute-start(s32[1,64]{1,0:T(1,128)S(1)} %copy-done.2), channel_id=1, source_target_pairs={{0,3},{1,2},{2,1},{3,0},{4,7},{5,6},{6,5},{7,4},{8,11},{9,10},{10,... | collective-permute-start | bytes 776 | tf_op jit(solution)/shard_map/ppermute | solution.py:543
  20.5 12.3 %collective-permute-start.3 = (bf16[16,5120]{1,0:T(8,128)(2,1)S(1)}, bf16[16,5120]{1,0:T(8,128)(2,1)S(1)}, u32[]{:S(2)}, u32[]{:S(2)}) collective-permute-start(bf16[16,5120]{1,0:T(8,128)(2,1)S(1)} %get-tuple-element.55), channel_id=1, source_target_pairs={{0,1},{1,0},{2,3},{3,2},{4,5},{5,4},{6,7},{7,6},{8,9},{9,8},{10,11... | collective-permute-start | bytes 491528 | tf_op jit(solution)/shard_map/ppermute | solution.py:543
  20.6 15.7 %collective-permute-start.4 = (bf16[16,5120]{1,0:T(8,128)(2,1)S(1)}, bf16[16,5120]{1,0:T(8,128)(2,1)S(1)}, u32[]{:S(2)}, u32[]{:S(2)}) collective-permute-start(bf16[16,5120]{1,0:T(8,128)(2,1)S(1)} %get-tuple-element.61), channel_id=1, source_target_pairs={{0,2},{1,3},{2,0},{3,1},{4,6},{5,7},{6,4},{7,5},{8,10},{9,11},{10,... | collective-permute-start | bytes 491528 | tf_op jit(solution)/shard_map/ppermute | solution.py:543
  21.4 15.0 %collective-permute-start.5 = (bf16[16,5120]{1,0:T(8,128)(2,1)S(1)}, bf16[16,5120]{1,0:T(8,128)(2,1)S(1)}, u32[]{:S(2)}, u32[]{:S(2)}) collective-permute-start(bf16[16,5120]{1,0:T(8,128)(2,1)S(1)} %get-tuple-element.62), channel_id=1, source_target_pairs={{0,3},{1,2},{2,1},{3,0},{4,7},{5,6},{6,5},{7,4},{8,11},{9,10},{10,... | collective-permute-start | bytes 491528 | tf_op jit(solution)/shard_map/ppermute | solution.py:543
  32.8 10.0 %collective-permute-start.6 = (bf16[2,80,256]{2,1,0:T(8,128)(2,1)S(1)}, bf16[2,80,256]{2,1,0:T(8,128)(2,1)S(1)}, u32[]{:S(2)}, u32[]{:S(2)}) collective-permute-start(bf16[2,80,256]{2,1,0:T(8,128)(2,1)S(1)} %get-tuple-element.71), channel_id=1, source_target_pairs={{0,8},{4,12},{8,0},{12,4},{16,24},{20,28},{24,16},{28,20},{1,9},{5... | collective-permute-start | bytes 245768 | tf_op jit(solution)/shard_map/ppermute | solution.py:543
  33.9 8.9 %collective-permute-start.7 = (bf16[2,80,256]{2,1,0:T(8,128)(2,1)S(1)}, bf16[2,80,256]{2,1,0:T(8,128)(2,1)S(1)}, u32[]{:S(2)}, u32[]{:S(2)}) collective-permute-start(bf16[2,80,256]{2,1,0:T(8,128)(2,1)S(1)} %get-tuple-element.72), channel_id=1, source_target_pairs={{0,16},{4,20},{8,24},{12,28},{16,0},{20,4},{24,8},{28,12},{1,17},{... | collective-permute-start | bytes 245768 | tf_op jit(solution)/shard_map/ppermute | solution.py:543
  35.4 7.4 %collective-permute-start.8 = (bf16[2,80,256]{2,1,0:T(8,128)(2,1)S(1)}, bf16[2,80,256]{2,1,0:T(8,128)(2,1)S(1)}, u32[]{:S(2)}, u32[]{:S(2)}) collective-permute-start(bf16[2,80,256]{2,1,0:T(8,128)(2,1)S(1)} %get-tuple-element.73), channel_id=1, source_target_pairs={{0,24},{4,28},{8,16},{12,20},{16,8},{20,12},{24,0},{28,4},{1,25},{... | collective-permute-start | bytes 245768 | tf_op jit(solution)/shard_map/ppermute | solution.py:543
  36.3 1.4 %copy-start = (bf16[640,1280]{1,0:T(8,128)(2,1)S(1)}, bf16[640,1280]{1,0:T(8,128)(2,1)}, u32[]{:S(2)}) copy-start(bf16[640,1280]{1,0:T(8,128)(2,1)} %weight_ref.1) | copy-start | bytes 4915204
  39.3 11.0 %all-to-all-start.1 = ((bf16[8,80,256]{2,1,0:T(8,128)(2,1)}), bf16[8,80,256]{2,1,0:T(8,128)(2,1)S(1)}, u32[]{:S(2)}, u32[]{:S(2)}) async-start(bf16[8,80,256]{2,1,0:T(8,128)(2,1)} %get-tuple-element.68), calls=%async_computation.1 | async-start | bytes 655360 | tf_op jit(solution)/shard_map/all_to_all | solution.py:575
  42.9 1.5 %collective-permute-start.9 = (bf16[320,256]{1,0:T(8,128)(2,1)S(1)}, bf16[320,256]{1,0:T(8,128)(2,1)S(1)}, u32[]{:S(2)}, u32[]{:S(2)}) collective-permute-start(bf16[320,256]{1,0:T(8,128)(2,1)S(1)} %get-tuple-element.78), channel_id=1, source_target_pairs={{0,4},{4,0},{8,12},{12,8},{16,20},{20,16},{24,28},{28,24},{1,5},{5... | collective-permute-start | bytes 491528 | tf_op jit(solution)/shard_map/ppermute | solution.py:543
  43.3 1.4 %collective-permute-start.10 = (bf16[320,256]{1,0:T(8,128)(2,1)S(1)}, bf16[320,256]{1,0:T(8,128)(2,1)S(1)}, u32[]{:S(2)}, u32[]{:S(2)}) collective-permute-start(bf16[320,256]{1,0:T(8,128)(2,1)S(1)} %get-tuple-element.79), channel_id=1, source_target_pairs={{0,4},{4,0},{8,12},{12,8},{16,20},{20,16},{24,28},{28,24},{1,5},{5... | collective-permute-start | bytes 491528 | tf_op jit(solution)/shard_map/ppermute | solution.py:543
  43.4 1.5 %collective-permute-start.11 = (bf16[320,256]{1,0:T(8,128)(2,1)S(1)}, bf16[320,256]{1,0:T(8,128)(2,1)S(1)}, u32[]{:S(2)}, u32[]{:S(2)}) collective-permute-start(bf16[320,256]{1,0:T(8,128)(2,1)S(1)} %get-tuple-element.80), channel_id=1, source_target_pairs={{0,4},{4,0},{8,12},{12,8},{16,20},{20,16},{24,28},{28,24},{1,5},{5... | collective-permute-start | bytes 491528 | tf_op jit(solution)/shard_map/ppermute | solution.py:543
  43.8 1.4 %collective-permute-start.12 = (bf16[320,256]{1,0:T(8,128)(2,1)S(1)}, bf16[320,256]{1,0:T(8,128)(2,1)S(1)}, u32[]{:S(2)}, u32[]{:S(2)}) collective-permute-start(bf16[320,256]{1,0:T(8,128)(2,1)S(1)} %get-tuple-element.81), channel_id=1, source_target_pairs={{0,4},{4,0},{8,12},{12,8},{16,20},{20,16},{24,28},{28,24},{1,5},{5... | collective-permute-start | bytes 491528 | tf_op jit(solution)/shard_map/ppermute | solution.py:543
  50.3 16.9 %collective-permute-start.13 = (bf16[160,640]{1,0:T(8,128)(2,1)S(1)}, bf16[160,640]{1,0:T(8,128)(2,1)S(1)}, u32[]{:S(2)}, u32[]{:S(2)}) collective-permute-start(bf16[160,640]{1,0:T(8,128)(2,1)S(1)} %get-tuple-element.93), channel_id=1, source_target_pairs={{0,8},{4,12},{8,0},{12,4},{16,24},{20,28},{24,16},{28,20},{1,9},{5... | collective-permute-start | bytes 614408 | tf_op jit(solution)/shard_map/ppermute | solution.py:543
  50.9 16.4 %collective-permute-start.14 = (bf16[160,640]{1,0:T(8,128)(2,1)S(1)}, bf16[160,640]{1,0:T(8,128)(2,1)S(1)}, u32[]{:S(2)}, u32[]{:S(2)}) collective-permute-start(bf16[160,640]{1,0:T(8,128)(2,1)S(1)} %get-tuple-element.94), channel_id=1, source_target_pairs={{0,16},{4,20},{8,24},{12,28},{16,0},{20,4},{24,8},{28,12},{1,17},{... | collective-permute-start | bytes 614408 | tf_op jit(solution)/shard_map/ppermute | solution.py:543
  51.5 15.8 %collective-permute-start.15 = (bf16[160,640]{1,0:T(8,128)(2,1)S(1)}, bf16[160,640]{1,0:T(8,128)(2,1)S(1)}, u32[]{:S(2)}, u32[]{:S(2)}) collective-permute-start(bf16[160,640]{1,0:T(8,128)(2,1)S(1)} %get-tuple-element.95), channel_id=1, source_target_pairs={{0,24},{4,28},{8,16},{12,20},{16,8},{20,12},{24,0},{28,4},{1,25},{... | collective-permute-start | bytes 614408 | tf_op jit(solution)/shard_map/ppermute | solution.py:543
  63.7 18.2 %all-to-all-start.2 = ((bf16[8,240,256]{2,1,0:T(8,128)(2,1)}), bf16[8,240,256]{2,1,0:T(8,128)(2,1)S(1)}, u32[]{:S(2)}, u32[]{:S(2)}) async-start(bf16[8,240,256]{2,1,0:T(8,128)(2,1)} %shard_map.117), calls=%async_computation.2 | async-start | bytes 1966080 | tf_op jit(solution)/shard_map/all_to_all | solution.py:580
  67.6 4.8 %collective-permute-start.16 = (bf16[160,160]{1,0:T(8,128)(2,1)S(1)}, bf16[160,160]{1,0:T(8,128)(2,1)S(1)}, u32[]{:S(2)}, u32[]{:S(2)}) collective-permute-start(bf16[160,160]{1,0:T(8,128)(2,1)S(1)} %get-tuple-element.101), channel_id=1, source_target_pairs={{0,1},{1,0},{2,3},{3,2},{4,5},{5,4},{6,7},{7,6},{8,9},{9,8},{10,11... | collective-permute-start | bytes 153608 | tf_op jit(solution)/shard_map/ppermute | solution.py:543
  69.3 9.5 %collective-permute-start.17 = (bf16[160,160]{1,0:T(8,128)(2,1)S(1)}, bf16[160,160]{1,0:T(8,128)(2,1)S(1)}, u32[]{:S(2)}, u32[]{:S(2)}) collective-permute-start(bf16[160,160]{1,0:T(8,128)(2,1)S(1)} %get-tuple-element.102), channel_id=1, source_target_pairs={{0,2},{1,3},{2,0},{3,1},{4,6},{5,7},{6,4},{7,5},{8,10},{9,11},{10,... | collective-permute-start | bytes 153608 | tf_op jit(solution)/shard_map/ppermute | solution.py:543
  71.8 7.0 %collective-permute-start.18 = (bf16[160,160]{1,0:T(8,128)(2,1)S(1)}, bf16[160,160]{1,0:T(8,128)(2,1)S(1)}, u32[]{:S(2)}, u32[]{:S(2)}) collective-permute-start(bf16[160,160]{1,0:T(8,128)(2,1)S(1)} %get-tuple-element.103), channel_id=1, source_target_pairs={{0,3},{1,2},{2,1},{3,0},{4,7},{5,6},{6,5},{7,4},{8,11},{9,10},{10,... | collective-permute-start | bytes 153608 | tf_op jit(solution)/shard_map/ppermute | solution.py:543

commit v4 on v3

--- a/solution.py
+++ b/solution.py
@@ -39,29 +39,30 @@
     return lax.dot_general(left, right, (((0,), (0,)), ((), ())), preferred_element_type=F32)
 
 
-def pack_kernel(page_ref, query_ref, key_ref, value_ref, out_ref, *, groups):
+def pack_kernel(start_ref, size_ref, query_ref, key_ref, value_ref, out_ref, *, groups):
     rows, width = query_ref.shape
     feat = width // groups
     for slot, ref in enumerate((query_ref, key_ref, value_ref)):
         turned = ref[...].T
         for g in range(groups):
             out_ref[g, slot * feat : (slot + 1) * feat, :] = turned[g * feat : (g + 1) * feat, :]
+    line = lax.broadcasted_iota(jnp.int32, (INFO, rows), 0)
+    page = jnp.where(line < INFO // 2, start_ref[...], size_ref[...])
+    info = page.astype(F32).astype(BF16)
     for g in range(groups):
-        out_ref[g, 3 * feat :, :] = page_ref[...]
+        out_ref[g, 3 * feat :, :] = info
 
 
 def pack(page_start, page_size, query, key, value, groups):
     rows, width = query.shape
-    line = lax.broadcasted_iota(jnp.int32, (INFO, rows), 0)
-    page = jnp.where(line < INFO // 2, page_start, page_size).astype(BF16)
     return pl.pallas_call(
         functools.partial(pack_kernel, groups=groups),
         out_shape=jax.ShapeDtypeStruct((groups, 3 * (width // groups) + INFO, rows), BF16),
-        in_specs=[VMEM] * 4,
+        in_specs=[VMEM] * 5,
         out_specs=VMEM,
         cost_estimate=cost(2.6),
         compiler_params=WHOLE,
-    )(page, query, key, value)
+    )(page_start, page_size, query, key, value)
 
 
 def project_kernel(weight_ref, *refs, groups, lanes, chips, cores):
@@ -198,9 +199,14 @@
     blocks, _, rows = all_ref.shape
     chips = blocks // CORES
     context_refs = refs[:chips]
-    mixes, log_ref, keys, even, odd = refs[chips:]
+    mixes, log_ref, keys, hides, even, odd = refs[chips:]
     count = blocks // shares
     feat = heads * HD
+    for index in range(count):
+        info = all_ref[shared_block(index, shares), 3 * feat : 3 * feat + INFO, :].astype(F32)
+        begin, size = info[0:1, :], info[INFO // 2 : INFO // 2 + 1, :]
+        for j in range(blocks):
+            hides[index, j : j + 1, :] = jnp.where((begin <= j) & (begin + size > j), 0.0, HIDE)
     for h in range(heads):
         own = slice(h * HD, (h + 1) * HD)
         value_own = slice(2 * feat + h * HD, 2 * feat + (h + 1) * HD)
@@ -213,42 +219,52 @@
             b = shared_block(index, shares)
             part = dot_nn(keys[j * rows : (j + 1) * rows, :], all_ref[b, own, :])
             into[j * rows : (j + 1) * rows, :] = part
-            return jnp.max(part, axis=0, keepdims=True) + hidden_row(all_ref, b, j, feat)
-
-        def one_block(index, following, held, into, top):
-            b = shared_block(index, shares)
+            return jnp.max(part, axis=0, keepdims=True) + hides[index, j : j + 1, :]
+
+        def one_block(index, seen, following, next_seen, held, into, top):
             base = top * SCALING
             total, mixed, waiting, next_top = None, None, None, None
-            for j in range(blocks + 1):
+            for step in range(max(len(seen) + 1, len(next_seen))):
                 weight = None
-                if j < blocks:
-                    part_top = score(following, j, into)
+                if step < len(next_seen):
+                    part_top = score(following, next_seen[step], into)
                     next_top = part_top if next_top is None else jnp.maximum(next_top, part_top)
+                if step < len(seen):
+                    j = seen[step]
                     weight = jnp.exp(
-                        held[j * rows : (j + 1) * rows, :] * SCALING
-                        + (hidden_row(all_ref, b, j, feat) - base)
+                        held[j * rows : (j + 1) * rows, :] * SCALING + (hides[index, j : j + 1, :] - base)
                     )
                     part_sum = jnp.sum(weight, axis=0, keepdims=True)
                     total = part_sum if total is None else total + part_sum
                     weight = weight.astype(BF16)
                 if waiting is not None:
-                    part_mix = dot_nn(all_ref[j - 1, value_own, :], waiting)
+                    part_mix = dot_nn(all_ref[seen[step - 1], value_own, :], waiting)
                     mixed = part_mix if mixed is None else mixed + part_mix
                 waiting = weight
             mixes[index, own, :] = (mixed / total).astype(BF16)
             log_ref[index, h : h + 1, :] = base + jnp.log(total)
             return next_top
 
+        every = list(range(blocks))
+        lists = [seen_blocks(b, blocks) if shares == 1 else every for b in range(count)] + [[]]
+        alike = 2
+        while alike + 2 < count and lists[alike + 1] == lists[0] and lists[alike + 2] == lists[0]:
+            alike += 2
+
         def step(pair, top):
-            top = one_block(2 * pair, 2 * pair + 1, even, odd, top)
-            return one_block(2 * pair + 1, jnp.minimum(2 * pair + 2, count - 1), odd, even, top)
-
-        top = score(0, 0, even)
-        for j in range(1, blocks):
-            top = jnp.maximum(top, score(0, j, even))
-        if count % 2:
-            raise ValueError("odd count")
-        lax.fori_loop(0, count // 2, step, top)
+            top = one_block(2 * pair, lists[0], 2 * pair + 1, lists[0], even, odd, top)
+            return one_block(2 * pair + 1, lists[0], 2 * pair + 2, lists[0], odd, even, top)
+
+        top = None
+        for j in lists[0]:
+            part_top = score(0, j, even)
+            top = part_top if top is None else jnp.maximum(top, part_top)
+        if count % 2 or lists[alike] != lists[0]:
+            raise ValueError("block count")
+        top = lax.fori_loop(0, alike // 2, step, top)
+        for index in range(alike, count):
+            held, into = (odd, even) if index % 2 else (even, odd)
+            top = one_block(index, lists[index], index + 1, lists[index + 1], held, into, top)
     me = lax.axis_index("blk")
     for k, ref in enumerate(context_refs):
         for c in range(CORES):
@@ -274,6 +290,7 @@
         out_specs=(VMEM,) * (chips + 2),
         scratch_shapes=[
             pltpu.VMEM((blocks * rows, HD), BF16),
+            pltpu.VMEM((count, blocks, rows), F32),
             pltpu.VMEM((blocks * rows, rows), F32),
             pltpu.VMEM((blocks * rows, rows), F32),
         ],

time: 83.4 us -> 82 us (0.983)
  Pallas kernels: 24.6 us -> 22.7 us
  starting transfers between devices: 33.8 us -> 35.1 us
    pallas_call x1, Pallas kernels: 6.94 us -> 4.94 us  [forward(): pl.pallas_call(functools.partial(forward_kernel, heads=heads, shares=shar...]
  transfers between devices with their start and end apart: 22 -> 22, of which waited for: 12 -> 13; matrix products, arithmetic and copies ran while one was open for 0% -> 0% of each run, Pallas kernels for 25% -> 23%
where the time goes in v4:
time: 82 us; the launch traced here: 81.6 us
  starting transfers between devices  35.1 us (43%)
  Pallas kernels  22.7 us (28%)
  waiting for transfers between devices  20.4 us (25%)
  between operations  2.05 us (2%)
  local copies, waits for them, and re-layouts  1.44 us (2%)
    ppermute x19, starting transfers between devices, swap(): return lax.ppermute(array, axis, [(i, i ^ mask) for i in range(size)])  22.1 us
    ppermute x19, waiting for transfers between devices, swap(): return lax.ppermute(array, axis, [(i, i ^ mask) for i in range(size)])  13.7 us
    pallas_call x1, Pallas kernels, backward(): pl.pallas_call(functools.partial(backward_kernel, heads=heads, shares=sha...  9.95 us
    all_to_all x1, starting transfers between devices, body(): lax.all_to_all(packed, 'blk', split_axis=0, concat_axis=0, tiled=True)  5.3 us
    pallas_call x1, Pallas kernels, forward(): pl.pallas_call(functools.partial(forward_kernel, heads=heads, shares=shar...  4.94 us
    all_to_all x1, starting transfers between devices, body(): lax.all_to_all(grads, 'blk', split_axis=0, concat_axis=0, tiled=True)  4.14 us
    all_to_all x1, waiting for transfers between devices, body(): lax.all_to_all(grads, 'blk', split_axis=0, concat_axis=0, tiled=True)  3.99 us
    all_to_all x1, starting transfers between devices, body(): lax.all_to_all(results, 'blk', split_axis=0, concat_axis=0, tiled=True)  3.55 us
  transfers between devices with their start and end apart: 22, of which 13 were waited for; matrix products, arithmetic and copies ran while one was open for 0% of the time, Pallas kernels for 23%

profile of v4, /device:TPU:0, one launch (start us, length us, event | category | flops | bytes accessed | tf_op | source)
XLA Modules:
  0.0 81.6 jit_solution(15015785728320737697)
XLA Ops:
  1.9 2.5 %shard_map.111 = bf16[8,256,256]{2,1,0:T(8,128)(2,1)} custom-call(s32[1,1]{1,0:T(1,128)S(6)} %copy.12.start_ref, s32[1,1]{1,0:T(1,128)S(6)} %copy.13.size_ref, bf16[256,640]{1,0:T(8,128)(2,1)} %bitcast.6, bf16[256,640]{1,0:T(8,128)(2,1)} %bitcast.7, bf16[256,640]{1,0:T(8,128)(2,1)} %bitcast.8), custom_call_target="tpu_custom_call" | custom-call | flops 2990000128 | tf_op jit(solution)/shard_map/pallas_call | solution.py:58
  4.4 5.3 %all-to-all-start = ((bf16[8,256,256]{2,1,0:T(8,128)(2,1)}), bf16[8,256,256]{2,1,0:T(8,128)(2,1)S(1)}, u32[]{:S(2)}, u32[]{:S(2)}) async-start(bf16[8,256,256]{2,1,0:T(8,128)(2,1)} %shard_map.111), calls=%async_computation | async-start | bytes 2097152 | tf_op jit(solution)/shard_map/all_to_all | solution.py:582
  9.7 2.7 %collective-permute-start.1 = (s32[1,64]{1,0:T(1,128)S(1)}, s32[1,64]{1,0:T(1,128)S(1)}, u32[]{:S(2)}, u32[]{:S(2)}) collective-permute-start(s32[1,64]{1,0:T(1,128)S(1)} %copy-done.2), channel_id=1, source_target_pairs={{0,2},{1,3},{2,0},{3,1},{4,6},{5,7},{6,4},{7,5},{8,10},{9,11},{10,... | collective-permute-start | bytes 776 | tf_op jit(solution)/shard_map/ppermute | solution.py:560
  12.4 1.6 %collective-permute-start = (s32[1,64]{1,0:T(1,128)S(1)}, s32[1,64]{1,0:T(1,128)S(1)}, u32[]{:S(2)}, u32[]{:S(2)}) collective-permute-start(s32[1,64]{1,0:T(1,128)S(1)} %copy-done.2), channel_id=1, source_target_pairs={{0,1},{1,0},{2,3},{3,2},{4,5},{5,4},{6,7},{7,6},{8,9},{9,8},{10,11... | collective-permute-start | bytes 776 | tf_op jit(solution)/shard_map/ppermute | solution.py:560
  14.2 1.7 %collective-permute-done.refs_1_ = s32[1,64]{1,0:T(1,128)S(1)} collective-permute-done((s32[1,64]{1,0:T(1,128)S(1)}, s32[1,64]{1,0:T(1,128)S(1)}, u32[]{:S(2)}, u32[]{:S(2)}) %collective-permute-start) | collective-permute-done | bytes 288 | tf_op jit(solution)/shard_map/ppermute | solution.py:560
  15.9 3.4 %collective-permute-done.2.refs_3_ = s32[1,64]{1,0:T(1,128)S(1)} collective-permute-done((s32[1,64]{1,0:T(1,128)S(1)}, s32[1,64]{1,0:T(1,128)S(1)}, u32[]{:S(2)}, u32[]{:S(2)}) %collective-permute-start.2) | collective-permute-done | bytes 288 | tf_op jit(solution)/shard_map/ppermute | solution.py:560
  19.3 0.5 shard_map.112
  19.9 0.8 collective-permute-start.4
  20.7 3.6 %collective-permute-start.5 = (bf16[16,5120]{1,0:T(8,128)(2,1)S(1)}, bf16[16,5120]{1,0:T(8,128)(2,1)S(1)}, u32[]{:S(2)}, u32[]{:S(2)}) collective-permute-start(bf16[16,5120]{1,0:T(8,128)(2,1)S(1)} %get-tuple-element.62), channel_id=1, source_target_pairs={{0,3},{1,2},{2,1},{3,0},{4,7},{5,6},{6,5},{7,4},{8,11},{9,10},{10,... | collective-permute-start | bytes 491528 | tf_op jit(solution)/shard_map/ppermute | solution.py:560
  24.3 0.9 %all-to-all-done.all_ref = bf16[8,256,256]{2,1,0:T(8,128)(2,1)S(1)} async-done(((bf16[8,256,256]{2,1,0:T(8,128)(2,1)}), bf16[8,256,256]{2,1,0:T(8,128)(2,1)S(1)}, u32[]{:S(2)}, u32[]{:S(2)}) %all-to-all-start) | async-done | bytes 1048608 | tf_op jit(solution)/shard_map/all_to_all | solution.py:582
  25.1 4.9 %shard_map.113 = (bf16[2,80,256]{2,1,0:T(8,128)(2,1)S(1)}, bf16[2,80,256]{2,1,0:T(8,128)(2,1)S(1)}, bf16[2,80,256]{2,1,0:T(8,128)(2,1)S(1)}, bf16[2,80,256]{2,1,...) custom-call(bf16[8,256,256]{2,1,0:T(8,128)(2,1)S(1)} %all-to-all-done.all_ref), custom_call_target="tpu_custom_call" | custom-call | flops 8049999872 | tf_op jit(solution)/shard_map/pallas_call | solution.py:282
  30.1 1.2 %collective-permute-start.6 = (bf16[2,80,256]{2,1,0:T(8,128)(2,1)S(1)}, bf16[2,80,256]{2,1,0:T(8,128)(2,1)S(1)}, u32[]{:S(2)}, u32[]{:S(2)}) collective-permute-start(bf16[2,80,256]{2,1,0:T(8,128)(2,1)S(1)} %get-tuple-element.71), channel_id=1, source_target_pairs={{0,8},{4,12},{8,0},{12,4},{16,24},{20,28},{24,16},{28,20},{1,9},{5... | collective-permute-start | bytes 245768 | tf_op jit(solution)/shard_map/ppermute | solution.py:560
  31.2 1.5 %collective-permute-start.7 = (bf16[2,80,256]{2,1,0:T(8,128)(2,1)S(1)}, bf16[2,80,256]{2,1,0:T(8,128)(2,1)S(1)}, u32[]{:S(2)}, u32[]{:S(2)}) collective-permute-start(bf16[2,80,256]{2,1,0:T(8,128)(2,1)S(1)} %get-tuple-element.72), channel_id=1, source_target_pairs={{0,16},{4,20},{8,24},{12,28},{16,0},{20,4},{24,8},{28,12},{1,17},{... | collective-permute-start | bytes 245768 | tf_op jit(solution)/shard_map/ppermute | solution.py:560
  32.7 0.9 %collective-permute-start.8 = (bf16[2,80,256]{2,1,0:T(8,128)(2,1)S(1)}, bf16[2,80,256]{2,1,0:T(8,128)(2,1)S(1)}, u32[]{:S(2)}, u32[]{:S(2)}) collective-permute-start(bf16[2,80,256]{2,1,0:T(8,128)(2,1)S(1)} %get-tuple-element.73), channel_id=1, source_target_pairs={{0,24},{4,28},{8,16},{12,20},{16,8},{20,12},{24,0},{28,4},{1,25},{... | collective-permute-start | bytes 245768 | tf_op jit(solution)/shard_map/ppermute | solution.py:560
  34.1 1.4 %copy-done = bf16[640,1280]{1,0:T(8,128)(2,1)S(1)} copy-done((bf16[640,1280]{1,0:T(8,128)(2,1)S(1)}, bf16[640,1280]{1,0:T(8,128)(2,1)}, u32[]{:S(2)}) %copy-start) | copy-done | bytes 1638424
  35.5 1.6 %shard_map.114 = (bf16[8,80,256]{2,1,0:T(8,128)(2,1)}, bf16[64,2560]{1,0:T(8,128)(2,1)S(1)}, bf16[160,256]{1,0:T(8,128)(2,1)S(1)}, bf16[160,256]{1,0:T(8,128)(2,...) custom-call(bf16[640,1280]{1,0:T(8,128)(2,1)S(1)} %copy-done, ...), custom_call_target="tpu_custom_call" | custom-call | flops 805000000 | tf_op jit(solution)/shard_map/pallas_call | solution.py:120
  37.1 4.1 %all-to-all-start.1 = ((bf16[8,80,256]{2,1,0:T(8,128)(2,1)}), bf16[8,80,256]{2,1,0:T(8,128)(2,1)S(1)}, u32[]{:S(2)}, u32[]{:S(2)}) async-start(bf16[8,80,256]{2,1,0:T(8,128)(2,1)} %get-tuple-element.68), calls=%async_computation.1 | async-start | bytes 655360 | tf_op jit(solution)/shard_map/all_to_all | solution.py:592
  41.3 0.6 collective-permute-start.9
  43.8 1.1 %shard_map.116 = (bf16[160,640]{1,0:T(8,128)(2,1)S(1)}, bf16[160,640]{1,0:T(8,128)(2,1)S(1)}, bf16[160,640]{1,0:T(8,128)(2,1)S(1)}, bf16[160,640]{1,0:T(8,128)(2,1)S(1)}) custom-call(bf16[64,2560]{1,0:T(8,128)(2,1)S(1)} %get-tuple-element.69.keep_ref, bf16[2,80,256]{2,1,0:T(8,128)(2,1)S(1)} %get-tuple-element.70.refs_0_, ...), custom_call_target="tpu_custom_call" | custom-call | flops 230000000 | tf_op jit(solution)/shard_map/pallas_call | solution.py:497
  44.9 4.0 %all-to-all-done.1.grads_ref = bf16[8,80,256]{2,1,0:T(8,128)(2,1)S(1)} async-done(((bf16[8,80,256]{2,1,0:T(8,128)(2,1)}), bf16[8,80,256]{2,1,0:T(8,128)(2,1)S(1)}, u32[]{:S(2)}, u32[]{:S(2)}) %all-to-all-start.1) | async-done | bytes 327712 | tf_op jit(solution)/shard_map/all_to_all | solution.py:592
  48.9 0.6 collective-permute-start.13
  49.4 0.6 collective-permute-start.14
  50.0 2.4 %collective-permute-start.15 = (bf16[160,640]{1,0:T(8,128)(2,1)S(1)}, bf16[160,640]{1,0:T(8,128)(2,1)S(1)}, u32[]{:S(2)}, u32[]{:S(2)}) collective-permute-start(bf16[160,640]{1,0:T(8,128)(2,1)S(1)} %get-tuple-element.95), channel_id=1, source_target_pairs={{0,24},{4,28},{8,16},{12,20},{16,8},{20,12},{24,0},{28,4},{1,25},{... | collective-permute-start | bytes 614408 | tf_op jit(solution)/shard_map/ppermute | solution.py:560
  52.4 10.0 %shard_map.117 = bf16[8,240,256]{2,1,0:T(8,128)(2,1)} custom-call(bf16[8,256,256]{2,1,0:T(8,128)(2,1)S(1)} %all-to-all-done.all_ref, bf16[8,80,256]{2,1,0:T(8,128)(2,1)S(1)} %all-to-all-done.1.grads_ref, bf16[8,80,256]{2,1,0:T(8,128)(2,1)S(1)} %get-tuple-element.87.context_ref, f32[8,1,256]{2,1,0:T(1,128)S(1)} %get-tuple-element.88.log_ref), custom_call_target="tpu_custom_call" | custom-call | flops 12650000384 | tf_op jit(solution)/shard_map/pallas_call | solution.py:373
  62.3 3.6 %all-to-all-start.2 = ((bf16[8,240,256]{2,1,0:T(8,128)(2,1)}), bf16[8,240,256]{2,1,0:T(8,128)(2,1)S(1)}, u32[]{:S(2)}, u32[]{:S(2)}) async-start(bf16[8,240,256]{2,1,0:T(8,128)(2,1)} %shard_map.117), calls=%async_computation.2 | async-start | bytes 1966080 | tf_op jit(solution)/shard_map/all_to_all | solution.py:597
  66.2 2.5 %collective-permute-start.16 = (bf16[160,160]{1,0:T(8,128)(2,1)S(1)}, bf16[160,160]{1,0:T(8,128)(2,1)S(1)}, u32[]{:S(2)}, u32[]{:S(2)}) collective-permute-start(bf16[160,160]{1,0:T(8,128)(2,1)S(1)} %get-tuple-element.101), channel_id=1, source_target_pairs={{0,1},{1,0},{2,3},{3,2},{4,5},{5,4},{6,7},{7,6},{8,9},{9,8},{10,11... | collective-permute-start | bytes 153608 | tf_op jit(solution)/shard_map/ppermute | solution.py:560
  69.2 1.9 %collective-permute-start.18 = (bf16[160,160]{1,0:T(8,128)(2,1)S(1)}, bf16[160,160]{1,0:T(8,128)(2,1)S(1)}, u32[]{:S(2)}, u32[]{:S(2)}) collective-permute-start(bf16[160,160]{1,0:T(8,128)(2,1)S(1)} %get-tuple-element.103), channel_id=1, source_target_pairs={{0,3},{1,2},{2,1},{3,0},{4,7},{5,6},{6,5},{7,4},{8,11},{9,10},{10,... | collective-permute-start | bytes 153608 | tf_op jit(solution)/shard_map/ppermute | solution.py:560
  71.2 0.5 collective-permute-done.16.refs_1_
  71.7 6.2 %collective-permute-done.17.refs_2_ = bf16[160,160]{1,0:T(8,128)(2,1)S(1)} collective-permute-done((bf16[160,160]{1,0:T(8,128)(2,1)S(1)}, bf16[160,160]{1,0:T(8,128)(2,1)S(1)}, u32[]{:S(2)}, u32[]{:S(2)}) %collective-permute-start.17) | collective-permute-done | bytes 51232 | tf_op jit(solution)/shard_map/ppermute | solution.py:560
  78.0 0.7 shard_map.120
  78.7 1.9 %all-to-all-done.2.all_ref = bf16[8,240,256]{2,1,0:T(8,128)(2,1)S(1)} async-done(((bf16[8,240,256]{2,1,0:T(8,128)(2,1)}), bf16[8,240,256]{2,1,0:T(8,128)(2,1)S(1)}, u32[]{:S(2)}, u32[]{:S(2)}) %all-to-all-start.2) | async-done | bytes 983072 | tf_op jit(solution)/shard_map/all_to_all | solution.py:597
  80.5 1.1 %shard_map.118 = (bf16[256,640]{1,0:T(8,128)(2,1)}, bf16[256,640]{1,0:T(8,128)(2,1)}, bf16[256,640]{1,0:T(8,128)(2,1)}) custom-call(bf16[8,240,256]{2,1,0:T(8,128)(2,1)S(1)} %all-to-all-done.2.all_ref), custom_call_target="tpu_custom_call" | custom-call | flops 1264999936 | tf_op jit(solution)/shard_map/pallas_call | solution.py:413
  (28 shorter events, 3.6 us)
Async XLA Ops:
  4.4 5.3 %copy-start.2 = (s32[1,64]{1,0:T(1,128)S(1)}, s32[1,64]{1,0:T(1,128)}, u32[]{:S(2)}) copy-start(s32[1,64]{1,0:T(1,128)} %refs_0_.1) | copy-start | bytes 772
  4.4 14.9 %copy-start.1 = (bf16[64,5120]{1,0:T(8,128)(2,1)S(1)}, bf16[64,5120]{1,0:T(8,128)(2,1)}, u32[]{:S(2)}) copy-start(bf16[64,5120]{1,0:T(8,128)(2,1)} %grad_ref.1) | copy-start | bytes 1966084
  4.4 20.7 %all-to-all-start = ((bf16[8,256,256]{2,1,0:T(8,128)(2,1)}), bf16[8,256,256]{2,1,0:T(8,128)(2,1)S(1)}, u32[]{:S(2)}, u32[]{:S(2)}) async-start(bf16[8,256,256]{2,1,0:T(8,128)(2,1)} %shard_map.111), calls=%async_computation | async-start | bytes 2097152 | tf_op jit(solution)/shard_map/all_to_all | solution.py:582
  9.7 4.5 %collective-permute-start.1 = (s32[1,64]{1,0:T(1,128)S(1)}, s32[1,64]{1,0:T(1,128)S(1)}, u32[]{:S(2)}, u32[]{:S(2)}) collective-permute-start(s32[1,64]{1,0:T(1,128)S(1)} %copy-done.2), channel_id=1, source_target_pairs={{0,2},{1,3},{2,0},{3,1},{4,6},{5,7},{6,4},{7,5},{8,10},{9,11},{10,... | collective-permute-start | bytes 776 | tf_op jit(solution)/shard_map/ppermute | solution.py:560
  12.4 3.5 %collective-permute-start = (s32[1,64]{1,0:T(1,128)S(1)}, s32[1,64]{1,0:T(1,128)S(1)}, u32[]{:S(2)}, u32[]{:S(2)}) collective-permute-start(s32[1,64]{1,0:T(1,128)S(1)} %copy-done.2), channel_id=1, source_target_pairs={{0,1},{1,0},{2,3},{3,2},{4,5},{5,4},{6,7},{7,6},{8,9},{9,8},{10,11... | collective-permute-start | bytes 776 | tf_op jit(solution)/shard_map/ppermute | solution.py:560
  14.0 5.3 %collective-permute-start.2 = (s32[1,64]{1,0:T(1,128)S(1)}, s32[1,64]{1,0:T(1,128)S(1)}, u32[]{:S(2)}, u32[]{:S(2)}) collective-permute-start(s32[1,64]{1,0:T(1,128)S(1)} %copy-done.2), channel_id=1, source_target_pairs={{0,3},{1,2},{2,1},{3,0},{4,7},{5,6},{6,5},{7,4},{8,11},{9,10},{10,... | collective-permute-start | bytes 776 | tf_op jit(solution)/shard_map/ppermute | solution.py:560
  19.8 10.2 %collective-permute-start.3 = (bf16[16,5120]{1,0:T(8,128)(2,1)S(1)}, bf16[16,5120]{1,0:T(8,128)(2,1)S(1)}, u32[]{:S(2)}, u32[]{:S(2)}) collective-permute-start(bf16[16,5120]{1,0:T(8,128)(2,1)S(1)} %get-tuple-element.55), channel_id=1, source_target_pairs={{0,1},{1,0},{2,3},{3,2},{4,5},{5,4},{6,7},{7,6},{8,9},{9,8},{10,11... | collective-permute-start | bytes 491528 | tf_op jit(solution)/shard_map/ppermute | solution.py:560
  19.9 14.2 %collective-permute-start.4 = (bf16[16,5120]{1,0:T(8,128)(2,1)S(1)}, bf16[16,5120]{1,0:T(8,128)(2,1)S(1)}, u32[]{:S(2)}, u32[]{:S(2)}) collective-permute-start(bf16[16,5120]{1,0:T(8,128)(2,1)S(1)} %get-tuple-element.61), channel_id=1, source_target_pairs={{0,2},{1,3},{2,0},{3,1},{4,6},{5,7},{6,4},{7,5},{8,10},{9,11},{10,... | collective-permute-start | bytes 491528 | tf_op jit(solution)/shard_map/ppermute | solution.py:560
  20.7 13.4 %collective-permute-start.5 = (bf16[16,5120]{1,0:T(8,128)(2,1)S(1)}, bf16[16,5120]{1,0:T(8,128)(2,1)S(1)}, u32[]{:S(2)}, u32[]{:S(2)}) collective-permute-start(bf16[16,5120]{1,0:T(8,128)(2,1)S(1)} %get-tuple-element.62), channel_id=1, source_target_pairs={{0,3},{1,2},{2,1},{3,0},{4,7},{5,6},{6,5},{7,4},{8,11},{9,10},{10,... | collective-permute-start | bytes 491528 | tf_op jit(solution)/shard_map/ppermute | solution.py:560
  30.1 11.2 %collective-permute-start.6 = (bf16[2,80,256]{2,1,0:T(8,128)(2,1)S(1)}, bf16[2,80,256]{2,1,0:T(8,128)(2,1)S(1)}, u32[]{:S(2)}, u32[]{:S(2)}) collective-permute-start(bf16[2,80,256]{2,1,0:T(8,128)(2,1)S(1)} %get-tuple-element.71), channel_id=1, source_target_pairs={{0,8},{4,12},{8,0},{12,4},{16,24},{20,28},{24,16},{28,20},{1,9},{5... | collective-permute-start | bytes 245768 | tf_op jit(solution)/shard_map/ppermute | solution.py:560
  31.2 10.0 %collective-permute-start.7 = (bf16[2,80,256]{2,1,0:T(8,128)(2,1)S(1)}, bf16[2,80,256]{2,1,0:T(8,128)(2,1)S(1)}, u32[]{:S(2)}, u32[]{:S(2)}) collective-permute-start(bf16[2,80,256]{2,1,0:T(8,128)(2,1)S(1)} %get-tuple-element.72), channel_id=1, source_target_pairs={{0,16},{4,20},{8,24},{12,28},{16,0},{20,4},{24,8},{28,12},{1,17},{... | collective-permute-start | bytes 245768 | tf_op jit(solution)/shard_map/ppermute | solution.py:560
  32.7 8.5 %collective-permute-start.8 = (bf16[2,80,256]{2,1,0:T(8,128)(2,1)S(1)}, bf16[2,80,256]{2,1,0:T(8,128)(2,1)S(1)}, u32[]{:S(2)}, u32[]{:S(2)}) collective-permute-start(bf16[2,80,256]{2,1,0:T(8,128)(2,1)S(1)} %get-tuple-element.73), channel_id=1, source_target_pairs={{0,24},{4,28},{8,16},{12,20},{16,8},{20,12},{24,0},{28,4},{1,25},{... | collective-permute-start | bytes 245768 | tf_op jit(solution)/shard_map/ppermute | solution.py:560
  34.1 1.4 %copy-start = (bf16[640,1280]{1,0:T(8,128)(2,1)S(1)}, bf16[640,1280]{1,0:T(8,128)(2,1)}, u32[]{:S(2)}) copy-start(bf16[640,1280]{1,0:T(8,128)(2,1)} %weight_ref.1) | copy-start | bytes 4915204
  37.1 11.8 %all-to-all-start.1 = ((bf16[8,80,256]{2,1,0:T(8,128)(2,1)}), bf16[8,80,256]{2,1,0:T(8,128)(2,1)S(1)}, u32[]{:S(2)}, u32[]{:S(2)}) async-start(bf16[8,80,256]{2,1,0:T(8,128)(2,1)} %get-tuple-element.68), calls=%async_computation.1 | async-start | bytes 655360 | tf_op jit(solution)/shard_map/all_to_all | solution.py:592
  41.3 1.6 %collective-permute-start.9 = (bf16[320,256]{1,0:T(8,128)(2,1)S(1)}, bf16[320,256]{1,0:T(8,128)(2,1)S(1)}, u32[]{:S(2)}, u32[]{:S(2)}) collective-permute-start(bf16[320,256]{1,0:T(8,128)(2,1)S(1)} %get-tuple-element.78), channel_id=1, source_target_pairs={{0,4},{4,0},{8,12},{12,8},{16,20},{20,16},{24,28},{28,24},{1,5},{5... | collective-permute-start | bytes 491528 | tf_op jit(solution)/shard_map/ppermute | solution.py:560
  41.9 1.4 %collective-permute-start.10 = (bf16[320,256]{1,0:T(8,128)(2,1)S(1)}, bf16[320,256]{1,0:T(8,128)(2,1)S(1)}, u32[]{:S(2)}, u32[]{:S(2)}) collective-permute-start(bf16[320,256]{1,0:T(8,128)(2,1)S(1)} %get-tuple-element.79), channel_id=1, source_target_pairs={{0,4},{4,0},{8,12},{12,8},{16,20},{20,16},{24,28},{28,24},{1,5},{5... | collective-permute-start | bytes 491528 | tf_op jit(solution)/shard_map/ppermute | solution.py:560
  42.0 1.6 %collective-permute-start.11 = (bf16[320,256]{1,0:T(8,128)(2,1)S(1)}, bf16[320,256]{1,0:T(8,128)(2,1)S(1)}, u32[]{:S(2)}, u32[]{:S(2)}) collective-permute-start(bf16[320,256]{1,0:T(8,128)(2,1)S(1)} %get-tuple-element.80), channel_id=1, source_target_pairs={{0,4},{4,0},{8,12},{12,8},{16,20},{20,16},{24,28},{28,24},{1,5},{5... | collective-permute-start | bytes 491528 | tf_op jit(solution)/shard_map/ppermute | solution.py:560
  42.4 1.4 %collective-permute-start.12 = (bf16[320,256]{1,0:T(8,128)(2,1)S(1)}, bf16[320,256]{1,0:T(8,128)(2,1)S(1)}, u32[]{:S(2)}, u32[]{:S(2)}) collective-permute-start(bf16[320,256]{1,0:T(8,128)(2,1)S(1)} %get-tuple-element.81), channel_id=1, source_target_pairs={{0,4},{4,0},{8,12},{12,8},{16,20},{20,16},{24,28},{28,24},{1,5},{5... | collective-permute-start | bytes 491528 | tf_op jit(solution)/shard_map/ppermute | solution.py:560
  48.9 17.0 %collective-permute-start.13 = (bf16[160,640]{1,0:T(8,128)(2,1)S(1)}, bf16[160,640]{1,0:T(8,128)(2,1)S(1)}, u32[]{:S(2)}, u32[]{:S(2)}) collective-permute-start(bf16[160,640]{1,0:T(8,128)(2,1)S(1)} %get-tuple-element.93), channel_id=1, source_target_pairs={{0,8},{4,12},{8,0},{12,4},{16,24},{20,28},{24,16},{28,20},{1,9},{5... | collective-permute-start | bytes 614408 | tf_op jit(solution)/shard_map/ppermute | solution.py:560
  49.4 16.5 %collective-permute-start.14 = (bf16[160,640]{1,0:T(8,128)(2,1)S(1)}, bf16[160,640]{1,0:T(8,128)(2,1)S(1)}, u32[]{:S(2)}, u32[]{:S(2)}) collective-permute-start(bf16[160,640]{1,0:T(8,128)(2,1)S(1)} %get-tuple-element.94), channel_id=1, source_target_pairs={{0,16},{4,20},{8,24},{12,28},{16,0},{20,4},{24,8},{28,12},{1,17},{... | collective-permute-start | bytes 614408 | tf_op jit(solution)/shard_map/ppermute | solution.py:560
  50.0 15.9 %collective-permute-start.15 = (bf16[160,640]{1,0:T(8,128)(2,1)S(1)}, bf16[160,640]{1,0:T(8,128)(2,1)S(1)}, u32[]{:S(2)}, u32[]{:S(2)}) collective-permute-start(bf16[160,640]{1,0:T(8,128)(2,1)S(1)} %get-tuple-element.95), channel_id=1, source_target_pairs={{0,24},{4,28},{8,16},{12,20},{16,8},{20,12},{24,0},{28,4},{1,25},{... | collective-permute-start | bytes 614408 | tf_op jit(solution)/shard_map/ppermute | solution.py:560
  62.3 18.2 %all-to-all-start.2 = ((bf16[8,240,256]{2,1,0:T(8,128)(2,1)}), bf16[8,240,256]{2,1,0:T(8,128)(2,1)S(1)}, u32[]{:S(2)}, u32[]{:S(2)}) async-start(bf16[8,240,256]{2,1,0:T(8,128)(2,1)} %shard_map.117), calls=%async_computation.2 | async-start | bytes 1966080 | tf_op jit(solution)/shard_map/all_to_all | solution.py:597
  66.2 5.5 %collective-permute-start.16 = (bf16[160,160]{1,0:T(8,128)(2,1)S(1)}, bf16[160,160]{1,0:T(8,128)(2,1)S(1)}, u32[]{:S(2)}, u32[]{:S(2)}) collective-permute-start(bf16[160,160]{1,0:T(8,128)(2,1)S(1)} %get-tuple-element.101), channel_id=1, source_target_pairs={{0,1},{1,0},{2,3},{3,2},{4,5},{5,4},{6,7},{7,6},{8,9},{9,8},{10,11... | collective-permute-start | bytes 153608 | tf_op jit(solution)/shard_map/ppermute | solution.py:560
  68.7 9.2 %collective-permute-start.17 = (bf16[160,160]{1,0:T(8,128)(2,1)S(1)}, bf16[160,160]{1,0:T(8,128)(2,1)S(1)}, u32[]{:S(2)}, u32[]{:S(2)}) collective-permute-start(bf16[160,160]{1,0:T(8,128)(2,1)S(1)} %get-tuple-element.102), channel_id=1, source_target_pairs={{0,2},{1,3},{2,0},{3,1},{4,6},{5,7},{6,4},{7,5},{8,10},{9,11},{10,... | collective-permute-start | bytes 153608 | tf_op jit(solution)/shard_map/ppermute | solution.py:560
  69.2 8.7 %collective-permute-start.18 = (bf16[160,160]{1,0:T(8,128)(2,1)S(1)}, bf16[160,160]{1,0:T(8,128)(2,1)S(1)}, u32[]{:S(2)}, u32[]{:S(2)}) collective-permute-start(bf16[160,160]{1,0:T(8,128)(2,1)S(1)} %get-tuple-element.103), channel_id=1, source_target_pairs={{0,3},{1,2},{2,1},{3,0},{4,7},{5,6},{6,5},{7,4},{8,11},{9,10},{10,... | collective-permute-start | bytes 153608 | tf_op jit(solution)/shard_map/ppermute | solution.py:560

commit v5 on v4

--- a/solution.py
+++ b/solution.py
@@ -592,7 +592,7 @@
     grads = lax.all_to_all(grads, "blk", split_axis=0, concat_axis=0, tiled=True)
     far = [swap(array, "blk", cycle, 1) for array in join(near, pieces)]
     terms = weight_terms(keep, near, far, width, lanes, CORES, shares)
-    grads, terms = after((grads, terms))
+    grads, _ = after((grads, terms))
     results = backward(gathered, grads, context, log_total, heads, shares)
     returned = lax.all_to_all(results, "blk", split_axis=0, concat_axis=0, tiled=True)
     sums, results = after((swap_all(terms, "blk", cycle, CORES), results))

time: 82 us -> 78.5 us (0.957)
  waiting for transfers between devices: 20.4 us -> 16.9 us
    all_to_all x1, waiting for transfers between devices: 3.99 us -> 0.43 us  [body(): lax.all_to_all(grads, 'blk', split_axis=0, concat_axis=0, tiled=True)]
  transfers between devices with their start and end apart: 22 -> 22, of which waited for: 13 -> 13; matrix products, arithmetic and copies ran while one was open for 0% -> 0% of each run, Pallas kernels for 23% -> 24%
where the time goes in v5:
time: 78.5 us; the launch traced here: 78.1 us
  starting transfers between devices  35.1 us (45%)
  Pallas kernels  22.7 us (29%)
  waiting for transfers between devices  16.9 us (22%)
  between operations  2.05 us (3%)
  local copies, waits for them, and re-layouts  1.44 us (2%)
    ppermute x19, starting transfers between devices, swap(): return lax.ppermute(array, axis, [(i, i ^ mask) for i in range(size)])  22.1 us
    ppermute x19, waiting for transfers between devices, swap(): return lax.ppermute(array, axis, [(i, i ^ mask) for i in range(size)])  13.8 us
    pallas_call x1, Pallas kernels, backward(): pl.pallas_call(functools.partial(backward_kernel, heads=heads, shares=sha...  9.95 us
    all_to_all x1, starting transfers between devices, body(): lax.all_to_all(packed, 'blk', split_axis=0, concat_axis=0, tiled=True)  5.3 us
    pallas_call x1, Pallas kernels, forward(): pl.pallas_call(functools.partial(forward_kernel, heads=heads, shares=shar...  4.94 us
    all_to_all x1, starting transfers between devices, body(): lax.all_to_all(grads, 'blk', split_axis=0, concat_axis=0, tiled=True)  4.14 us
    all_to_all x1, starting transfers between devices, body(): lax.all_to_all(results, 'blk', split_axis=0, concat_axis=0, tiled=True)  3.55 us
    pallas_call x1, Pallas kernels, pack(): pl.pallas_call(functools.partial(pack_kernel, groups=groups), out_shape=j...  2.48 us
  transfers between devices with their start and end apart: 22, of which 13 were waited for; matrix products, arithmetic and copies ran while one was open for 0% of the time, Pallas kernels for 24%

profile of v5, /device:TPU:0, one launch (start us, length us, event | category | flops | bytes accessed | tf_op | source)
XLA Modules:
  0.0 78.1 jit_solution(4498492626614522347)
XLA Ops:
  1.9 2.5 %shard_map.111 = bf16[8,256,256]{2,1,0:T(8,128)(2,1)} custom-call(s32[1,1]{1,0:T(1,128)S(6)} %copy.12.start_ref, s32[1,1]{1,0:T(1,128)S(6)} %copy.13.size_ref, bf16[256,640]{1,0:T(8,128)(2,1)} %bitcast.6, bf16[256,640]{1,0:T(8,128)(2,1)} %bitcast.7, bf16[256,640]{1,0:T(8,128)(2,1)} %bitcast.8), custom_call_target="tpu_custom_call" | custom-call | flops 2990000128 | tf_op jit(solution)/shard_map/pallas_call | solution.py:58
  4.4 5.3 %all-to-all-start = ((bf16[8,256,256]{2,1,0:T(8,128)(2,1)}), bf16[8,256,256]{2,1,0:T(8,128)(2,1)S(1)}, u32[]{:S(2)}, u32[]{:S(2)}) async-start(bf16[8,256,256]{2,1,0:T(8,128)(2,1)} %shard_map.111), calls=%async_computation | async-start | bytes 2097152 | tf_op jit(solution)/shard_map/all_to_all | solution.py:582
  9.7 2.7 %collective-permute-start.1 = (s32[1,64]{1,0:T(1,128)S(1)}, s32[1,64]{1,0:T(1,128)S(1)}, u32[]{:S(2)}, u32[]{:S(2)}) collective-permute-start(s32[1,64]{1,0:T(1,128)S(1)} %copy-done.2), channel_id=1, source_target_pairs={{0,2},{1,3},{2,0},{3,1},{4,6},{5,7},{6,4},{7,5},{8,10},{9,11},{10,... | collective-permute-start | bytes 776 | tf_op jit(solution)/shard_map/ppermute | solution.py:560
  12.4 1.6 %collective-permute-start = (s32[1,64]{1,0:T(1,128)S(1)}, s32[1,64]{1,0:T(1,128)S(1)}, u32[]{:S(2)}, u32[]{:S(2)}) collective-permute-start(s32[1,64]{1,0:T(1,128)S(1)} %copy-done.2), channel_id=1, source_target_pairs={{0,1},{1,0},{2,3},{3,2},{4,5},{5,4},{6,7},{7,6},{8,9},{9,8},{10,11... | collective-permute-start | bytes 776 | tf_op jit(solution)/shard_map/ppermute | solution.py:560
  14.2 1.7 %collective-permute-done.refs_1_ = s32[1,64]{1,0:T(1,128)S(1)} collective-permute-done((s32[1,64]{1,0:T(1,128)S(1)}, s32[1,64]{1,0:T(1,128)S(1)}, u32[]{:S(2)}, u32[]{:S(2)}) %collective-permute-start) | collective-permute-done | bytes 288 | tf_op jit(solution)/shard_map/ppermute | solution.py:560
  15.9 3.4 %collective-permute-done.2.refs_3_ = s32[1,64]{1,0:T(1,128)S(1)} collective-permute-done((s32[1,64]{1,0:T(1,128)S(1)}, s32[1,64]{1,0:T(1,128)S(1)}, u32[]{:S(2)}, u32[]{:S(2)}) %collective-permute-start.2) | collective-permute-done | bytes 288 | tf_op jit(solution)/shard_map/ppermute | solution.py:560
  19.3 0.5 shard_map.112
  19.9 0.8 collective-permute-start.4
  20.7 3.6 %collective-permute-start.5 = (bf16[16,5120]{1,0:T(8,128)(2,1)S(1)}, bf16[16,5120]{1,0:T(8,128)(2,1)S(1)}, u32[]{:S(2)}, u32[]{:S(2)}) collective-permute-start(bf16[16,5120]{1,0:T(8,128)(2,1)S(1)} %get-tuple-element.58), channel_id=1, source_target_pairs={{0,3},{1,2},{2,1},{3,0},{4,7},{5,6},{6,5},{7,4},{8,11},{9,10},{10,... | collective-permute-start | bytes 491528 | tf_op jit(solution)/shard_map/ppermute | solution.py:560
  24.3 0.9 %all-to-all-done.all_ref = bf16[8,256,256]{2,1,0:T(8,128)(2,1)S(1)} async-done(((bf16[8,256,256]{2,1,0:T(8,128)(2,1)}), bf16[8,256,256]{2,1,0:T(8,128)(2,1)S(1)}, u32[]{:S(2)}, u32[]{:S(2)}) %all-to-all-start) | async-done | bytes 1048608 | tf_op jit(solution)/shard_map/all_to_all | solution.py:582
  25.1 4.9 %shard_map.113 = (bf16[2,80,256]{2,1,0:T(8,128)(2,1)S(1)}, bf16[2,80,256]{2,1,0:T(8,128)(2,1)S(1)}, bf16[2,80,256]{2,1,0:T(8,128)(2,1)S(1)}, bf16[2,80,256]{2,1,...) custom-call(bf16[8,256,256]{2,1,0:T(8,128)(2,1)S(1)} %all-to-all-done.all_ref), custom_call_target="tpu_custom_call" | custom-call | flops 8049999872 | tf_op jit(solution)/shard_map/pallas_call | solution.py:282
  30.1 1.2 %collective-permute-start.6 = (bf16[2,80,256]{2,1,0:T(8,128)(2,1)S(1)}, bf16[2,80,256]{2,1,0:T(8,128)(2,1)S(1)}, u32[]{:S(2)}, u32[]{:S(2)}) collective-permute-start(bf16[2,80,256]{2,1,0:T(8,128)(2,1)S(1)} %get-tuple-element.67), channel_id=1, source_target_pairs={{0,8},{4,12},{8,0},{12,4},{16,24},{20,28},{24,16},{28,20},{1,9},{5... | collective-permute-start | bytes 245768 | tf_op jit(solution)/shard_map/ppermute | solution.py:560
  31.2 1.5 %collective-permute-start.7 = (bf16[2,80,256]{2,1,0:T(8,128)(2,1)S(1)}, bf16[2,80,256]{2,1,0:T(8,128)(2,1)S(1)}, u32[]{:S(2)}, u32[]{:S(2)}) collective-permute-start(bf16[2,80,256]{2,1,0:T(8,128)(2,1)S(1)} %get-tuple-element.68), channel_id=1, source_target_pairs={{0,16},{4,20},{8,24},{12,28},{16,0},{20,4},{24,8},{28,12},{1,17},{... | collective-permute-start | bytes 245768 | tf_op jit(solution)/shard_map/ppermute | solution.py:560
  32.7 0.9 %collective-permute-start.8 = (bf16[2,80,256]{2,1,0:T(8,128)(2,1)S(1)}, bf16[2,80,256]{2,1,0:T(8,128)(2,1)S(1)}, u32[]{:S(2)}, u32[]{:S(2)}) collective-permute-start(bf16[2,80,256]{2,1,0:T(8,128)(2,1)S(1)} %get-tuple-element.69), channel_id=1, source_target_pairs={{0,24},{4,28},{8,16},{12,20},{16,8},{20,12},{24,0},{28,4},{1,25},{... | collective-permute-start | bytes 245768 | tf_op jit(solution)/shard_map/ppermute | solution.py:560
  33.6 0.5 collective-permute-done.4.refs_2_
  34.1 1.4 %copy-done = bf16[640,1280]{1,0:T(8,128)(2,1)S(1)} copy-done((bf16[640,1280]{1,0:T(8,128)(2,1)S(1)}, bf16[640,1280]{1,0:T(8,128)(2,1)}, u32[]{:S(2)}) %copy-start) | copy-done | bytes 1638424
  35.5 1.6 %shard_map.114 = (bf16[8,80,256]{2,1,0:T(8,128)(2,1)}, bf16[64,2560]{1,0:T(8,128)(2,1)S(1)}, bf16[160,256]{1,0:T(8,128)(2,1)S(1)}, bf16[160,256]{1,0:T(8,128)(2,...) custom-call(bf16[640,1280]{1,0:T(8,128)(2,1)S(1)} %copy-done, ...), custom_call_target="tpu_custom_call" | custom-call | flops 805000000 | tf_op jit(solution)/shard_map/pallas_call | solution.py:120
  37.1 4.1 %all-to-all-start.1 = ((bf16[8,80,256]{2,1,0:T(8,128)(2,1)}), bf16[8,80,256]{2,1,0:T(8,128)(2,1)S(1)}, u32[]{:S(2)}, u32[]{:S(2)}) async-start(bf16[8,80,256]{2,1,0:T(8,128)(2,1)} %get-tuple-element.64), calls=%async_computation.1 | async-start | bytes 655360 | tf_op jit(solution)/shard_map/all_to_all | solution.py:592
  41.3 0.6 collective-permute-start.9
  43.8 1.1 %shard_map.116 = (bf16[160,640]{1,0:T(8,128)(2,1)S(1)}, bf16[160,640]{1,0:T(8,128)(2,1)S(1)}, bf16[160,640]{1,0:T(8,128)(2,1)S(1)}, bf16[160,640]{1,0:T(8,128)(2,1)S(1)}) custom-call(bf16[64,2560]{1,0:T(8,128)(2,1)S(1)} %get-tuple-element.65.keep_ref, bf16[2,80,256]{2,1,0:T(8,128)(2,1)S(1)} %get-tuple-element.66.refs_0_, ...), custom_call_target="tpu_custom_call" | custom-call | flops 230000000 | tf_op jit(solution)/shard_map/pallas_call | solution.py:497
  44.9 1.8 %collective-permute-start.13 = (bf16[160,640]{1,0:T(8,128)(2,1)S(1)}, bf16[160,640]{1,0:T(8,128)(2,1)S(1)}, u32[]{:S(2)}, u32[]{:S(2)}) collective-permute-start(bf16[160,640]{1,0:T(8,128)(2,1)S(1)} %get-tuple-element.79), channel_id=1, source_target_pairs={{0,8},{4,12},{8,0},{12,4},{16,24},{20,28},{24,16},{28,20},{1,9},{5... | collective-permute-start | bytes 614408 | tf_op jit(solution)/shard_map/ppermute | solution.py:560
  46.7 1.5 %collective-permute-start.14 = (bf16[160,640]{1,0:T(8,128)(2,1)S(1)}, bf16[160,640]{1,0:T(8,128)(2,1)S(1)}, u32[]{:S(2)}, u32[]{:S(2)}) collective-permute-start(bf16[160,640]{1,0:T(8,128)(2,1)S(1)} %get-tuple-element.80), channel_id=1, source_target_pairs={{0,16},{4,20},{8,24},{12,28},{16,0},{20,4},{24,8},{28,12},{1,17},{... | collective-permute-start | bytes 614408 | tf_op jit(solution)/shard_map/ppermute | solution.py:560
  48.9 9.9 %shard_map.117 = bf16[8,240,256]{2,1,0:T(8,128)(2,1)} custom-call(bf16[8,256,256]{2,1,0:T(8,128)(2,1)S(1)} %all-to-all-done.all_ref, bf16[8,80,256]{2,1,0:T(8,128)(2,1)S(1)} %all-to-all-done.1.grads_ref, bf16[8,80,256]{2,1,0:T(8,128)(2,1)S(1)} %get-tuple-element.83.context_ref, f32[8,1,256]{2,1,0:T(1,128)S(1)} %get-tuple-element.84.log_ref), custom_call_target="tpu_custom_call" | custom-call | flops 12650000384 | tf_op jit(solution)/shard_map/pallas_call | solution.py:373
  58.8 3.6 %all-to-all-start.2 = ((bf16[8,240,256]{2,1,0:T(8,128)(2,1)}), bf16[8,240,256]{2,1,0:T(8,128)(2,1)S(1)}, u32[]{:S(2)}, u32[]{:S(2)}) async-start(bf16[8,240,256]{2,1,0:T(8,128)(2,1)} %shard_map.117), calls=%async_computation.2 | async-start | bytes 1966080 | tf_op jit(solution)/shard_map/all_to_all | solution.py:597
  62.7 2.5 %collective-permute-start.16 = (bf16[160,160]{1,0:T(8,128)(2,1)S(1)}, bf16[160,160]{1,0:T(8,128)(2,1)S(1)}, u32[]{:S(2)}, u32[]{:S(2)}) collective-permute-start(bf16[160,160]{1,0:T(8,128)(2,1)S(1)} %get-tuple-element.93), channel_id=1, source_target_pairs={{0,1},{1,0},{2,3},{3,2},{4,5},{5,4},{6,7},{7,6},{8,9},{9,8},{10,11... | collective-permute-start | bytes 153608 | tf_op jit(solution)/shard_map/ppermute | solution.py:560
  65.2 0.5 collective-permute-start.17
  65.7 1.9 %collective-permute-start.18 = (bf16[160,160]{1,0:T(8,128)(2,1)S(1)}, bf16[160,160]{1,0:T(8,128)(2,1)S(1)}, u32[]{:S(2)}, u32[]{:S(2)}) collective-permute-start(bf16[160,160]{1,0:T(8,128)(2,1)S(1)} %get-tuple-element.95), channel_id=1, source_target_pairs={{0,3},{1,2},{2,1},{3,0},{4,7},{5,6},{6,5},{7,4},{8,11},{9,10},{10,... | collective-permute-start | bytes 153608 | tf_op jit(solution)/shard_map/ppermute | solution.py:560
  67.7 0.6 collective-permute-done.16.refs_1_
  68.3 6.3 %collective-permute-done.17.refs_2_ = bf16[160,160]{1,0:T(8,128)(2,1)S(1)} collective-permute-done((bf16[160,160]{1,0:T(8,128)(2,1)S(1)}, bf16[160,160]{1,0:T(8,128)(2,1)S(1)}, u32[]{:S(2)}, u32[]{:S(2)}) %collective-permute-start.17) | collective-permute-done | bytes 51232 | tf_op jit(solution)/shard_map/ppermute | solution.py:560
  74.5 0.7 shard_map.120
  75.2 1.8 %all-to-all-done.2.all_ref = bf16[8,240,256]{2,1,0:T(8,128)(2,1)S(1)} async-done(((bf16[8,240,256]{2,1,0:T(8,128)(2,1)}), bf16[8,240,256]{2,1,0:T(8,128)(2,1)S(1)}, u32[]{:S(2)}, u32[]{:S(2)}) %all-to-all-start.2) | async-done | bytes 983072 | tf_op jit(solution)/shard_map/all_to_all | solution.py:597
  77.0 1.1 %shard_map.118 = (bf16[256,640]{1,0:T(8,128)(2,1)}, bf16[256,640]{1,0:T(8,128)(2,1)}, bf16[256,640]{1,0:T(8,128)(2,1)}) custom-call(bf16[8,240,256]{2,1,0:T(8,128)(2,1)S(1)} %all-to-all-done.2.all_ref), custom_call_target="tpu_custom_call" | custom-call | flops 1264999936 | tf_op jit(solution)/shard_map/pallas_call | solution.py:413
  (28 shorter events, 3.3 us)
Async XLA Ops:
  4.4 5.3 %copy-start.2 = (s32[1,64]{1,0:T(1,128)S(1)}, s32[1,64]{1,0:T(1,128)}, u32[]{:S(2)}) copy-start(s32[1,64]{1,0:T(1,128)} %refs_0_.1) | copy-start | bytes 772
  4.4 14.9 %copy-start.1 = (bf16[64,5120]{1,0:T(8,128)(2,1)S(1)}, bf16[64,5120]{1,0:T(8,128)(2,1)}, u32[]{:S(2)}) copy-start(bf16[64,5120]{1,0:T(8,128)(2,1)} %grad_ref.1) | copy-start | bytes 1966084
  4.4 20.7 %all-to-all-start = ((bf16[8,256,256]{2,1,0:T(8,128)(2,1)}), bf16[8,256,256]{2,1,0:T(8,128)(2,1)S(1)}, u32[]{:S(2)}, u32[]{:S(2)}) async-start(bf16[8,256,256]{2,1,0:T(8,128)(2,1)} %shard_map.111), calls=%async_computation | async-start | bytes 2097152 | tf_op jit(solution)/shard_map/all_to_all | solution.py:582
  9.7 4.5 %collective-permute-start.1 = (s32[1,64]{1,0:T(1,128)S(1)}, s32[1,64]{1,0:T(1,128)S(1)}, u32[]{:S(2)}, u32[]{:S(2)}) collective-permute-start(s32[1,64]{1,0:T(1,128)S(1)} %copy-done.2), channel_id=1, source_target_pairs={{0,2},{1,3},{2,0},{3,1},{4,6},{5,7},{6,4},{7,5},{8,10},{9,11},{10,... | collective-permute-start | bytes 776 | tf_op jit(solution)/shard_map/ppermute | solution.py:560
  12.4 3.5 %collective-permute-start = (s32[1,64]{1,0:T(1,128)S(1)}, s32[1,64]{1,0:T(1,128)S(1)}, u32[]{:S(2)}, u32[]{:S(2)}) collective-permute-start(s32[1,64]{1,0:T(1,128)S(1)} %copy-done.2), channel_id=1, source_target_pairs={{0,1},{1,0},{2,3},{3,2},{4,5},{5,4},{6,7},{7,6},{8,9},{9,8},{10,11... | collective-permute-start | bytes 776 | tf_op jit(solution)/shard_map/ppermute | solution.py:560
  14.0 5.3 %collective-permute-start.2 = (s32[1,64]{1,0:T(1,128)S(1)}, s32[1,64]{1,0:T(1,128)S(1)}, u32[]{:S(2)}, u32[]{:S(2)}) collective-permute-start(s32[1,64]{1,0:T(1,128)S(1)} %copy-done.2), channel_id=1, source_target_pairs={{0,3},{1,2},{2,1},{3,0},{4,7},{5,6},{6,5},{7,4},{8,11},{9,10},{10,... | collective-permute-start | bytes 776 | tf_op jit(solution)/shard_map/ppermute | solution.py:560
  19.8 10.2 %collective-permute-start.3 = (bf16[16,5120]{1,0:T(8,128)(2,1)S(1)}, bf16[16,5120]{1,0:T(8,128)(2,1)S(1)}, u32[]{:S(2)}, u32[]{:S(2)}) collective-permute-start(bf16[16,5120]{1,0:T(8,128)(2,1)S(1)} %get-tuple-element.51), channel_id=1, source_target_pairs={{0,1},{1,0},{2,3},{3,2},{4,5},{5,4},{6,7},{7,6},{8,9},{9,8},{10,11... | collective-permute-start | bytes 491528 | tf_op jit(solution)/shard_map/ppermute | solution.py:560
  19.9 14.2 %collective-permute-start.4 = (bf16[16,5120]{1,0:T(8,128)(2,1)S(1)}, bf16[16,5120]{1,0:T(8,128)(2,1)S(1)}, u32[]{:S(2)}, u32[]{:S(2)}) collective-permute-start(bf16[16,5120]{1,0:T(8,128)(2,1)S(1)} %get-tuple-element.57), channel_id=1, source_target_pairs={{0,2},{1,3},{2,0},{3,1},{4,6},{5,7},{6,4},{7,5},{8,10},{9,11},{10,... | collective-permute-start | bytes 491528 | tf_op jit(solution)/shard_map/ppermute | solution.py:560
  20.7 13.4 %collective-permute-start.5 = (bf16[16,5120]{1,0:T(8,128)(2,1)S(1)}, bf16[16,5120]{1,0:T(8,128)(2,1)S(1)}, u32[]{:S(2)}, u32[]{:S(2)}) collective-permute-start(bf16[16,5120]{1,0:T(8,128)(2,1)S(1)} %get-tuple-element.58), channel_id=1, source_target_pairs={{0,3},{1,2},{2,1},{3,0},{4,7},{5,6},{6,5},{7,4},{8,11},{9,10},{10,... | collective-permute-start | bytes 491528 | tf_op jit(solution)/shard_map/ppermute | solution.py:560
  30.1 11.2 %collective-permute-start.6 = (bf16[2,80,256]{2,1,0:T(8,128)(2,1)S(1)}, bf16[2,80,256]{2,1,0:T(8,128)(2,1)S(1)}, u32[]{:S(2)}, u32[]{:S(2)}) collective-permute-start(bf16[2,80,256]{2,1,0:T(8,128)(2,1)S(1)} %get-tuple-element.67), channel_id=1, source_target_pairs={{0,8},{4,12},{8,0},{12,4},{16,24},{20,28},{24,16},{28,20},{1,9},{5... | collective-permute-start | bytes 245768 | tf_op jit(solution)/shard_map/ppermute | solution.py:560
  31.2 10.0 %collective-permute-start.7 = (bf16[2,80,256]{2,1,0:T(8,128)(2,1)S(1)}, bf16[2,80,256]{2,1,0:T(8,128)(2,1)S(1)}, u32[]{:S(2)}, u32[]{:S(2)}) collective-permute-start(bf16[2,80,256]{2,1,0:T(8,128)(2,1)S(1)} %get-tuple-element.68), channel_id=1, source_target_pairs={{0,16},{4,20},{8,24},{12,28},{16,0},{20,4},{24,8},{28,12},{1,17},{... | collective-permute-start | bytes 245768 | tf_op jit(solution)/shard_map/ppermute | solution.py:560
  32.7 8.5 %collective-permute-start.8 = (bf16[2,80,256]{2,1,0:T(8,128)(2,1)S(1)}, bf16[2,80,256]{2,1,0:T(8,128)(2,1)S(1)}, u32[]{:S(2)}, u32[]{:S(2)}) collective-permute-start(bf16[2,80,256]{2,1,0:T(8,128)(2,1)S(1)} %get-tuple-element.69), channel_id=1, source_target_pairs={{0,24},{4,28},{8,16},{12,20},{16,8},{20,12},{24,0},{28,4},{1,25},{... | collective-permute-start | bytes 245768 | tf_op jit(solution)/shard_map/ppermute | solution.py:560
  34.1 1.4 %copy-start = (bf16[640,1280]{1,0:T(8,128)(2,1)S(1)}, bf16[640,1280]{1,0:T(8,128)(2,1)}, u32[]{:S(2)}) copy-start(bf16[640,1280]{1,0:T(8,128)(2,1)} %weight_ref.1) | copy-start | bytes 4915204
  37.1 11.8 %all-to-all-start.1 = ((bf16[8,80,256]{2,1,0:T(8,128)(2,1)}), bf16[8,80,256]{2,1,0:T(8,128)(2,1)S(1)}, u32[]{:S(2)}, u32[]{:S(2)}) async-start(bf16[8,80,256]{2,1,0:T(8,128)(2,1)} %get-tuple-element.64), calls=%async_computation.1 | async-start | bytes 655360 | tf_op jit(solution)/shard_map/all_to_all | solution.py:592
  41.3 1.6 %collective-permute-start.9 = (bf16[320,256]{1,0:T(8,128)(2,1)S(1)}, bf16[320,256]{1,0:T(8,128)(2,1)S(1)}, u32[]{:S(2)}, u32[]{:S(2)}) collective-permute-start(bf16[320,256]{1,0:T(8,128)(2,1)S(1)} %get-tuple-element.74), channel_id=1, source_target_pairs={{0,4},{4,0},{8,12},{12,8},{16,20},{20,16},{24,28},{28,24},{1,5},{5... | collective-permute-start | bytes 491528 | tf_op jit(solution)/shard_map/ppermute | solution.py:560
  41.9 1.4 %collective-permute-start.10 = (bf16[320,256]{1,0:T(8,128)(2,1)S(1)}, bf16[320,256]{1,0:T(8,128)(2,1)S(1)}, u32[]{:S(2)}, u32[]{:S(2)}) collective-permute-start(bf16[320,256]{1,0:T(8,128)(2,1)S(1)} %get-tuple-element.75), channel_id=1, source_target_pairs={{0,4},{4,0},{8,12},{12,8},{16,20},{20,16},{24,28},{28,24},{1,5},{5... | collective-permute-start | bytes 491528 | tf_op jit(solution)/shard_map/ppermute | solution.py:560
  42.0 1.6 %collective-permute-start.11 = (bf16[320,256]{1,0:T(8,128)(2,1)S(1)}, bf16[320,256]{1,0:T(8,128)(2,1)S(1)}, u32[]{:S(2)}, u32[]{:S(2)}) collective-permute-start(bf16[320,256]{1,0:T(8,128)(2,1)S(1)} %get-tuple-element.76), channel_id=1, source_target_pairs={{0,4},{4,0},{8,12},{12,8},{16,20},{20,16},{24,28},{28,24},{1,5},{5... | collective-permute-start | bytes 491528 | tf_op jit(solution)/shard_map/ppermute | solution.py:560
  42.4 1.4 %collective-permute-start.12 = (bf16[320,256]{1,0:T(8,128)(2,1)S(1)}, bf16[320,256]{1,0:T(8,128)(2,1)S(1)}, u32[]{:S(2)}, u32[]{:S(2)}) collective-permute-start(bf16[320,256]{1,0:T(8,128)(2,1)S(1)} %get-tuple-element.77), channel_id=1, source_target_pairs={{0,4},{4,0},{8,12},{12,8},{16,20},{20,16},{24,28},{28,24},{1,5},{5... | collective-permute-start | bytes 491528 | tf_op jit(solution)/shard_map/ppermute | solution.py:560
  44.9 17.5 %collective-permute-start.13 = (bf16[160,640]{1,0:T(8,128)(2,1)S(1)}, bf16[160,640]{1,0:T(8,128)(2,1)S(1)}, u32[]{:S(2)}, u32[]{:S(2)}) collective-permute-start(bf16[160,640]{1,0:T(8,128)(2,1)S(1)} %get-tuple-element.79), channel_id=1, source_target_pairs={{0,8},{4,12},{8,0},{12,4},{16,24},{20,28},{24,16},{28,20},{1,9},{5... | collective-permute-start | bytes 614408 | tf_op jit(solution)/shard_map/ppermute | solution.py:560
  46.7 15.7 %collective-permute-start.14 = (bf16[160,640]{1,0:T(8,128)(2,1)S(1)}, bf16[160,640]{1,0:T(8,128)(2,1)S(1)}, u32[]{:S(2)}, u32[]{:S(2)}) collective-permute-start(bf16[160,640]{1,0:T(8,128)(2,1)S(1)} %get-tuple-element.80), channel_id=1, source_target_pairs={{0,16},{4,20},{8,24},{12,28},{16,0},{20,4},{24,8},{28,12},{1,17},{... | collective-permute-start | bytes 614408 | tf_op jit(solution)/shard_map/ppermute | solution.py:560
  48.2 14.2 %collective-permute-start.15 = (bf16[160,640]{1,0:T(8,128)(2,1)S(1)}, bf16[160,640]{1,0:T(8,128)(2,1)S(1)}, u32[]{:S(2)}, u32[]{:S(2)}) collective-permute-start(bf16[160,640]{1,0:T(8,128)(2,1)S(1)} %get-tuple-element.81), channel_id=1, source_target_pairs={{0,24},{4,28},{8,16},{12,20},{16,8},{20,12},{24,0},{28,4},{1,25},{... | collective-permute-start | bytes 614408 | tf_op jit(solution)/shard_map/ppermute | solution.py:560
  58.8 18.2 %all-to-all-start.2 = ((bf16[8,240,256]{2,1,0:T(8,128)(2,1)}), bf16[8,240,256]{2,1,0:T(8,128)(2,1)S(1)}, u32[]{:S(2)}, u32[]{:S(2)}) async-start(bf16[8,240,256]{2,1,0:T(8,128)(2,1)} %shard_map.117), calls=%async_computation.2 | async-start | bytes 1966080 | tf_op jit(solution)/shard_map/all_to_all | solution.py:597
  62.7 5.6 %collective-permute-start.16 = (bf16[160,160]{1,0:T(8,128)(2,1)S(1)}, bf16[160,160]{1,0:T(8,128)(2,1)S(1)}, u32[]{:S(2)}, u32[]{:S(2)}) collective-permute-start(bf16[160,160]{1,0:T(8,128)(2,1)S(1)} %get-tuple-element.93), channel_id=1, source_target_pairs={{0,1},{1,0},{2,3},{3,2},{4,5},{5,4},{6,7},{7,6},{8,9},{9,8},{10,11... | collective-permute-start | bytes 153608 | tf_op jit(solution)/shard_map/ppermute | solution.py:560
  65.2 9.3 %collective-permute-start.17 = (bf16[160,160]{1,0:T(8,128)(2,1)S(1)}, bf16[160,160]{1,0:T(8,128)(2,1)S(1)}, u32[]{:S(2)}, u32[]{:S(2)}) collective-permute-start(bf16[160,160]{1,0:T(8,128)(2,1)S(1)} %get-tuple-element.94), channel_id=1, source_target_pairs={{0,2},{1,3},{2,0},{3,1},{4,6},{5,7},{6,4},{7,5},{8,10},{9,11},{10,... | collective-permute-start | bytes 153608 | tf_op jit(solution)/shard_map/ppermute | solution.py:560
  65.7 8.8 %collective-permute-start.18 = (bf16[160,160]{1,0:T(8,128)(2,1)S(1)}, bf16[160,160]{1,0:T(8,128)(2,1)S(1)}, u32[]{:S(2)}, u32[]{:S(2)}) collective-permute-start(bf16[160,160]{1,0:T(8,128)(2,1)S(1)} %get-tuple-element.95), channel_id=1, source_target_pairs={{0,3},{1,2},{2,1},{3,0},{4,7},{5,6},{6,5},{7,4},{8,11},{9,10},{10,... | collective-permute-start | bytes 153608 | tf_op jit(solution)/shard_map/ppermute | solution.py:560

commit v6 on v5

--- a/solution.py
+++ b/solution.py
@@ -39,30 +39,54 @@
     return lax.dot_general(left, right, (((0,), (0,)), ((), ())), preferred_element_type=F32)
 
 
-def pack_kernel(start_ref, size_ref, query_ref, key_ref, value_ref, out_ref, *, groups):
+def pack_kernel(
+    start_ref, query_ref, key_ref, value_ref, out_ref, came, made, page, arrived, left,
+    *, groups
+):
     rows, width = query_ref.shape
     feat = width // groups
-    for slot, ref in enumerate((query_ref, key_ref, value_ref)):
-        turned = ref[...].T
+    arriving = [
+        pltpu.make_async_copy(ref, came.at[slot], arrived.at[slot])
+        for slot, ref in enumerate((query_ref, key_ref, value_ref))
+    ]
+    for copy in arriving:
+        copy.start()
+    info = jnp.broadcast_to(start_ref[...], (INFO, rows)).astype(F32).astype(BF16)
+    for g in range(groups):
+        page[g] = info
+    leaving = [pltpu.make_async_copy(page, out_ref.at[:, 3 * feat :, :], left.at[3])]
+    leaving[0].start()
+    for slot, copy in enumerate(arriving):
+        copy.wait()
+        turned = came[slot].T
         for g in range(groups):
-            out_ref[g, slot * feat : (slot + 1) * feat, :] = turned[g * feat : (g + 1) * feat, :]
-    line = lax.broadcasted_iota(jnp.int32, (INFO, rows), 0)
-    page = jnp.where(line < INFO // 2, start_ref[...], size_ref[...])
-    info = page.astype(F32).astype(BF16)
-    for g in range(groups):
-        out_ref[g, 3 * feat :, :] = info
-
-
-def pack(page_start, page_size, query, key, value, groups):
+            made[slot, g] = turned[g * feat : (g + 1) * feat, :]
+        lines = slice(slot * feat, (slot + 1) * feat)
+        leaving.append(pltpu.make_async_copy(made.at[slot], out_ref.at[:, lines, :], left.at[slot]))
+        leaving[-1].start()
+    for copy in leaving:
+        copy.wait()
+
+
+def pack(page_start, query, key, value, groups):
     rows, width = query.shape
+    feat = width // groups
+    anywhere = pl.BlockSpec(memory_space=pl.ANY)
     return pl.pallas_call(
         functools.partial(pack_kernel, groups=groups),
-        out_shape=jax.ShapeDtypeStruct((groups, 3 * (width // groups) + INFO, rows), BF16),
-        in_specs=[VMEM] * 5,
-        out_specs=VMEM,
+        out_shape=jax.ShapeDtypeStruct((groups, 3 * feat + INFO, rows), BF16),
+        in_specs=[VMEM] + [anywhere] * 3,
+        out_specs=anywhere,
+        scratch_shapes=[
+            pltpu.VMEM((3, rows, width), BF16),
+            pltpu.VMEM((3, groups, feat, rows), BF16),
+            pltpu.VMEM((groups, INFO, rows), BF16),
+            pltpu.SemaphoreType.DMA((3,)),
+            pltpu.SemaphoreType.DMA((4,)),
+        ],
         cost_estimate=cost(2.6),
         compiler_params=WHOLE,
-    )(page_start, page_size, query, key, value)
+    )(page_start, query, key, value)
 
 
 def project_kernel(weight_ref, *refs, groups, lanes, chips, cores):
@@ -176,10 +200,9 @@
 
 
 def hidden_row(ref, block, key_block, feat):
-    info = ref[block, 3 * feat : 3 * feat + INFO, :].astype(F32)
-    first = info[0:1, :]
-    count = info[INFO // 2 : INFO // 2 + 1, :]
-    return jnp.where((first <= key_block) & (first + count > key_block), 0.0, HIDE)
+    first = ref[block, 3 * feat : 3 * feat + INFO, :].astype(F32)[0:1, :]
+    key_first = ref[key_block, 3 * feat : 3 * feat + INFO, :].astype(F32)[0:1, :]
+    return jnp.where(first == key_first, 0.0, HIDE)
 
 
 def shared_block(index, shares):
@@ -203,10 +226,8 @@
     count = blocks // shares
     feat = heads * HD
     for index in range(count):
-        info = all_ref[shared_block(index, shares), 3 * feat : 3 * feat + INFO, :].astype(F32)
-        begin, size = info[0:1, :], info[INFO // 2 : INFO // 2 + 1, :]
         for j in range(blocks):
-            hides[index, j : j + 1, :] = jnp.where((begin <= j) & (begin + size > j), 0.0, HIDE)
+            hides[index, j : j + 1, :] = hidden_row(all_ref, shared_block(index, shares), j, feat)
     for h in range(heads):
         own = slice(h * HD, (h + 1) * HD)
         value_own = slice(2 * feat + h * HD, 2 * feat + (h + 1) * HD)
@@ -576,7 +597,7 @@
     after = lax.optimization_barrier
 
     asked = swap_all([row_source] * lanes, "dp", lanes)
-    packed = pack(page_start, page_size, saved_query[0], saved_key[0], saved_value[0], groups)
+    packed = pack(page_start, saved_query[0], saved_key[0], saved_value[0], groups)
     if shares > 1:
         packed = jnp.repeat(packed, shares, axis=0)
     gathered = lax.all_to_all(packed, "blk", split_axis=0, concat_axis=0, tiled=True)

time: 78.5 us -> 77.6 us (0.989)
  transfers between devices with their start and end apart: 22 -> 22, of which waited for: 13 -> 13; matrix products, arithmetic and copies ran while one was open for 0% -> 0% of each run, Pallas kernels for 24% -> 25%
where the time goes in v6:
time: 77.6 us; the launch traced here: 77.2 us
  starting transfers between devices  35.1 us (45%)
  Pallas kernels  22.3 us (29%)
  waiting for transfers between devices  16.9 us (22%)
  local copies, waits for them, and re-layouts  1.44 us (2%)
  between operations  1.43 us (2%)
    ppermute x19, starting transfers between devices, swap(): return lax.ppermute(array, axis, [(i, i ^ mask) for i in range(size)])  22.1 us
    ppermute x19, waiting for transfers between devices, swap(): return lax.ppermute(array, axis, [(i, i ^ mask) for i in range(size)])  13.8 us
    pallas_call x1, Pallas kernels, backward(): pl.pallas_call(functools.partial(backward_kernel, heads=heads, shares=sha...  9.92 us
    all_to_all x1, starting transfers between devices, body(): lax.all_to_all(packed, 'blk', split_axis=0, concat_axis=0, tiled=True)  5.31 us
    pallas_call x1, Pallas kernels, forward(): pl.pallas_call(functools.partial(forward_kernel, heads=heads, shares=shar...  4.88 us
    all_to_all x1, starting transfers between devices, body(): lax.all_to_all(grads, 'blk', split_axis=0, concat_axis=0, tiled=True)  4.13 us
    all_to_all x1, starting transfers between devices, body(): lax.all_to_all(results, 'blk', split_axis=0, concat_axis=0, tiled=True)  3.55 us
    pallas_call x1, Pallas kernels, pack(): pl.pallas_call(functools.partial(pack_kernel, groups=groups), out_shape=j...  2.22 us
  transfers between devices with their start and end apart: 22, of which 13 were waited for; matrix products, arithmetic and copies ran while one was open for 0% of the time, Pallas kernels for 25%

profile of v6, /device:TPU:0, one launch (start us, length us, event | category | flops | bytes accessed | tf_op | source)
XLA Modules:
  0.0 77.2 jit_solution(17082378065330219922)
XLA Ops:
  1.3 2.2 %shard_map.102 = bf16[8,256,256]{2,1,0:T(8,128)(2,1)} custom-call(s32[1,1]{1,0:T(1,128)S(6)} %copy.11.start_ref, bf16[256,640]{1,0:T(8,128)(2,1)} %bitcast.6, bf16[256,640]{1,0:T(8,128)(2,1)} %bitcast.7, bf16[256,640]{1,0:T(8,128)(2,1)} %bitcast.8), custom_call_target="tpu_custom_call" | custom-call | flops 2990000128 | tf_op jit(solution)/shard_map/pallas_call | solution.py:75
  3.5 5.3 %all-to-all-start = ((bf16[8,256,256]{2,1,0:T(8,128)(2,1)}), bf16[8,256,256]{2,1,0:T(8,128)(2,1)S(1)}, u32[]{:S(2)}, u32[]{:S(2)}) async-start(bf16[8,256,256]{2,1,0:T(8,128)(2,1)} %shard_map.102), calls=%async_computation | async-start | bytes 2097152 | tf_op jit(solution)/shard_map/all_to_all | solution.py:603
  8.8 2.7 %collective-permute-start.1 = (s32[1,64]{1,0:T(1,128)S(1)}, s32[1,64]{1,0:T(1,128)S(1)}, u32[]{:S(2)}, u32[]{:S(2)}) collective-permute-start(s32[1,64]{1,0:T(1,128)S(1)} %copy-done.2), channel_id=1, source_target_pairs={{0,2},{1,3},{2,0},{3,1},{4,6},{5,7},{6,4},{7,5},{8,10},{9,11},{10,... | collective-permute-start | bytes 776 | tf_op jit(solution)/shard_map/ppermute | solution.py:581
  11.5 1.6 %collective-permute-start = (s32[1,64]{1,0:T(1,128)S(1)}, s32[1,64]{1,0:T(1,128)S(1)}, u32[]{:S(2)}, u32[]{:S(2)}) collective-permute-start(s32[1,64]{1,0:T(1,128)S(1)} %copy-done.2), channel_id=1, source_target_pairs={{0,1},{1,0},{2,3},{3,2},{4,5},{5,4},{6,7},{7,6},{8,9},{9,8},{10,11... | collective-permute-start | bytes 776 | tf_op jit(solution)/shard_map/ppermute | solution.py:581
  13.4 1.7 %collective-permute-done.refs_1_ = s32[1,64]{1,0:T(1,128)S(1)} collective-permute-done((s32[1,64]{1,0:T(1,128)S(1)}, s32[1,64]{1,0:T(1,128)S(1)}, u32[]{:S(2)}, u32[]{:S(2)}) %collective-permute-start) | collective-permute-done | bytes 288 | tf_op jit(solution)/shard_map/ppermute | solution.py:581
  15.0 3.4 %collective-permute-done.2.refs_3_ = s32[1,64]{1,0:T(1,128)S(1)} collective-permute-done((s32[1,64]{1,0:T(1,128)S(1)}, s32[1,64]{1,0:T(1,128)S(1)}, u32[]{:S(2)}, u32[]{:S(2)}) %collective-permute-start.2) | collective-permute-done | bytes 288 | tf_op jit(solution)/shard_map/ppermute | solution.py:581
  18.4 0.5 shard_map.103
  19.0 0.8 collective-permute-start.4
  19.8 3.6 %collective-permute-start.5 = (bf16[16,5120]{1,0:T(8,128)(2,1)S(1)}, bf16[16,5120]{1,0:T(8,128)(2,1)S(1)}, u32[]{:S(2)}, u32[]{:S(2)}) collective-permute-start(bf16[16,5120]{1,0:T(8,128)(2,1)S(1)} %get-tuple-element.58), channel_id=1, source_target_pairs={{0,3},{1,2},{2,1},{3,0},{4,7},{5,6},{6,5},{7,4},{8,11},{9,10},{10,... | collective-permute-start | bytes 491528 | tf_op jit(solution)/shard_map/ppermute | solution.py:581
  23.4 0.9 %all-to-all-done.all_ref = bf16[8,256,256]{2,1,0:T(8,128)(2,1)S(1)} async-done(((bf16[8,256,256]{2,1,0:T(8,128)(2,1)}), bf16[8,256,256]{2,1,0:T(8,128)(2,1)S(1)}, u32[]{:S(2)}, u32[]{:S(2)}) %all-to-all-start) | async-done | bytes 1048608 | tf_op jit(solution)/shard_map/all_to_all | solution.py:603
  24.3 4.9 %shard_map.104 = (bf16[2,80,256]{2,1,0:T(8,128)(2,1)S(1)}, bf16[2,80,256]{2,1,0:T(8,128)(2,1)S(1)}, bf16[2,80,256]{2,1,0:T(8,128)(2,1)S(1)}, bf16[2,80,256]{2,1,...) custom-call(bf16[8,256,256]{2,1,0:T(8,128)(2,1)S(1)} %all-to-all-done.all_ref), custom_call_target="tpu_custom_call" | custom-call | flops 8049999872 | tf_op jit(solution)/shard_map/pallas_call | solution.py:303
  29.1 1.2 %collective-permute-start.6 = (bf16[2,80,256]{2,1,0:T(8,128)(2,1)S(1)}, bf16[2,80,256]{2,1,0:T(8,128)(2,1)S(1)}, u32[]{:S(2)}, u32[]{:S(2)}) collective-permute-start(bf16[2,80,256]{2,1,0:T(8,128)(2,1)S(1)} %get-tuple-element.67), channel_id=1, source_target_pairs={{0,8},{4,12},{8,0},{12,4},{16,24},{20,28},{24,16},{28,20},{1,9},{5... | collective-permute-start | bytes 245768 | tf_op jit(solution)/shard_map/ppermute | solution.py:581
  30.3 1.5 %collective-permute-start.7 = (bf16[2,80,256]{2,1,0:T(8,128)(2,1)S(1)}, bf16[2,80,256]{2,1,0:T(8,128)(2,1)S(1)}, u32[]{:S(2)}, u32[]{:S(2)}) collective-permute-start(bf16[2,80,256]{2,1,0:T(8,128)(2,1)S(1)} %get-tuple-element.68), channel_id=1, source_target_pairs={{0,16},{4,20},{8,24},{12,28},{16,0},{20,4},{24,8},{28,12},{1,17},{... | collective-permute-start | bytes 245768 | tf_op jit(solution)/shard_map/ppermute | solution.py:581
  31.8 0.9 %collective-permute-start.8 = (bf16[2,80,256]{2,1,0:T(8,128)(2,1)S(1)}, bf16[2,80,256]{2,1,0:T(8,128)(2,1)S(1)}, u32[]{:S(2)}, u32[]{:S(2)}) collective-permute-start(bf16[2,80,256]{2,1,0:T(8,128)(2,1)S(1)} %get-tuple-element.69), channel_id=1, source_target_pairs={{0,24},{4,28},{8,16},{12,20},{16,8},{20,12},{24,0},{28,4},{1,25},{... | collective-permute-start | bytes 245768 | tf_op jit(solution)/shard_map/ppermute | solution.py:581
  32.7 0.5 collective-permute-done.4.refs_2_
  33.2 1.4 %copy-done = bf16[640,1280]{1,0:T(8,128)(2,1)S(1)} copy-done((bf16[640,1280]{1,0:T(8,128)(2,1)S(1)}, bf16[640,1280]{1,0:T(8,128)(2,1)}, u32[]{:S(2)}) %copy-start) | copy-done | bytes 1638424
  34.7 1.6 %shard_map.105 = (bf16[8,80,256]{2,1,0:T(8,128)(2,1)}, bf16[64,2560]{1,0:T(8,128)(2,1)S(1)}, bf16[160,256]{1,0:T(8,128)(2,1)S(1)}, bf16[160,256]{1,0:T(8,128)(2,...) custom-call(bf16[640,1280]{1,0:T(8,128)(2,1)S(1)} %copy-done, ...), custom_call_target="tpu_custom_call" | custom-call | flops 805000000 | tf_op jit(solution)/shard_map/pallas_call | solution.py:144
  36.2 4.1 %all-to-all-start.1 = ((bf16[8,80,256]{2,1,0:T(8,128)(2,1)}), bf16[8,80,256]{2,1,0:T(8,128)(2,1)S(1)}, u32[]{:S(2)}, u32[]{:S(2)}) async-start(bf16[8,80,256]{2,1,0:T(8,128)(2,1)} %get-tuple-element.64), calls=%async_computation.1 | async-start | bytes 655360 | tf_op jit(solution)/shard_map/all_to_all | solution.py:613
  40.5 0.6 collective-permute-start.9
  41.6 0.4 collective-permute-done.9.refs_4_
  42.9 1.1 %shard_map.107 = (bf16[160,640]{1,0:T(8,128)(2,1)S(1)}, bf16[160,640]{1,0:T(8,128)(2,1)S(1)}, bf16[160,640]{1,0:T(8,128)(2,1)S(1)}, bf16[160,640]{1,0:T(8,128)(2,1)S(1)}) custom-call(bf16[64,2560]{1,0:T(8,128)(2,1)S(1)} %get-tuple-element.65.keep_ref, bf16[2,80,256]{2,1,0:T(8,128)(2,1)S(1)} %get-tuple-element.66.refs_0_, ...), custom_call_target="tpu_custom_call" | custom-call | flops 230000000 | tf_op jit(solution)/shard_map/pallas_call | solution.py:518
  44.0 1.8 %collective-permute-start.13 = (bf16[160,640]{1,0:T(8,128)(2,1)S(1)}, bf16[160,640]{1,0:T(8,128)(2,1)S(1)}, u32[]{:S(2)}, u32[]{:S(2)}) collective-permute-start(bf16[160,640]{1,0:T(8,128)(2,1)S(1)} %get-tuple-element.79), channel_id=1, source_target_pairs={{0,8},{4,12},{8,0},{12,4},{16,24},{20,28},{24,16},{28,20},{1,9},{5... | collective-permute-start | bytes 614408 | tf_op jit(solution)/shard_map/ppermute | solution.py:581
  45.8 1.5 %collective-permute-start.14 = (bf16[160,640]{1,0:T(8,128)(2,1)S(1)}, bf16[160,640]{1,0:T(8,128)(2,1)S(1)}, u32[]{:S(2)}, u32[]{:S(2)}) collective-permute-start(bf16[160,640]{1,0:T(8,128)(2,1)S(1)} %get-tuple-element.80), channel_id=1, source_target_pairs={{0,16},{4,20},{8,24},{12,28},{16,0},{20,4},{24,8},{28,12},{1,17},{... | collective-permute-start | bytes 614408 | tf_op jit(solution)/shard_map/ppermute | solution.py:581
  48.0 9.9 %shard_map.108 = bf16[8,240,256]{2,1,0:T(8,128)(2,1)} custom-call(bf16[8,256,256]{2,1,0:T(8,128)(2,1)S(1)} %all-to-all-done.all_ref, bf16[8,80,256]{2,1,0:T(8,128)(2,1)S(1)} %all-to-all-done.1.grads_ref, bf16[8,80,256]{2,1,0:T(8,128)(2,1)S(1)} %get-tuple-element.83.context_ref, f32[8,1,256]{2,1,0:T(1,128)S(1)} %get-tuple-element.84.log_ref), custom_call_target="tpu_custom_call" | custom-call | flops 12650000384 | tf_op jit(solution)/shard_map/pallas_call | solution.py:394
  57.9 3.6 %all-to-all-start.2 = ((bf16[8,240,256]{2,1,0:T(8,128)(2,1)}), bf16[8,240,256]{2,1,0:T(8,128)(2,1)S(1)}, u32[]{:S(2)}, u32[]{:S(2)}) async-start(bf16[8,240,256]{2,1,0:T(8,128)(2,1)} %shard_map.108), calls=%async_computation.2 | async-start | bytes 1966080 | tf_op jit(solution)/shard_map/all_to_all | solution.py:618
  61.8 2.5 %collective-permute-start.16 = (bf16[160,160]{1,0:T(8,128)(2,1)S(1)}, bf16[160,160]{1,0:T(8,128)(2,1)S(1)}, u32[]{:S(2)}, u32[]{:S(2)}) collective-permute-start(bf16[160,160]{1,0:T(8,128)(2,1)S(1)} %get-tuple-element.93), channel_id=1, source_target_pairs={{0,1},{1,0},{2,3},{3,2},{4,5},{5,4},{6,7},{7,6},{8,9},{9,8},{10,11... | collective-permute-start | bytes 153608 | tf_op jit(solution)/shard_map/ppermute | solution.py:581
  64.7 2.0 %collective-permute-start.18 = (bf16[160,160]{1,0:T(8,128)(2,1)S(1)}, bf16[160,160]{1,0:T(8,128)(2,1)S(1)}, u32[]{:S(2)}, u32[]{:S(2)}) collective-permute-start(bf16[160,160]{1,0:T(8,128)(2,1)S(1)} %get-tuple-element.95), channel_id=1, source_target_pairs={{0,3},{1,2},{2,1},{3,0},{4,7},{5,6},{6,5},{7,4},{8,11},{9,10},{10,... | collective-permute-start | bytes 153608 | tf_op jit(solution)/shard_map/ppermute | solution.py:581
  66.8 0.6 collective-permute-done.16.refs_1_
  67.4 6.3 %collective-permute-done.17.refs_2_ = bf16[160,160]{1,0:T(8,128)(2,1)S(1)} collective-permute-done((bf16[160,160]{1,0:T(8,128)(2,1)S(1)}, bf16[160,160]{1,0:T(8,128)(2,1)S(1)}, u32[]{:S(2)}, u32[]{:S(2)}) %collective-permute-start.17) | collective-permute-done | bytes 51232 | tf_op jit(solution)/shard_map/ppermute | solution.py:581
  73.6 0.7 shard_map.111
  74.3 1.8 %all-to-all-done.2.all_ref = bf16[8,240,256]{2,1,0:T(8,128)(2,1)S(1)} async-done(((bf16[8,240,256]{2,1,0:T(8,128)(2,1)}), bf16[8,240,256]{2,1,0:T(8,128)(2,1)S(1)}, u32[]{:S(2)}, u32[]{:S(2)}) %all-to-all-start.2) | async-done | bytes 983072 | tf_op jit(solution)/shard_map/all_to_all | solution.py:618
  76.1 1.1 %shard_map.109 = (bf16[256,640]{1,0:T(8,128)(2,1)}, bf16[256,640]{1,0:T(8,128)(2,1)}, bf16[256,640]{1,0:T(8,128)(2,1)}) custom-call(bf16[8,240,256]{2,1,0:T(8,128)(2,1)S(1)} %all-to-all-done.2.all_ref), custom_call_target="tpu_custom_call" | custom-call | flops 1264999936 | tf_op jit(solution)/shard_map/pallas_call | solution.py:434
  (28 shorter events, 3.3 us)
Async XLA Ops:
  3.5 5.3 %copy-start.2 = (s32[1,64]{1,0:T(1,128)S(1)}, s32[1,64]{1,0:T(1,128)}, u32[]{:S(2)}) copy-start(s32[1,64]{1,0:T(1,128)} %refs_0_.1) | copy-start | bytes 772
  3.5 14.9 %copy-start.1 = (bf16[64,5120]{1,0:T(8,128)(2,1)S(1)}, bf16[64,5120]{1,0:T(8,128)(2,1)}, u32[]{:S(2)}) copy-start(bf16[64,5120]{1,0:T(8,128)(2,1)} %grad_ref.1) | copy-start | bytes 1966084
  3.5 20.7 %all-to-all-start = ((bf16[8,256,256]{2,1,0:T(8,128)(2,1)}), bf16[8,256,256]{2,1,0:T(8,128)(2,1)S(1)}, u32[]{:S(2)}, u32[]{:S(2)}) async-start(bf16[8,256,256]{2,1,0:T(8,128)(2,1)} %shard_map.102), calls=%async_computation | async-start | bytes 2097152 | tf_op jit(solution)/shard_map/all_to_all | solution.py:603
  8.8 4.5 %collective-permute-start.1 = (s32[1,64]{1,0:T(1,128)S(1)}, s32[1,64]{1,0:T(1,128)S(1)}, u32[]{:S(2)}, u32[]{:S(2)}) collective-permute-start(s32[1,64]{1,0:T(1,128)S(1)} %copy-done.2), channel_id=1, source_target_pairs={{0,2},{1,3},{2,0},{3,1},{4,6},{5,7},{6,4},{7,5},{8,10},{9,11},{10,... | collective-permute-start | bytes 776 | tf_op jit(solution)/shard_map/ppermute | solution.py:581
  11.5 3.5 %collective-permute-start = (s32[1,64]{1,0:T(1,128)S(1)}, s32[1,64]{1,0:T(1,128)S(1)}, u32[]{:S(2)}, u32[]{:S(2)}) collective-permute-start(s32[1,64]{1,0:T(1,128)S(1)} %copy-done.2), channel_id=1, source_target_pairs={{0,1},{1,0},{2,3},{3,2},{4,5},{5,4},{6,7},{7,6},{8,9},{9,8},{10,11... | collective-permute-start | bytes 776 | tf_op jit(solution)/shard_map/ppermute | solution.py:581
  13.1 5.3 %collective-permute-start.2 = (s32[1,64]{1,0:T(1,128)S(1)}, s32[1,64]{1,0:T(1,128)S(1)}, u32[]{:S(2)}, u32[]{:S(2)}) collective-permute-start(s32[1,64]{1,0:T(1,128)S(1)} %copy-done.2), channel_id=1, source_target_pairs={{0,3},{1,2},{2,1},{3,0},{4,7},{5,6},{6,5},{7,4},{8,11},{9,10},{10,... | collective-permute-start | bytes 776 | tf_op jit(solution)/shard_map/ppermute | solution.py:581
  18.9 10.2 %collective-permute-start.3 = (bf16[16,5120]{1,0:T(8,128)(2,1)S(1)}, bf16[16,5120]{1,0:T(8,128)(2,1)S(1)}, u32[]{:S(2)}, u32[]{:S(2)}) collective-permute-start(bf16[16,5120]{1,0:T(8,128)(2,1)S(1)} %get-tuple-element.51), channel_id=1, source_target_pairs={{0,1},{1,0},{2,3},{3,2},{4,5},{5,4},{6,7},{7,6},{8,9},{9,8},{10,11... | collective-permute-start | bytes 491528 | tf_op jit(solution)/shard_map/ppermute | solution.py:581
  19.0 14.2 %collective-permute-start.4 = (bf16[16,5120]{1,0:T(8,128)(2,1)S(1)}, bf16[16,5120]{1,0:T(8,128)(2,1)S(1)}, u32[]{:S(2)}, u32[]{:S(2)}) collective-permute-start(bf16[16,5120]{1,0:T(8,128)(2,1)S(1)} %get-tuple-element.57), channel_id=1, source_target_pairs={{0,2},{1,3},{2,0},{3,1},{4,6},{5,7},{6,4},{7,5},{8,10},{9,11},{10,... | collective-permute-start | bytes 491528 | tf_op jit(solution)/shard_map/ppermute | solution.py:581
  19.8 13.4 %collective-permute-start.5 = (bf16[16,5120]{1,0:T(8,128)(2,1)S(1)}, bf16[16,5120]{1,0:T(8,128)(2,1)S(1)}, u32[]{:S(2)}, u32[]{:S(2)}) collective-permute-start(bf16[16,5120]{1,0:T(8,128)(2,1)S(1)} %get-tuple-element.58), channel_id=1, source_target_pairs={{0,3},{1,2},{2,1},{3,0},{4,7},{5,6},{6,5},{7,4},{8,11},{9,10},{10,... | collective-permute-start | bytes 491528 | tf_op jit(solution)/shard_map/ppermute | solution.py:581
  29.1 11.2 %collective-permute-start.6 = (bf16[2,80,256]{2,1,0:T(8,128)(2,1)S(1)}, bf16[2,80,256]{2,1,0:T(8,128)(2,1)S(1)}, u32[]{:S(2)}, u32[]{:S(2)}) collective-permute-start(bf16[2,80,256]{2,1,0:T(8,128)(2,1)S(1)} %get-tuple-element.67), channel_id=1, source_target_pairs={{0,8},{4,12},{8,0},{12,4},{16,24},{20,28},{24,16},{28,20},{1,9},{5... | collective-permute-start | bytes 245768 | tf_op jit(solution)/shard_map/ppermute | solution.py:581
  30.3 10.1 %collective-permute-start.7 = (bf16[2,80,256]{2,1,0:T(8,128)(2,1)S(1)}, bf16[2,80,256]{2,1,0:T(8,128)(2,1)S(1)}, u32[]{:S(2)}, u32[]{:S(2)}) collective-permute-start(bf16[2,80,256]{2,1,0:T(8,128)(2,1)S(1)} %get-tuple-element.68), channel_id=1, source_target_pairs={{0,16},{4,20},{8,24},{12,28},{16,0},{20,4},{24,8},{28,12},{1,17},{... | collective-permute-start | bytes 245768 | tf_op jit(solution)/shard_map/ppermute | solution.py:581
  31.8 8.6 %collective-permute-start.8 = (bf16[2,80,256]{2,1,0:T(8,128)(2,1)S(1)}, bf16[2,80,256]{2,1,0:T(8,128)(2,1)S(1)}, u32[]{:S(2)}, u32[]{:S(2)}) collective-permute-start(bf16[2,80,256]{2,1,0:T(8,128)(2,1)S(1)} %get-tuple-element.69), channel_id=1, source_target_pairs={{0,24},{4,28},{8,16},{12,20},{16,8},{20,12},{24,0},{28,4},{1,25},{... | collective-permute-start | bytes 245768 | tf_op jit(solution)/shard_map/ppermute | solution.py:581
  33.2 1.4 %copy-start = (bf16[640,1280]{1,0:T(8,128)(2,1)S(1)}, bf16[640,1280]{1,0:T(8,128)(2,1)}, u32[]{:S(2)}) copy-start(bf16[640,1280]{1,0:T(8,128)(2,1)} %weight_ref.1) | copy-start | bytes 4915204
  36.2 11.8 %all-to-all-start.1 = ((bf16[8,80,256]{2,1,0:T(8,128)(2,1)}), bf16[8,80,256]{2,1,0:T(8,128)(2,1)S(1)}, u32[]{:S(2)}, u32[]{:S(2)}) async-start(bf16[8,80,256]{2,1,0:T(8,128)(2,1)} %get-tuple-element.64), calls=%async_computation.1 | async-start | bytes 655360 | tf_op jit(solution)/shard_map/all_to_all | solution.py:613
  40.5 1.6 %collective-permute-start.9 = (bf16[320,256]{1,0:T(8,128)(2,1)S(1)}, bf16[320,256]{1,0:T(8,128)(2,1)S(1)}, u32[]{:S(2)}, u32[]{:S(2)}) collective-permute-start(bf16[320,256]{1,0:T(8,128)(2,1)S(1)} %get-tuple-element.74), channel_id=1, source_target_pairs={{0,4},{4,0},{8,12},{12,8},{16,20},{20,16},{24,28},{28,24},{1,5},{5... | collective-permute-start | bytes 491528 | tf_op jit(solution)/shard_map/ppermute | solution.py:581
  41.0 1.4 %collective-permute-start.10 = (bf16[320,256]{1,0:T(8,128)(2,1)S(1)}, bf16[320,256]{1,0:T(8,128)(2,1)S(1)}, u32[]{:S(2)}, u32[]{:S(2)}) collective-permute-start(bf16[320,256]{1,0:T(8,128)(2,1)S(1)} %get-tuple-element.75), channel_id=1, source_target_pairs={{0,4},{4,0},{8,12},{12,8},{16,20},{20,16},{24,28},{28,24},{1,5},{5... | collective-permute-start | bytes 491528 | tf_op jit(solution)/shard_map/ppermute | solution.py:581
  41.1 1.6 %collective-permute-start.11 = (bf16[320,256]{1,0:T(8,128)(2,1)S(1)}, bf16[320,256]{1,0:T(8,128)(2,1)S(1)}, u32[]{:S(2)}, u32[]{:S(2)}) collective-permute-start(bf16[320,256]{1,0:T(8,128)(2,1)S(1)} %get-tuple-element.76), channel_id=1, source_target_pairs={{0,4},{4,0},{8,12},{12,8},{16,20},{20,16},{24,28},{28,24},{1,5},{5... | collective-permute-start | bytes 491528 | tf_op jit(solution)/shard_map/ppermute | solution.py:581
  41.5 1.4 %collective-permute-start.12 = (bf16[320,256]{1,0:T(8,128)(2,1)S(1)}, bf16[320,256]{1,0:T(8,128)(2,1)S(1)}, u32[]{:S(2)}, u32[]{:S(2)}) collective-permute-start(bf16[320,256]{1,0:T(8,128)(2,1)S(1)} %get-tuple-element.77), channel_id=1, source_target_pairs={{0,4},{4,0},{8,12},{12,8},{16,20},{20,16},{24,28},{28,24},{1,5},{5... | collective-permute-start | bytes 491528 | tf_op jit(solution)/shard_map/ppermute | solution.py:581
  44.0 17.5 %collective-permute-start.13 = (bf16[160,640]{1,0:T(8,128)(2,1)S(1)}, bf16[160,640]{1,0:T(8,128)(2,1)S(1)}, u32[]{:S(2)}, u32[]{:S(2)}) collective-permute-start(bf16[160,640]{1,0:T(8,128)(2,1)S(1)} %get-tuple-element.79), channel_id=1, source_target_pairs={{0,8},{4,12},{8,0},{12,4},{16,24},{20,28},{24,16},{28,20},{1,9},{5... | collective-permute-start | bytes 614408 | tf_op jit(solution)/shard_map/ppermute | solution.py:581
  45.8 15.7 %collective-permute-start.14 = (bf16[160,640]{1,0:T(8,128)(2,1)S(1)}, bf16[160,640]{1,0:T(8,128)(2,1)S(1)}, u32[]{:S(2)}, u32[]{:S(2)}) collective-permute-start(bf16[160,640]{1,0:T(8,128)(2,1)S(1)} %get-tuple-element.80), channel_id=1, source_target_pairs={{0,16},{4,20},{8,24},{12,28},{16,0},{20,4},{24,8},{28,12},{1,17},{... | collective-permute-start | bytes 614408 | tf_op jit(solution)/shard_map/ppermute | solution.py:581
  47.3 14.2 %collective-permute-start.15 = (bf16[160,640]{1,0:T(8,128)(2,1)S(1)}, bf16[160,640]{1,0:T(8,128)(2,1)S(1)}, u32[]{:S(2)}, u32[]{:S(2)}) collective-permute-start(bf16[160,640]{1,0:T(8,128)(2,1)S(1)} %get-tuple-element.81), channel_id=1, source_target_pairs={{0,24},{4,28},{8,16},{12,20},{16,8},{20,12},{24,0},{28,4},{1,25},{... | collective-permute-start | bytes 614408 | tf_op jit(solution)/shard_map/ppermute | solution.py:581
  57.9 18.2 %all-to-all-start.2 = ((bf16[8,240,256]{2,1,0:T(8,128)(2,1)}), bf16[8,240,256]{2,1,0:T(8,128)(2,1)S(1)}, u32[]{:S(2)}, u32[]{:S(2)}) async-start(bf16[8,240,256]{2,1,0:T(8,128)(2,1)} %shard_map.108), calls=%async_computation.2 | async-start | bytes 1966080 | tf_op jit(solution)/shard_map/all_to_all | solution.py:618
  61.8 5.5 %collective-permute-start.16 = (bf16[160,160]{1,0:T(8,128)(2,1)S(1)}, bf16[160,160]{1,0:T(8,128)(2,1)S(1)}, u32[]{:S(2)}, u32[]{:S(2)}) collective-permute-start(bf16[160,160]{1,0:T(8,128)(2,1)S(1)} %get-tuple-element.93), channel_id=1, source_target_pairs={{0,1},{1,0},{2,3},{3,2},{4,5},{5,4},{6,7},{7,6},{8,9},{9,8},{10,11... | collective-permute-start | bytes 153608 | tf_op jit(solution)/shard_map/ppermute | solution.py:581
  64.3 9.3 %collective-permute-start.17 = (bf16[160,160]{1,0:T(8,128)(2,1)S(1)}, bf16[160,160]{1,0:T(8,128)(2,1)S(1)}, u32[]{:S(2)}, u32[]{:S(2)}) collective-permute-start(bf16[160,160]{1,0:T(8,128)(2,1)S(1)} %get-tuple-element.94), channel_id=1, source_target_pairs={{0,2},{1,3},{2,0},{3,1},{4,6},{5,7},{6,4},{7,5},{8,10},{9,11},{10,... | collective-permute-start | bytes 153608 | tf_op jit(solution)/shard_map/ppermute | solution.py:581
  64.7 8.9 %collective-permute-start.18 = (bf16[160,160]{1,0:T(8,128)(2,1)S(1)}, bf16[160,160]{1,0:T(8,128)(2,1)S(1)}, u32[]{:S(2)}, u32[]{:S(2)}) collective-permute-start(bf16[160,160]{1,0:T(8,128)(2,1)S(1)} %get-tuple-element.95), channel_id=1, source_target_pairs={{0,3},{1,2},{2,1},{3,0},{4,7},{5,6},{6,5},{7,4},{8,11},{9,10},{10,... | collective-permute-start | bytes 153608 | tf_op jit(solution)/shard_map/ppermute | solution.py:581

commit v7 on v6

--- a/solution.py
+++ b/solution.py
@@ -321,7 +321,7 @@
 
 
 def backward_kernel(
-    all_ref, grads_ref, context_ref, log_ref, out_ref, query_sum, delta, shift, keys, values,
+    all_ref, grads_ref, context_ref, log_ref, out_ref, query_sum, delta, shift,
     *, heads, shares
 ):
     blocks, _, rows = all_ref.shape
@@ -331,9 +331,6 @@
         own = slice(h * HD, (h + 1) * HD)
         key_own = slice(feat + h * HD, feat + (h + 1) * HD)
         value_own = slice(2 * feat + h * HD, 2 * feat + (h + 1) * HD)
-        for j in range(blocks):
-            keys[j] = all_ref[j, key_own, :].T
-            values[j] = all_ref[j, value_own, :].T
         for index in range(count):
             b = shared_block(index, shares)
             product = grads_ref[b, own, :].astype(F32) * context_ref[index, own, :].astype(F32)
@@ -344,43 +341,54 @@
                     hidden_row(all_ref, b, j, feat) - log_ref[index, h : h + 1, :]
                 )
 
-        def step(j, carried, seen):
-            key, value, turned_key = keys[j], values[j], all_ref[j, key_own, :]
-            key_sum = jnp.zeros((HD, rows), F32)
-            value_sum = jnp.zeros((HD, rows), F32)
-
-            def products(index):
+        def sweep(pairs, first_key, ahead):
+            turned, sums = {0: ahead}, {}
+
+            def natural(i):
+                if i not in turned:
+                    j = jnp.minimum(first_key + i, blocks - 1)
+                    turned[i] = (all_ref[j, key_own, :].T, all_ref[j, value_own, :].T)
+                return turned[i]
+
+            def products(i, index):
+                key, value = natural(i)
                 b = shared_block(index, shares)
                 return dot_nn(key, all_ref[b, own, :]), dot_nn(value, grads_ref[b, own, :])
 
-            def weights(index, score, d_probs):
-                probs = jnp.exp(score * SCALING + shift[index, pl.ds(j, 1), :])
+            def weights(i, index, score, d_probs):
+                row = shift[index, pl.ds(first_key + i, 1), :]
+                probs = jnp.exp(score * SCALING + row)
                 d_scores = probs * (d_probs - delta[index])
                 return probs.astype(BF16), d_scores.astype(BF16)
 
-            ready = weights(seen[0], *products(seen[0]))
-            formed = products(seen[1]) if len(seen) > 1 else None
-            for place, index in enumerate(seen):
+            ready = weights(*pairs[0], *products(*pairs[0]))
+            formed = products(*pairs[1]) if len(pairs) > 1 else None
+            for place, (i, index) in enumerate(pairs):
                 b = shared_block(index, shares)
                 probs, d_scores = ready
-                following = products(seen[place + 2]) if place + 2 < len(seen) else None
+                following = products(*pairs[place + 2]) if place + 2 < len(pairs) else None
                 if formed is not None:
-                    ready = weights(seen[place + 1], *formed)
+                    ready = weights(*pairs[place + 1], *formed)
                 formed = following
-                value_sum = value_sum + dot_nt(grads_ref[b, own, :], probs)
-                key_sum = key_sum + dot_nt(all_ref[b, own, :], d_scores)
-                query_sum[index] += dot_nn(turned_key, d_scores)
-            out_ref[j, key_own, :] = (key_sum * SCALING).astype(BF16)
-            out_ref[j, value_own, :] = value_sum.astype(BF16)
-            return carried
-
+                value_part = dot_nt(grads_ref[b, own, :], probs)
+                key_part = dot_nt(all_ref[b, own, :], d_scores)
+                if i in sums:
+                    sums[i] = (sums[i][0] + value_part, sums[i][1] + key_part)
+                else:
+                    sums[i] = (value_part, key_part)
+                j = first_key + i
+                query_sum[index] += dot_nn(all_ref[j, key_own, :], d_scores)
+                if place + 1 == len(pairs) or pairs[place + 1][0] != i:
+                    out_ref[j, value_own, :] = sums[i][0].astype(BF16)
+                    out_ref[j, key_own, :] = (sums[i][1] * SCALING).astype(BF16)
+            return natural(pairs[-1][0] + 1)
+
+        ahead = (all_ref[0, key_own, :].T, all_ref[0, value_own, :].T)
         if shares > 1:
-            lax.fori_loop(0, blocks, functools.partial(step, seen=list(range(count))), 0)
+            pairs = [(0, index) for index in range(count)]
+            lax.fori_loop(0, blocks, lambda j, carried: sweep(pairs, j, carried), ahead)
         else:
-            for begin, end in ((0, blocks // 2 + 1), (blocks // 2 + 1, blocks - 1), (blocks - 1, blocks)):
-                if begin < end:
-                    seen = seen_blocks(begin, blocks)
-                    lax.fori_loop(begin, end, functools.partial(step, seen=seen), 0)
+            sweep([(j, b) for j in range(blocks) for b in seen_blocks(j, blocks)], 0, ahead)
         if shares > 1:
             for b in range(blocks):
                 out_ref[b, own, :] = jnp.zeros((HD, rows), BF16)
@@ -400,8 +408,6 @@
             pltpu.VMEM((count, HD, rows), F32),
             pltpu.VMEM((count, 1, rows), F32),
             pltpu.VMEM((count, blocks, rows), F32),
-            pltpu.VMEM((blocks, rows, HD), BF16),
-            pltpu.VMEM((blocks, rows, HD), BF16),
         ],
         cost_estimate=cost(11.0),
         compiler_params=PARAMS,

time: 77.6 us -> 75.8 us (0.977)
  Pallas kernels: 22.3 us -> 20.5 us
    pallas_call x1, Pallas kernels: 9.92 us -> 8.08 us  [backward(): pl.pallas_call(functools.partial(backward_kernel, heads=heads, shares=sha...]
  transfers between devices with their start and end apart: 22 -> 22, of which waited for: 13 -> 13; matrix products, arithmetic and copies ran while one was open for 0% -> 0% of each run, Pallas kernels for 25% -> 23%
where the time goes in v7:
time: 75.8 us; the launch traced here: 75.4 us
  starting transfers between devices  35.1 us (46%)
  Pallas kernels  20.5 us (27%)
  waiting for transfers between devices  16.9 us (22%)
  local copies, waits for them, and re-layouts  1.44 us (2%)
  between operations  1.43 us (2%)
    ppermute x19, starting transfers between devices, swap(): return lax.ppermute(array, axis, [(i, i ^ mask) for i in range(size)])  22.1 us
    ppermute x19, waiting for transfers between devices, swap(): return lax.ppermute(array, axis, [(i, i ^ mask) for i in range(size)])  13.8 us
    pallas_call x1, Pallas kernels, backward(): pl.pallas_call(functools.partial(backward_kernel, heads=heads, shares=sha...  8.08 us
    all_to_all x1, starting transfers between devices, body(): lax.all_to_all(packed, 'blk', split_axis=0, concat_axis=0, tiled=True)  5.31 us
    pallas_call x1, Pallas kernels, forward(): pl.pallas_call(functools.partial(forward_kernel, heads=heads, shares=shar...  4.87 us
    all_to_all x1, starting transfers between devices, body(): lax.all_to_all(grads, 'blk', split_axis=0, concat_axis=0, tiled=True)  4.14 us
    all_to_all x1, starting transfers between devices, body(): lax.all_to_all(results, 'blk', split_axis=0, concat_axis=0, tiled=True)  3.55 us
    pallas_call x1, Pallas kernels, pack(): pl.pallas_call(functools.partial(pack_kernel, groups=groups), out_shape=j...  2.22 us
  transfers between devices with their start and end apart: 22, of which 13 were waited for; matrix products, arithmetic and copies ran while one was open for 0% of the time, Pallas kernels for 23%

profile of v7, /device:TPU:0, one launch (start us, length us, event | category | flops | bytes accessed | tf_op | source)
XLA Modules:
  0.0 75.4 jit_solution(9619481608313752128)
XLA Ops:
  1.3 2.2 %shard_map.102 = bf16[8,256,256]{2,1,0:T(8,128)(2,1)} custom-call(s32[1,1]{1,0:T(1,128)S(6)} %copy.11.start_ref, bf16[256,640]{1,0:T(8,128)(2,1)} %bitcast.6, bf16[256,640]{1,0:T(8,128)(2,1)} %bitcast.7, bf16[256,640]{1,0:T(8,128)(2,1)} %bitcast.8), custom_call_target="tpu_custom_call" | custom-call | flops 2990000128 | tf_op jit(solution)/shard_map/pallas_call | solution.py:75
  3.5 5.3 %all-to-all-start = ((bf16[8,256,256]{2,1,0:T(8,128)(2,1)}), bf16[8,256,256]{2,1,0:T(8,128)(2,1)S(1)}, u32[]{:S(2)}, u32[]{:S(2)}) async-start(bf16[8,256,256]{2,1,0:T(8,128)(2,1)} %shard_map.102), calls=%async_computation | async-start | bytes 2097152 | tf_op jit(solution)/shard_map/all_to_all | solution.py:609
  8.8 2.7 %collective-permute-start.1 = (s32[1,64]{1,0:T(1,128)S(1)}, s32[1,64]{1,0:T(1,128)S(1)}, u32[]{:S(2)}, u32[]{:S(2)}) collective-permute-start(s32[1,64]{1,0:T(1,128)S(1)} %copy-done.2), channel_id=1, source_target_pairs={{0,2},{1,3},{2,0},{3,1},{4,6},{5,7},{6,4},{7,5},{8,10},{9,11},{10,... | collective-permute-start | bytes 776 | tf_op jit(solution)/shard_map/ppermute | solution.py:587
  11.5 1.6 %collective-permute-start = (s32[1,64]{1,0:T(1,128)S(1)}, s32[1,64]{1,0:T(1,128)S(1)}, u32[]{:S(2)}, u32[]{:S(2)}) collective-permute-start(s32[1,64]{1,0:T(1,128)S(1)} %copy-done.2), channel_id=1, source_target_pairs={{0,1},{1,0},{2,3},{3,2},{4,5},{5,4},{6,7},{7,6},{8,9},{9,8},{10,11... | collective-permute-start | bytes 776 | tf_op jit(solution)/shard_map/ppermute | solution.py:587
  13.4 1.7 %collective-permute-done.refs_1_ = s32[1,64]{1,0:T(1,128)S(1)} collective-permute-done((s32[1,64]{1,0:T(1,128)S(1)}, s32[1,64]{1,0:T(1,128)S(1)}, u32[]{:S(2)}, u32[]{:S(2)}) %collective-permute-start) | collective-permute-done | bytes 288 | tf_op jit(solution)/shard_map/ppermute | solution.py:587
  15.0 3.4 %collective-permute-done.2.refs_3_ = s32[1,64]{1,0:T(1,128)S(1)} collective-permute-done((s32[1,64]{1,0:T(1,128)S(1)}, s32[1,64]{1,0:T(1,128)S(1)}, u32[]{:S(2)}, u32[]{:S(2)}) %collective-permute-start.2) | collective-permute-done | bytes 288 | tf_op jit(solution)/shard_map/ppermute | solution.py:587
  18.4 0.5 shard_map.103
  19.0 0.8 %collective-permute-start.4 = (bf16[16,5120]{1,0:T(8,128)(2,1)S(1)}, bf16[16,5120]{1,0:T(8,128)(2,1)S(1)}, u32[]{:S(2)}, u32[]{:S(2)}) collective-permute-start(bf16[16,5120]{1,0:T(8,128)(2,1)S(1)} %get-tuple-element.57), channel_id=1, source_target_pairs={{0,2},{1,3},{2,0},{3,1},{4,6},{5,7},{6,4},{7,5},{8,10},{9,11},{10,... | collective-permute-start | bytes 491528 | tf_op jit(solution)/shard_map/ppermute | solution.py:587
  19.8 3.6 %collective-permute-start.5 = (bf16[16,5120]{1,0:T(8,128)(2,1)S(1)}, bf16[16,5120]{1,0:T(8,128)(2,1)S(1)}, u32[]{:S(2)}, u32[]{:S(2)}) collective-permute-start(bf16[16,5120]{1,0:T(8,128)(2,1)S(1)} %get-tuple-element.58), channel_id=1, source_target_pairs={{0,3},{1,2},{2,1},{3,0},{4,7},{5,6},{6,5},{7,4},{8,11},{9,10},{10,... | collective-permute-start | bytes 491528 | tf_op jit(solution)/shard_map/ppermute | solution.py:587
  23.4 0.9 %all-to-all-done.all_ref = bf16[8,256,256]{2,1,0:T(8,128)(2,1)S(1)} async-done(((bf16[8,256,256]{2,1,0:T(8,128)(2,1)}), bf16[8,256,256]{2,1,0:T(8,128)(2,1)S(1)}, u32[]{:S(2)}, u32[]{:S(2)}) %all-to-all-start) | async-done | bytes 1048608 | tf_op jit(solution)/shard_map/all_to_all | solution.py:609
  24.3 4.9 %shard_map.104 = (bf16[2,80,256]{2,1,0:T(8,128)(2,1)S(1)}, bf16[2,80,256]{2,1,0:T(8,128)(2,1)S(1)}, bf16[2,80,256]{2,1,0:T(8,128)(2,1)S(1)}, bf16[2,80,256]{2,1,...) custom-call(bf16[8,256,256]{2,1,0:T(8,128)(2,1)S(1)} %all-to-all-done.all_ref), custom_call_target="tpu_custom_call" | custom-call | flops 8049999872 | tf_op jit(solution)/shard_map/pallas_call | solution.py:303
  29.1 1.1 %collective-permute-start.6 = (bf16[2,80,256]{2,1,0:T(8,128)(2,1)S(1)}, bf16[2,80,256]{2,1,0:T(8,128)(2,1)S(1)}, u32[]{:S(2)}, u32[]{:S(2)}) collective-permute-start(bf16[2,80,256]{2,1,0:T(8,128)(2,1)S(1)} %get-tuple-element.67), channel_id=1, source_target_pairs={{0,8},{4,12},{8,0},{12,4},{16,24},{20,28},{24,16},{28,20},{1,9},{5... | collective-permute-start | bytes 245768 | tf_op jit(solution)/shard_map/ppermute | solution.py:587
  30.3 1.5 %collective-permute-start.7 = (bf16[2,80,256]{2,1,0:T(8,128)(2,1)S(1)}, bf16[2,80,256]{2,1,0:T(8,128)(2,1)S(1)}, u32[]{:S(2)}, u32[]{:S(2)}) collective-permute-start(bf16[2,80,256]{2,1,0:T(8,128)(2,1)S(1)} %get-tuple-element.68), channel_id=1, source_target_pairs={{0,16},{4,20},{8,24},{12,28},{16,0},{20,4},{24,8},{28,12},{1,17},{... | collective-permute-start | bytes 245768 | tf_op jit(solution)/shard_map/ppermute | solution.py:587
  31.8 0.9 %collective-permute-start.8 = (bf16[2,80,256]{2,1,0:T(8,128)(2,1)S(1)}, bf16[2,80,256]{2,1,0:T(8,128)(2,1)S(1)}, u32[]{:S(2)}, u32[]{:S(2)}) collective-permute-start(bf16[2,80,256]{2,1,0:T(8,128)(2,1)S(1)} %get-tuple-element.69), channel_id=1, source_target_pairs={{0,24},{4,28},{8,16},{12,20},{16,8},{20,12},{24,0},{28,4},{1,25},{... | collective-permute-start | bytes 245768 | tf_op jit(solution)/shard_map/ppermute | solution.py:587
  32.7 0.5 collective-permute-done.4.refs_2_
  33.2 1.4 %copy-done = bf16[640,1280]{1,0:T(8,128)(2,1)S(1)} copy-done((bf16[640,1280]{1,0:T(8,128)(2,1)S(1)}, bf16[640,1280]{1,0:T(8,128)(2,1)}, u32[]{:S(2)}) %copy-start) | copy-done | bytes 1638424
  34.7 1.6 %shard_map.105 = (bf16[8,80,256]{2,1,0:T(8,128)(2,1)}, bf16[64,2560]{1,0:T(8,128)(2,1)S(1)}, bf16[160,256]{1,0:T(8,128)(2,1)S(1)}, bf16[160,256]{1,0:T(8,128)(2,...) custom-call(bf16[640,1280]{1,0:T(8,128)(2,1)S(1)} %copy-done, ...), custom_call_target="tpu_custom_call" | custom-call | flops 805000000 | tf_op jit(solution)/shard_map/pallas_call | solution.py:144
  36.2 4.1 %all-to-all-start.1 = ((bf16[8,80,256]{2,1,0:T(8,128)(2,1)}), bf16[8,80,256]{2,1,0:T(8,128)(2,1)S(1)}, u32[]{:S(2)}, u32[]{:S(2)}) async-start(bf16[8,80,256]{2,1,0:T(8,128)(2,1)} %get-tuple-element.64), calls=%async_computation.1 | async-start | bytes 655360 | tf_op jit(solution)/shard_map/all_to_all | solution.py:619
  40.5 0.6 collective-permute-start.9
  41.6 0.4 collective-permute-done.9.refs_4_
  42.9 1.1 %shard_map.107 = (bf16[160,640]{1,0:T(8,128)(2,1)S(1)}, bf16[160,640]{1,0:T(8,128)(2,1)S(1)}, bf16[160,640]{1,0:T(8,128)(2,1)S(1)}, bf16[160,640]{1,0:T(8,128)(2,1)S(1)}) custom-call(bf16[64,2560]{1,0:T(8,128)(2,1)S(1)} %get-tuple-element.65.keep_ref, bf16[2,80,256]{2,1,0:T(8,128)(2,1)S(1)} %get-tuple-element.66.refs_0_, ...), custom_call_target="tpu_custom_call" | custom-call | flops 230000000 | tf_op jit(solution)/shard_map/pallas_call | solution.py:524
  44.0 1.8 %collective-permute-start.13 = (bf16[160,640]{1,0:T(8,128)(2,1)S(1)}, bf16[160,640]{1,0:T(8,128)(2,1)S(1)}, u32[]{:S(2)}, u32[]{:S(2)}) collective-permute-start(bf16[160,640]{1,0:T(8,128)(2,1)S(1)} %get-tuple-element.79), channel_id=1, source_target_pairs={{0,8},{4,12},{8,0},{12,4},{16,24},{20,28},{24,16},{28,20},{1,9},{5... | collective-permute-start | bytes 614408 | tf_op jit(solution)/shard_map/ppermute | solution.py:587
  45.8 1.5 %collective-permute-start.14 = (bf16[160,640]{1,0:T(8,128)(2,1)S(1)}, bf16[160,640]{1,0:T(8,128)(2,1)S(1)}, u32[]{:S(2)}, u32[]{:S(2)}) collective-permute-start(bf16[160,640]{1,0:T(8,128)(2,1)S(1)} %get-tuple-element.80), channel_id=1, source_target_pairs={{0,16},{4,20},{8,24},{12,28},{16,0},{20,4},{24,8},{28,12},{1,17},{... | collective-permute-start | bytes 614408 | tf_op jit(solution)/shard_map/ppermute | solution.py:587
  48.0 8.1 %shard_map.108 = bf16[8,240,256]{2,1,0:T(8,128)(2,1)} custom-call(bf16[8,256,256]{2,1,0:T(8,128)(2,1)S(1)} %all-to-all-done.all_ref, bf16[8,80,256]{2,1,0:T(8,128)(2,1)S(1)} %all-to-all-done.1.grads_ref, bf16[8,80,256]{2,1,0:T(8,128)(2,1)S(1)} %get-tuple-element.83.context_ref, f32[8,1,256]{2,1,0:T(1,128)S(1)} %get-tuple-element.84.log_ref), custom_call_target="tpu_custom_call" | custom-call | flops 12650000384 | tf_op jit(solution)/shard_map/pallas_call | solution.py:402
  56.1 3.6 %all-to-all-start.2 = ((bf16[8,240,256]{2,1,0:T(8,128)(2,1)}), bf16[8,240,256]{2,1,0:T(8,128)(2,1)S(1)}, u32[]{:S(2)}, u32[]{:S(2)}) async-start(bf16[8,240,256]{2,1,0:T(8,128)(2,1)} %shard_map.108), calls=%async_computation.2 | async-start | bytes 1966080 | tf_op jit(solution)/shard_map/all_to_all | solution.py:624
  60.0 2.5 %collective-permute-start.16 = (bf16[160,160]{1,0:T(8,128)(2,1)S(1)}, bf16[160,160]{1,0:T(8,128)(2,1)S(1)}, u32[]{:S(2)}, u32[]{:S(2)}) collective-permute-start(bf16[160,160]{1,0:T(8,128)(2,1)S(1)} %get-tuple-element.93), channel_id=1, source_target_pairs={{0,1},{1,0},{2,3},{3,2},{4,5},{5,4},{6,7},{7,6},{8,9},{9,8},{10,11... | collective-permute-start | bytes 153608 | tf_op jit(solution)/shard_map/ppermute | solution.py:587
  62.9 2.0 %collective-permute-start.18 = (bf16[160,160]{1,0:T(8,128)(2,1)S(1)}, bf16[160,160]{1,0:T(8,128)(2,1)S(1)}, u32[]{:S(2)}, u32[]{:S(2)}) collective-permute-start(bf16[160,160]{1,0:T(8,128)(2,1)S(1)} %get-tuple-element.95), channel_id=1, source_target_pairs={{0,3},{1,2},{2,1},{3,0},{4,7},{5,6},{6,5},{7,4},{8,11},{9,10},{10,... | collective-permute-start | bytes 153608 | tf_op jit(solution)/shard_map/ppermute | solution.py:587
  64.9 0.6 collective-permute-done.16.refs_1_
  65.5 6.3 %collective-permute-done.17.refs_2_ = bf16[160,160]{1,0:T(8,128)(2,1)S(1)} collective-permute-done((bf16[160,160]{1,0:T(8,128)(2,1)S(1)}, bf16[160,160]{1,0:T(8,128)(2,1)S(1)}, u32[]{:S(2)}, u32[]{:S(2)}) %collective-permute-start.17) | collective-permute-done | bytes 51232 | tf_op jit(solution)/shard_map/ppermute | solution.py:587
  71.8 0.7 shard_map.111
  72.5 1.8 %all-to-all-done.2.all_ref = bf16[8,240,256]{2,1,0:T(8,128)(2,1)S(1)} async-done(((bf16[8,240,256]{2,1,0:T(8,128)(2,1)}), bf16[8,240,256]{2,1,0:T(8,128)(2,1)S(1)}, u32[]{:S(2)}, u32[]{:S(2)}) %all-to-all-start.2) | async-done | bytes 983072 | tf_op jit(solution)/shard_map/all_to_all | solution.py:624
  74.3 1.1 %shard_map.109 = (bf16[256,640]{1,0:T(8,128)(2,1)}, bf16[256,640]{1,0:T(8,128)(2,1)}, bf16[256,640]{1,0:T(8,128)(2,1)}) custom-call(bf16[8,240,256]{2,1,0:T(8,128)(2,1)S(1)} %all-to-all-done.2.all_ref), custom_call_target="tpu_custom_call" | custom-call | flops 1264999936 | tf_op jit(solution)/shard_map/pallas_call | solution.py:440
  (28 shorter events, 3.3 us)
Async XLA Ops:
  3.5 5.3 %copy-start.2 = (s32[1,64]{1,0:T(1,128)S(1)}, s32[1,64]{1,0:T(1,128)}, u32[]{:S(2)}) copy-start(s32[1,64]{1,0:T(1,128)} %refs_0_.1) | copy-start | bytes 772
  3.5 14.9 %copy-start.1 = (bf16[64,5120]{1,0:T(8,128)(2,1)S(1)}, bf16[64,5120]{1,0:T(8,128)(2,1)}, u32[]{:S(2)}) copy-start(bf16[64,5120]{1,0:T(8,128)(2,1)} %grad_ref.1) | copy-start | bytes 1966084
  3.5 20.7 %all-to-all-start = ((bf16[8,256,256]{2,1,0:T(8,128)(2,1)}), bf16[8,256,256]{2,1,0:T(8,128)(2,1)S(1)}, u32[]{:S(2)}, u32[]{:S(2)}) async-start(bf16[8,256,256]{2,1,0:T(8,128)(2,1)} %shard_map.102), calls=%async_computation | async-start | bytes 2097152 | tf_op jit(solution)/shard_map/all_to_all | solution.py:609
  8.8 4.5 %collective-permute-start.1 = (s32[1,64]{1,0:T(1,128)S(1)}, s32[1,64]{1,0:T(1,128)S(1)}, u32[]{:S(2)}, u32[]{:S(2)}) collective-permute-start(s32[1,64]{1,0:T(1,128)S(1)} %copy-done.2), channel_id=1, source_target_pairs={{0,2},{1,3},{2,0},{3,1},{4,6},{5,7},{6,4},{7,5},{8,10},{9,11},{10,... | collective-permute-start | bytes 776 | tf_op jit(solution)/shard_map/ppermute | solution.py:587
  11.5 3.5 %collective-permute-start = (s32[1,64]{1,0:T(1,128)S(1)}, s32[1,64]{1,0:T(1,128)S(1)}, u32[]{:S(2)}, u32[]{:S(2)}) collective-permute-start(s32[1,64]{1,0:T(1,128)S(1)} %copy-done.2), channel_id=1, source_target_pairs={{0,1},{1,0},{2,3},{3,2},{4,5},{5,4},{6,7},{7,6},{8,9},{9,8},{10,11... | collective-permute-start | bytes 776 | tf_op jit(solution)/shard_map/ppermute | solution.py:587
  13.1 5.3 %collective-permute-start.2 = (s32[1,64]{1,0:T(1,128)S(1)}, s32[1,64]{1,0:T(1,128)S(1)}, u32[]{:S(2)}, u32[]{:S(2)}) collective-permute-start(s32[1,64]{1,0:T(1,128)S(1)} %copy-done.2), channel_id=1, source_target_pairs={{0,3},{1,2},{2,1},{3,0},{4,7},{5,6},{6,5},{7,4},{8,11},{9,10},{10,... | collective-permute-start | bytes 776 | tf_op jit(solution)/shard_map/ppermute | solution.py:587
  18.9 10.2 %collective-permute-start.3 = (bf16[16,5120]{1,0:T(8,128)(2,1)S(1)}, bf16[16,5120]{1,0:T(8,128)(2,1)S(1)}, u32[]{:S(2)}, u32[]{:S(2)}) collective-permute-start(bf16[16,5120]{1,0:T(8,128)(2,1)S(1)} %get-tuple-element.51), channel_id=1, source_target_pairs={{0,1},{1,0},{2,3},{3,2},{4,5},{5,4},{6,7},{7,6},{8,9},{9,8},{10,11... | collective-permute-start | bytes 491528 | tf_op jit(solution)/shard_map/ppermute | solution.py:587
  19.0 14.2 %collective-permute-start.4 = (bf16[16,5120]{1,0:T(8,128)(2,1)S(1)}, bf16[16,5120]{1,0:T(8,128)(2,1)S(1)}, u32[]{:S(2)}, u32[]{:S(2)}) collective-permute-start(bf16[16,5120]{1,0:T(8,128)(2,1)S(1)} %get-tuple-element.57), channel_id=1, source_target_pairs={{0,2},{1,3},{2,0},{3,1},{4,6},{5,7},{6,4},{7,5},{8,10},{9,11},{10,... | collective-permute-start | bytes 491528 | tf_op jit(solution)/shard_map/ppermute | solution.py:587
  19.8 13.4 %collective-permute-start.5 = (bf16[16,5120]{1,0:T(8,128)(2,1)S(1)}, bf16[16,5120]{1,0:T(8,128)(2,1)S(1)}, u32[]{:S(2)}, u32[]{:S(2)}) collective-permute-start(bf16[16,5120]{1,0:T(8,128)(2,1)S(1)} %get-tuple-element.58), channel_id=1, source_target_pairs={{0,3},{1,2},{2,1},{3,0},{4,7},{5,6},{6,5},{7,4},{8,11},{9,10},{10,... | collective-permute-start | bytes 491528 | tf_op jit(solution)/shard_map/ppermute | solution.py:587
  29.1 11.2 %collective-permute-start.6 = (bf16[2,80,256]{2,1,0:T(8,128)(2,1)S(1)}, bf16[2,80,256]{2,1,0:T(8,128)(2,1)S(1)}, u32[]{:S(2)}, u32[]{:S(2)}) collective-permute-start(bf16[2,80,256]{2,1,0:T(8,128)(2,1)S(1)} %get-tuple-element.67), channel_id=1, source_target_pairs={{0,8},{4,12},{8,0},{12,4},{16,24},{20,28},{24,16},{28,20},{1,9},{5... | collective-permute-start | bytes 245768 | tf_op jit(solution)/shard_map/ppermute | solution.py:587
  30.3 10.1 %collective-permute-start.7 = (bf16[2,80,256]{2,1,0:T(8,128)(2,1)S(1)}, bf16[2,80,256]{2,1,0:T(8,128)(2,1)S(1)}, u32[]{:S(2)}, u32[]{:S(2)}) collective-permute-start(bf16[2,80,256]{2,1,0:T(8,128)(2,1)S(1)} %get-tuple-element.68), channel_id=1, source_target_pairs={{0,16},{4,20},{8,24},{12,28},{16,0},{20,4},{24,8},{28,12},{1,17},{... | collective-permute-start | bytes 245768 | tf_op jit(solution)/shard_map/ppermute | solution.py:587
  31.8 8.6 %collective-permute-start.8 = (bf16[2,80,256]{2,1,0:T(8,128)(2,1)S(1)}, bf16[2,80,256]{2,1,0:T(8,128)(2,1)S(1)}, u32[]{:S(2)}, u32[]{:S(2)}) collective-permute-start(bf16[2,80,256]{2,1,0:T(8,128)(2,1)S(1)} %get-tuple-element.69), channel_id=1, source_target_pairs={{0,24},{4,28},{8,16},{12,20},{16,8},{20,12},{24,0},{28,4},{1,25},{... | collective-permute-start | bytes 245768 | tf_op jit(solution)/shard_map/ppermute | solution.py:587
  33.2 1.4 %copy-start = (bf16[640,1280]{1,0:T(8,128)(2,1)S(1)}, bf16[640,1280]{1,0:T(8,128)(2,1)}, u32[]{:S(2)}) copy-start(bf16[640,1280]{1,0:T(8,128)(2,1)} %weight_ref.1) | copy-start | bytes 4915204
  36.2 11.8 %all-to-all-start.1 = ((bf16[8,80,256]{2,1,0:T(8,128)(2,1)}), bf16[8,80,256]{2,1,0:T(8,128)(2,1)S(1)}, u32[]{:S(2)}, u32[]{:S(2)}) async-start(bf16[8,80,256]{2,1,0:T(8,128)(2,1)} %get-tuple-element.64), calls=%async_computation.1 | async-start | bytes 655360 | tf_op jit(solution)/shard_map/all_to_all | solution.py:619
  40.5 1.6 %collective-permute-start.9 = (bf16[320,256]{1,0:T(8,128)(2,1)S(1)}, bf16[320,256]{1,0:T(8,128)(2,1)S(1)}, u32[]{:S(2)}, u32[]{:S(2)}) collective-permute-start(bf16[320,256]{1,0:T(8,128)(2,1)S(1)} %get-tuple-element.74), channel_id=1, source_target_pairs={{0,4},{4,0},{8,12},{12,8},{16,20},{20,16},{24,28},{28,24},{1,5},{5... | collective-permute-start | bytes 491528 | tf_op jit(solution)/shard_map/ppermute | solution.py:587
  41.0 1.4 %collective-permute-start.10 = (bf16[320,256]{1,0:T(8,128)(2,1)S(1)}, bf16[320,256]{1,0:T(8,128)(2,1)S(1)}, u32[]{:S(2)}, u32[]{:S(2)}) collective-permute-start(bf16[320,256]{1,0:T(8,128)(2,1)S(1)} %get-tuple-element.75), channel_id=1, source_target_pairs={{0,4},{4,0},{8,12},{12,8},{16,20},{20,16},{24,28},{28,24},{1,5},{5... | collective-permute-start | bytes 491528 | tf_op jit(solution)/shard_map/ppermute | solution.py:587
  41.1 1.6 %collective-permute-start.11 = (bf16[320,256]{1,0:T(8,128)(2,1)S(1)}, bf16[320,256]{1,0:T(8,128)(2,1)S(1)}, u32[]{:S(2)}, u32[]{:S(2)}) collective-permute-start(bf16[320,256]{1,0:T(8,128)(2,1)S(1)} %get-tuple-element.76), channel_id=1, source_target_pairs={{0,4},{4,0},{8,12},{12,8},{16,20},{20,16},{24,28},{28,24},{1,5},{5... | collective-permute-start | bytes 491528 | tf_op jit(solution)/shard_map/ppermute | solution.py:587
  41.5 1.4 %collective-permute-start.12 = (bf16[320,256]{1,0:T(8,128)(2,1)S(1)}, bf16[320,256]{1,0:T(8,128)(2,1)S(1)}, u32[]{:S(2)}, u32[]{:S(2)}) collective-permute-start(bf16[320,256]{1,0:T(8,128)(2,1)S(1)} %get-tuple-element.77), channel_id=1, source_target_pairs={{0,4},{4,0},{8,12},{12,8},{16,20},{20,16},{24,28},{28,24},{1,5},{5... | collective-permute-start | bytes 491528 | tf_op jit(solution)/shard_map/ppermute | solution.py:587
  44.0 15.6 %collective-permute-start.13 = (bf16[160,640]{1,0:T(8,128)(2,1)S(1)}, bf16[160,640]{1,0:T(8,128)(2,1)S(1)}, u32[]{:S(2)}, u32[]{:S(2)}) collective-permute-start(bf16[160,640]{1,0:T(8,128)(2,1)S(1)} %get-tuple-element.79), channel_id=1, source_target_pairs={{0,8},{4,12},{8,0},{12,4},{16,24},{20,28},{24,16},{28,20},{1,9},{5... | collective-permute-start | bytes 614408 | tf_op jit(solution)/shard_map/ppermute | solution.py:587
  45.8 13.8 %collective-permute-start.14 = (bf16[160,640]{1,0:T(8,128)(2,1)S(1)}, bf16[160,640]{1,0:T(8,128)(2,1)S(1)}, u32[]{:S(2)}, u32[]{:S(2)}) collective-permute-start(bf16[160,640]{1,0:T(8,128)(2,1)S(1)} %get-tuple-element.80), channel_id=1, source_target_pairs={{0,16},{4,20},{8,24},{12,28},{16,0},{20,4},{24,8},{28,12},{1,17},{... | collective-permute-start | bytes 614408 | tf_op jit(solution)/shard_map/ppermute | solution.py:587
  47.3 12.4 %collective-permute-start.15 = (bf16[160,640]{1,0:T(8,128)(2,1)S(1)}, bf16[160,640]{1,0:T(8,128)(2,1)S(1)}, u32[]{:S(2)}, u32[]{:S(2)}) collective-permute-start(bf16[160,640]{1,0:T(8,128)(2,1)S(1)} %get-tuple-element.81), channel_id=1, source_target_pairs={{0,24},{4,28},{8,16},{12,20},{16,8},{20,12},{24,0},{28,4},{1,25},{... | collective-permute-start | bytes 614408 | tf_op jit(solution)/shard_map/ppermute | solution.py:587
  56.1 18.2 %all-to-all-start.2 = ((bf16[8,240,256]{2,1,0:T(8,128)(2,1)}), bf16[8,240,256]{2,1,0:T(8,128)(2,1)S(1)}, u32[]{:S(2)}, u32[]{:S(2)}) async-start(bf16[8,240,256]{2,1,0:T(8,128)(2,1)} %shard_map.108), calls=%async_computation.2 | async-start | bytes 1966080 | tf_op jit(solution)/shard_map/all_to_all | solution.py:624
  60.0 5.6 %collective-permute-start.16 = (bf16[160,160]{1,0:T(8,128)(2,1)S(1)}, bf16[160,160]{1,0:T(8,128)(2,1)S(1)}, u32[]{:S(2)}, u32[]{:S(2)}) collective-permute-start(bf16[160,160]{1,0:T(8,128)(2,1)S(1)} %get-tuple-element.93), channel_id=1, source_target_pairs={{0,1},{1,0},{2,3},{3,2},{4,5},{5,4},{6,7},{7,6},{8,9},{9,8},{10,11... | collective-permute-start | bytes 153608 | tf_op jit(solution)/shard_map/ppermute | solution.py:587
  62.5 9.3 %collective-permute-start.17 = (bf16[160,160]{1,0:T(8,128)(2,1)S(1)}, bf16[160,160]{1,0:T(8,128)(2,1)S(1)}, u32[]{:S(2)}, u32[]{:S(2)}) collective-permute-start(bf16[160,160]{1,0:T(8,128)(2,1)S(1)} %get-tuple-element.94), channel_id=1, source_target_pairs={{0,2},{1,3},{2,0},{3,1},{4,6},{5,7},{6,4},{7,5},{8,10},{9,11},{10,... | collective-permute-start | bytes 153608 | tf_op jit(solution)/shard_map/ppermute | solution.py:587
  62.9 8.9 %collective-permute-start.18 = (bf16[160,160]{1,0:T(8,128)(2,1)S(1)}, bf16[160,160]{1,0:T(8,128)(2,1)S(1)}, u32[]{:S(2)}, u32[]{:S(2)}) collective-permute-start(bf16[160,160]{1,0:T(8,128)(2,1)S(1)} %get-tuple-element.95), channel_id=1, source_target_pairs={{0,3},{1,2},{2,1},{3,0},{4,7},{5,6},{6,5},{7,4},{8,11},{9,10},{10,... | collective-permute-start | bytes 153608 | tf_op jit(solution)/shard_map/ppermute | solution.py:587
